TPU v7x, 256 devices: a whole 4x4x8 slice. The times are simulated.
256 devices in a mesh: ctx: 64 (over z, y, core), head: 4 (over x).
Axes of the slice: x: 4, y: 4, z: 8, core: 2. Of those that a mesh axis runs over, the one named last changes fastest.
Arguments:
- inputs: bfloat16 [16384, 8, 1024], P('ctx', None, 'head'), may hold values from -6 to 6
- step_size: float32 [16384, 8, 16], P('ctx', None, 'head'), may hold values from 0.125 to 2
- decay_rate: float32 [8, 16], P(None, 'head'), may hold values from -0.1 to 0
- b_proj: bfloat16 [16384, 8, 128], P('ctx'), may hold values from -6 to 6
- c_proj: bfloat16 [16384, 8, 128], P('ctx'), may hold values from -6 to 6
- grad_out: bfloat16 [16384, 8, 1024], P('ctx', None, 'head'), may hold values from -0.005859375 to 0.005859375
- segment_ids: int32 [16384], P('ctx'), may hold values from 0 to 15, never falling along the last dimension, each value on 1 to 4096 neighbouring positions
Outputs:
- grad_in: bfloat16 [16384, 8, 1024], P('ctx', None, 'head')
- grad_step: float32 [16384, 8, 16], P('ctx', None, 'head')
- grad_b: float32 [16384, 8, 128], P('ctx', 'head')
- grad_c: float32 [16384, 8, 128], P('ctx', 'head')
All inputs are finite; a program needn't handle non-finite values.
Results may differ from a plain program's by a relative error of at most 0.001.
Values sent between devices are 32-bit elements; how exact they have to be, the bound alone decides.
No kernel may reach another device: no remote copies, remote signals or barrier semaphores. Data moves between devices by JAX's collectives and lax.ppermute only.
A program may use at most 320 MiB of HBM per device.

v0:
```python
import jax
import jax.numpy as jnp
from jax import lax
from jax.sharding import PartitionSpec as P

P_SIZE = 64
N = 128
SPAN = 128


PRECISE = lax.Precision.HIGHEST


def prefix(value, axis, join, neutral, backward):
    count, mine = (lax.axis_size(axis), lax.axis_index(axis))
    pieces = jax.tree.map(lambda part: lax.all_gather(part, axis), value)
    if backward:
        pieces = jax.tree.map(lambda part: part[::-1], pieces)
        mine = count - 1 - mine
    total = jax.tree.map(
        lambda part, zero: jnp.full_like(part, 0) + jnp.asarray(zero, part.dtype), value, neutral
    )

    def turn(position, total):
        longer = join(total, jax.tree.map(lambda part: part[position], pieces))
        return jax.tree.map(lambda new, old: jnp.where(position < mine, new, old), longer, total)

    return lax.fori_loop(0, count - 1, turn, total)


def product(pattern, first_op, second_op):
    return jnp.einsum(pattern, first_op, second_op, precision=PRECISE)


def span_weights(step_size, decay_rate, segment):
    cumlog = jnp.cumsum(step_size * decay_rate[None], axis=0)
    at_first = (segment == segment[0]).astype(jnp.float32)[:, None, None]
    at_last = (segment == segment[-1]).astype(jnp.float32)[:, None, None]
    alpha_w = jnp.exp(cumlog) * at_first
    beta_w = jnp.exp(cumlog[-1][None] - cumlog) * at_last
    return (cumlog, alpha_w, beta_w)


def span_summary(inputs, step_size, decay_rate, b_proj, c_proj, grad_out, segment):
    cumlog, alpha_w, beta_w = span_weights(step_size, decay_rate, segment)
    decayed = jnp.exp(cumlog[-1]) * (segment[0] == segment[-1]).astype(jnp.float32)
    forward_sum = product("sgjp,sgn->gjpn", inputs * (beta_w * step_size)[..., None], b_proj)
    reverse_sum = product("rgjp,rgn->gjpn", grad_out * alpha_w[..., None], c_proj)
    return (decayed, forward_sum, reverse_sum)


def span_grads(x_raw, dy_raw, b_raw, c_raw, step_size, decay_rate, segment, state_in, adjoint_in):
    inputs = x_raw.astype(jnp.float32)
    grad_out = dy_raw.astype(jnp.float32)
    b_proj = b_raw.astype(jnp.float32)
    c_proj = c_raw.astype(jnp.float32)
    length = segment.shape[0]
    cumlog, alpha_w, beta_w = span_weights(step_size, decay_rate, segment)
    row_ids = lax.broadcasted_iota(jnp.int32, (length, length), 0)
    col_ids = lax.broadcasted_iota(jnp.int32, (length, length), 1)
    linked = (segment[:, None] == segment[None, :]) & (row_ids >= col_ids)
    cum_cols = jnp.transpose(cumlog, (1, 2, 0))
    differ = cum_cols[:, :, :, None] - cum_cols[:, :, None, :]
    decays = jnp.where(linked[None, None], jnp.exp(jnp.minimum(differ, 0.0)), 0.0)
    upper_tri = (row_ids <= col_ids).astype(jnp.float32)
    lower_tri = (row_ids >= col_ids).astype(jnp.float32)
    step_cols = jnp.transpose(step_size, (1, 2, 0))
    cross_dx = jnp.einsum("tgjp,sgjp->gjts", dy_raw, x_raw, preferred_element_type=jnp.float32)
    cross_cb = jnp.einsum("tgn,sgn->gts", c_raw, b_raw, preferred_element_type=jnp.float32)
    weighted = decays * cross_dx * step_cols[:, :, None, :]
    summed = jnp.sum(weighted, axis=1)
    dy_state = product("tgjp,gjpn->tgjn", grad_out, state_in)
    x_adjoint = product("sgjp,gjpn->sgjn", inputs, adjoint_in)
    grad_c = product("gts,sgn->tgn", summed, b_proj) + jnp.sum(
        alpha_w[..., None] * dy_state, axis=2
    )
    grad_b = product("gts,tgn->sgn", summed, c_proj) + jnp.sum(
        (step_size * beta_w)[..., None] * x_adjoint, axis=2
    )
    raw_dx = product("gjrt,rgjp->tgjp", decays * cross_cb[:, None], grad_out)
    raw_dx = raw_dx + beta_w[..., None] * product("tgn,gjpn->tgjp", b_proj, adjoint_in)
    running = product("gjrs,st->gjrt", weighted * cross_cb[:, None], upper_tri)
    term_four = jnp.transpose(jnp.sum(running * lower_tri[None, None], axis=2), (2, 0, 1))
    term_one = alpha_w * beta_w * jnp.sum(state_in * adjoint_in, axis=(2, 3))[None]
    dy_c = jnp.sum(dy_state * c_proj[:, :, None, :], axis=3)
    term_two = alpha_w * product("gjrt,rgj->tgj", decays, dy_c)
    x_b = step_size * jnp.sum(x_adjoint * b_proj[:, :, None, :], axis=3)
    term_three = beta_w * product("gjts,sgj->tgj", decays, x_b)
    along_x = jnp.sum(inputs * raw_dx, axis=3)
    total_s = term_one + term_two + term_three + term_four
    grad_step = along_x + decay_rate[None] * (total_s - step_size * along_x)
    grad_in = step_size[..., None] * raw_dx
    return (grad_in, grad_step, grad_b, grad_c)


def forward_join(earlier, latter):
    dec_e, sta_e, first_e, last_e = earlier
    dec_l, sta_l, first_l, last_l = latter
    linked = ((first_l == last_e) | (last_e < 0) | (first_l < 0)).astype(jnp.float32)
    factor = dec_l * linked
    return (
        dec_e * factor,
        factor[..., None, None] * sta_e + sta_l,
        jnp.where(first_e < 0, first_l, first_e),
        jnp.where(last_l < 0, last_e, last_l),
    )


def reverse_join(earlier, latter):
    dec_e, sta_e, first_e, last_e = earlier
    dec_l, sta_l, first_l, last_l = latter
    linked = ((first_e == last_l) | (first_e < 0) | (last_l < 0)).astype(jnp.float32)
    factor = dec_l * linked
    return (
        dec_e * factor,
        sta_l + factor[..., None, None] * sta_e,
        jnp.where(first_l < 0, first_e, first_l),
        jnp.where(last_e < 0, last_l, last_e),
    )


def per_device(inputs, step_size, decay_rate, b_proj, c_proj, grad_out, segment_ids):
    span_count = inputs.shape[0] // SPAN
    groups = inputs.shape[1]
    per_group = step_size.shape[2]
    x_all = inputs.reshape(span_count, SPAN, groups, per_group, P_SIZE)
    dy_all = grad_out.reshape(span_count, SPAN, groups, per_group, P_SIZE)
    dt_all = step_size.reshape(span_count, SPAN, groups, per_group)
    b_all = b_proj.reshape(span_count, SPAN, groups, N)
    c_all = c_proj.reshape(span_count, SPAN, groups, N)
    seg_all = segment_ids.reshape(span_count, SPAN)
    seg_float = segment_ids.astype(jnp.float32)
    summaries = []
    for number in range(span_count):
        summaries.append(
            span_summary(
                x_all[number].astype(jnp.float32),
                dt_all[number],
                decay_rate,
                b_all[number].astype(jnp.float32),
                c_all[number].astype(jnp.float32),
                dy_all[number].astype(jnp.float32),
                seg_all[number],
            )
        )

    def span_ids(number):
        seg_blk = seg_all[number].astype(jnp.float32)
        return (seg_blk[:1], seg_blk[-1:])

    forward_elem = None
    for number in range(span_count):
        first_id, last_id = span_ids(number)
        element = (summaries[number][0], summaries[number][1], first_id, last_id)
        forward_elem = element if number == 0 else forward_join(forward_elem, element)
    reverse_elem = None
    for number in reversed(range(span_count)):
        first_id, last_id = span_ids(number)
        element = (summaries[number][0], summaries[number][2], first_id, last_id)
        reverse_elem = element if number == span_count - 1 else reverse_join(reverse_elem, element)
    identity = (
        jnp.ones_like(summaries[0][0]),
        jnp.zeros_like(summaries[0][1]),
        -jnp.ones((1,), jnp.float32),
        -jnp.ones((1,), jnp.float32),
    )
    before = prefix(
        (forward_elem[0], forward_elem[1], forward_elem[2], forward_elem[3]),
        "ctx",
        forward_join,
        identity,
        False,
    )
    from_after = prefix(
        (reverse_elem[0], reverse_elem[1], reverse_elem[2], reverse_elem[3]),
        "ctx",
        reverse_join,
        identity,
        True,
    )
    entering = before[1] * (before[3][0] == seg_float[0]).astype(jnp.float32)
    states = []
    for number in range(span_count):
        states.append(entering)
        carried = summaries[number][0][..., None, None] * entering + summaries[number][1]
        if number + 1 < span_count:
            entering = carried * (seg_all[number][-1] == seg_all[number + 1][0]).astype(jnp.float32)
    arriving = from_after[1] * (from_after[2][0] == seg_float[-1]).astype(jnp.float32)
    prev_link = jnp.concatenate(
        [jnp.zeros((1,), jnp.float32), (seg_all[1:, 0] == seg_all[:-1, -1]).astype(jnp.float32)]
    )
    decayed_all = jnp.stack([item[0] for item in summaries])
    reverse_all = jnp.stack([item[2] for item in summaries])
    state_all = jnp.stack(states)

    def backward_step(adjoint_now, blocks):
        x_blk, dt_blk, b_blk, c_blk, dy_blk, seg_blk, state_in, decayed, reverse_sum, link = blocks
        grads = span_grads(
            x_blk, dy_blk, b_blk, c_blk, dt_blk, decay_rate, seg_blk, state_in, adjoint_now
        )
        carried = decayed[..., None, None] * adjoint_now + reverse_sum
        return (carried * link, grads)

    final_adjoint, results = lax.scan(
        backward_step,
        arriving,
        (
            x_all,
            dt_all,
            b_all,
            c_all,
            dy_all,
            seg_all,
            state_all,
            decayed_all,
            reverse_all,
            prev_link,
        ),
        reverse=True,
    )
    grad_in = results[0].reshape(inputs.shape).astype(jnp.bfloat16)
    grad_step = results[1].reshape(step_size.shape)
    part_b = results[2].reshape(b_proj.shape)
    part_c = results[3].reshape(c_proj.shape)
    whole_b, whole_c = lax.psum((part_b, part_c), "head")
    own_width = part_b.shape[1] // lax.axis_size("head")
    offset = lax.axis_index("head") * own_width
    total_b = lax.dynamic_slice_in_dim(whole_b, offset, own_width, 1)
    total_c = lax.dynamic_slice_in_dim(whole_c, offset, own_width, 1)
    return (grad_in, grad_step, total_b, total_c)


def solution(mesh):
    placed = (
        P("ctx", None, "head"),
        P("ctx", None, "head"),
        P(None, "head"),
        P("ctx", None, None),
        P("ctx", None, None),
        P("ctx", None, "head"),
        P("ctx"),
    )
    return jax.shard_map(
        per_device,
        mesh=mesh,
        in_specs=placed,
        out_specs=(
            P("ctx", None, "head"),
            P("ctx", None, "head"),
            P("ctx", "head", None),
            P("ctx", "head", None),
        ),
        check_vma=False,
    )
```

profile of v0, /device:TPU:1, one launch (start us, length us, event | category | flops | bytes accessed | tf_op | source)
XLA Modules:
  0.0 1175.4 jit_solution(16546699100830403924)
XLA Ops:
  17.0 3.3 compare_convert_fusion.2
  22.1 23.3 %fusion.98 = f32[128,8,4]{2,1,0:T(8,128)S(1)} fusion(f32[128,8,4]{2,1,0:T(8,128)S(1)} %copy.204), kind=kOutput, calls=%fused_computation.176 | output fusion | flops 520192 | bytes 32768 | tf_op jit(solution)/shard_map/jit(cumsum)/reduce_window_sum | solution.py:36
  45.6 23.3 %fusion.99 = f32[128,8,4]{2,1,0:T(8,128)S(1)} fusion(f32[128,8,4]{2,1,0:T(8,128)S(1)} %copy.211), kind=kOutput, calls=%fused_computation.177 | output fusion | flops 520192 | bytes 32768 | tf_op jit(solution)/shard_map/jit(cumsum)/reduce_window_sum | solution.py:36
  84.4 4.4 reshape.312
  88.9 4.4 reshape.313
  95.0 54.4 %all_gather.38 = f32[64,8,4]{1,2,0:T(4,128)S(1)} all-gather(f32[1,8,4]{1,2,0:T(4,128)S(1)} %copy.214), channel_id=1, replica_groups=mesh['ctx'=64,'head'=4] {'ctx'}, dimensions={0}, use_global_device_ids=true | all-gather | bytes 8320 | tf_op jit(solution)/shard_map/all_gather | solution.py:16
  150.2 126.9 %all-reduce.2 = (f32[64]{0:T(128)S(1)}, f32[64]{0:T(128)S(1)}) all-reduce(f32[64]{0:T(128)S(1)} %fusion.85, f32[64]{0:T(128)S(1)} %get-tuple-element.922), channel_id=3, replica_groups=mesh['ctx'=64,'head'=4] {'ctx'}, use_global_device_ids=true, to_apply=%add | all-reduce | flops 128 | bytes 1024
  277.4 4.3 copy.231
  281.7 4.3 copy.235
  288.0 49.5 %all_gather.43 = f32[64,8,4]{1,2,0:T(4,128)S(1)} all-gather(f32[1,8,4]{1,2,0:T(4,128)S(1)} %copy.218), channel_id=1, replica_groups=mesh['ctx'=64,'head'=4] {'ctx'}, dimensions={0}, use_global_device_ids=true | all-gather | bytes 8320 | tf_op jit(solution)/shard_map/all_gather | solution.py:16
  341.0 288.6 %while.56 = (s32[]{:T(128)}, f32[8,4,64,128]{3,2,1,0:T(8,128)S(1)}, f32[1]{0:T(128)}, s32[]{:T(128)}, f32[64,8,4]{1,2,0:T(4,128)S(1)}, /*index=5*/f32[64,1]{0,1:...) while((s32[]{:T(128)}, f32[8,4,64,128]{3,2,1,0:T(8,128)S(1)}, ...), condition=%wide.region_5.6_spmd.clone, body=%wide.region_4.5_spmd.clone.sunk | while | flops 1048621 | bytes 3146602 | solution.py:28
  630.2 43.7 %rev.12 = f32[64,8,4,64,128]{4,3,2,1,0:T(8,128)} reverse(f32[64,8,4,64,128]{4,3,2,1,0:T(8,128)} %bitcast.48), dimensions={0} | reverse | bytes 134217728 | tf_op jit(solution)/shard_map/rev | solution.py:18
  673.9 297.8 %while.55 = (s32[]{:T(128)}, f32[8,4,64,128]{3,2,1,0:T(8,128)S(1)}, f32[1]{0:T(128)}, s32[]{:T(128)}, f32[64,8,4,64,128]{4,3,2,1,0:T(8,128)}, /*index=5*/f32[64,...) while((s32[]{:T(128)}, f32[8,4,64,128]{3,2,1,0:T(8,128)S(1)}, ...), condition=%wide.region_3.4_spmd.clone, body=%wide.region_2.3_spmd.clone.sunk | while | flops 1048621 | bytes 3146602 | solution.py:28
  978.5 123.4 %while.54 = (s32[]{:T(128)}, f32[8,4,64,128]{3,2,1,0:T(8,128)S(1)}, bf16[2,128,8,4,64]{1,4,3,2,0:T(8,128)(2,1)}, f32[2,128,8,4]{3,2,1,0:T(8,128)}, f32[2,128,8,1...) while((s32[]{:T(128)}, f32[8,4,64,128]{3,2,1,0:T(8,128)S(1)}, ...), condition=%wide.region_16.17_spmd, body=%wide.region_6.16_spmd.sunk | while | flops 2944414208 | bytes 62161760 | solution.py:204
  987.7 4.3 fusion.162
  993.5 3.6 fusion.164
  1005.7 3.1 fusion.166
  1018.6 2.9 bitcast_dynamic-update-slice_fusion.2
  1031.6 2.8 multiply_reduce_fusion.7
  1049.3 4.3 fusion.162
  1055.2 3.6 fusion.164
  1067.3 3.1 fusion.166
  1080.3 2.9 bitcast_dynamic-update-slice_fusion.2
  1108.1 56.7 %all-reduce.6.cloned.1.call-done = (f32[256,8,128]{2,1,0:T(8,128)}, f32[256,8,128]{2,1,0:T(8,128)}) async-done(((f32[256,8,128]{2,1,0:T(8,128)}, f32[256,8,128]{2,1,0:T(8,128)}), (f32[256,8,128]{2,1,0:T(8,128)}, f32[256,8,128]{2,1,0:T(8,128)})) %all-reduce.6.cloned.1.call-update) | async-done | bytes 2097168 | tf_op jit(solution)/shard_map/psum | solution.py:225
  (739 shorter events, 408.6 us)
Async XLA Ops:
  7.2 333.8 %all-gather.9.cloned.1.call-start = ((), (), s32[]{:S(2)}) async-start(), calls=%async_computation.1 | async-start | bytes 68157440 | tf_op jit(solution)/shard_map/all_gather | solution.py:16
  21.8 47.9 %copy-start.14 = (bf16[256,8,256]{2,1,0:T(8,128)(2,1)S(1)}, bf16[256,8,256]{2,1,0:T(8,128)(2,1)}, u32[]{:S(2)}) copy-start(bf16[256,8,256]{2,1,0:T(8,128)(2,1)} %param.13) | copy-start | bytes 3145732
  69.0 3.1 copy-start.10
  76.1 554.1 %all-gather.7.cloned.1.call-start = ((), (), s32[]{:S(2)}) async-start(), calls=%async_computation | async-start | bytes 68157440 | tf_op jit(solution)/shard_map/all_gather | solution.py:16
  77.3 3.0 copy-start.12
  83.1 1081.7 %all-reduce.6.cloned.1.call-start = ((), (), s32[]{:S(2)}) async-start(), calls=%async_computation.2 | async-start | bytes 4194304 | tf_op jit(solution)/shard_map/psum | solution.py:225
  88.9 4.4 copy-start.20
  88.9 5.8 copy-start.22
  673.9 298.4 %copy-start.9 = (f32[8,4,64,128]{3,2,1,0:T(8,128)S(1)}, f32[8,4,64,128]{3,2,1,0:T(8,128)}, u32[]{:S(2)}) copy-start(f32[8,4,64,128]{3,2,1,0:T(8,128)} %copy-done.8) | copy-start | bytes 3145732
  993.5 3.6 copy-start.11
  993.5 4.4 copy-start.7
  1005.7 3.1 copy-start.1
  1012.1 3.4 copy-start.19
  1018.6 2.9 copy-start.6
  1036.1 2.8 copy-start.3
  1036.1 2.8 copy-start.4
  1036.1 2.8 copy-start.16
  1055.2 3.6 copy-start.11
  1055.2 4.4 copy-start.7
  1067.3 3.1 copy-start.1
  1073.8 3.5 copy-start.19
  1080.3 2.9 copy-start.6
  1097.8 2.8 copy-start.4
  1097.8 2.8 copy-start.16
  (14 other events, 21.2 us)
Sparse Core Ops, SparseCore 0:
  76.2 242.4 all-gather.8
  322.0 233.1 all-gather.6
  1102.0 62.7 all-reduce.5
where the time goes:
time: 1190 us; the launch traced here: 1180 us
  loops' own time  314 us (26%)
  other arithmetic  267 us (22%)
  blocking collectives  231 us (19%)
  local copies, waits for them, and re-layouts  229 us (19%)
  waiting for transfers between devices  56.8 us (5%)
  matrix products  54 us (5%)
  between operations  23.1 us (2%)
    another operation x2, loops' own time, prefix(): return lax.fori_loop(0, count - 1, turn, total)  314 us
    select_n x126, other arithmetic, turn(): jnp.where(position < mine, new, old)  185 us
    unnamed x1, blocking collectives  127 us
    all_gather x2, blocking collectives, prefix(): pieces = jax.tree.map(lambda part: lax.all_gather(part, axis), value)  104 us
    dynamic_slice x126, local copies, waits for them, and re-layouts, turn(): longer = join(total, jax.tree.map(lambda part: part[position], pieces))  75.2 us
    psum x1, waiting for transfers between devices, per_device(): whole_b, whole_c = lax.psum((part_b, part_c), 'head')  56.7 us
    another operation x4, other arithmetic, span_weights(): cumlog = jnp.cumsum(step_size * decay_rate[None], axis=0)  46.9 us
    dot_general x20, matrix products, product(): return jnp.einsum(pattern, first_op, second_op, precision=PRECISE)  46.2 us
  transfers between devices with their start and end apart: 3, of which 1 were waited for; matrix products, arithmetic and copies ran while one was open for 15% of the time, Pallas kernels for 0%

commit v1 on v0

v1 whole, which is shorter than its diff:
```python
import functools

import jax
import jax.numpy as jnp
from jax import lax
from jax.experimental import pallas as pl
from jax.experimental.pallas import tpu as pltpu
from jax.sharding import Mesh, PartitionSpec as P

F32 = jnp.float32
BF16 = jnp.bfloat16
T = 256
G = 8
J = 4
W = 256
N = 128
ROWS = N + 8
DEC, FIRST, LAST, ELAST = N, N + 1, N + 2, N + 3
VMEM = pltpu.CompilerParams(vmem_limit_bytes=56 * 1024 * 1024)
Z, Y, C, X = "z", "y", "core", "head"


def dot(a, b):
    return lax.dot_general(a, b, (((1,), (0,)), ((), ())), preferred_element_type=F32)


def dot_t(a, b):
    return lax.dot_general(a, b, (((1,), (1,)), ((), ())), preferred_element_type=F32)


def split2(v):
    hi = v.astype(BF16)
    return hi, (v - hi.astype(F32)).astype(BF16)


def split3(v):
    hi = v.astype(BF16)
    rest = v - hi.astype(F32)
    mid = rest.astype(BF16)
    return hi, mid, (rest - mid.astype(F32)).astype(BF16)


def iota(shape, dim):
    return lax.broadcasted_iota(jnp.int32, shape, dim)


def head_ones():
    return (iota((8, W), 0) == iota((8, W), 1) // 64).astype(BF16)


def expander(g):
    k = iota((128, W), 0)
    return ((k < 96) & (k % 32 == J * g + iota((128, W), 1) // 64)).astype(BF16)


def head_sums(ones, z):
    hi, lo = split2(z)
    return dot_t(ones, hi) + dot_t(ones, lo)


def token_rows(seg_row):
    padded = jnp.concatenate([seg_row, jnp.zeros((7, T), F32)], axis=0).astype(BF16)
    ones = jnp.ones((8, T), BF16)
    return lax.dot_general(padded, ones, (((0,), (0,)), ((), ())), preferred_element_type=F32)


def masks(seg_row):
    seg_t = token_rows(seg_row)
    same = seg_t == seg_row
    low = same & (iota((T, T), 1) <= iota((T, T), 0))
    high = same & (iota((T, T), 1) >= iota((T, T), 0))
    first = seg_t[:, :N] == seg_t[0:1, :N]
    last = seg_t[:, :N] == seg_t[T - 1 : T, :N]
    return low, high, first, last


def order(i, pos):
    half = jnp.where(i < 4, 1 - pos[0], pos[0])
    return 4 * half + lax.rem(pos[1] + lax.rem(i, 4), 4)


def summary_kernel(
    pos, dt_ref, rate_ref, seg_ref, x_ref, dy_ref, b_ref, c_ref,
    xh_ref, xl_ref, dh_ref, dl_ref, bt_ref, ct_ref, qt_ref, fs_ref, fk_ref, rs_ref, rk_ref,
    x_s, dy_s, b_s, c_s, a_s, dt_s, et_s, first_s, last_s, meta_s,
):
    i = pl.program_id(0)
    g = order(i, pos)

    @pl.when(i == 0)
    def _():
        for j in range(J):
            for k in range(G):
                dt_s[J * k + j : J * k + j + 1, :] = dt_ref[k, j : j + 1, :]
                a_s[J * k + j : J * k + j + 1, :] = dt_ref[k, j : j + 1, :] * rate_ref[j, k]
        x_s[...] = jnp.swapaxes(x_ref[...], 0, 1)
        dy_s[...] = jnp.swapaxes(dy_ref[...], 0, 1)
        b_s[...] = jnp.swapaxes(b_ref[...], 0, 1)
        c_s[...] = jnp.swapaxes(c_ref[...], 0, 1)
        upto = (iota((T, T), 0) <= iota((T, T), 1)).astype(BF16)
        cum3 = dot(jnp.concatenate(split3(a_s[...]), axis=0), upto)
        cum = cum3[:32] + cum3[32:64] + cum3[64:96]
        e = jnp.exp(cum)
        q = jnp.exp(-cum) * dt_s[...]
        zero = jnp.zeros((32, T), F32)

        def columns(v):
            pieces = [piece.astype(F32) for piece in split3(v)]
            return jnp.transpose(jnp.concatenate(pieces + [zero], axis=0)).astype(BF16)

        et_s[...] = columns(e)
        qt_ref[...] = columns(q)
        seg_row = seg_ref[...].astype(F32)
        seg_t = token_rows(seg_row)
        first_s[...] = (seg_t[:, :N] == seg_t[0:1, :N]).astype(BF16)
        last_s[...] = (seg_t[:, :N] == seg_t[T - 1 : T, :N]).astype(BF16)
        meta_s[0:1, :] = seg_t[0:1, :]
        meta_s[1:2, :] = seg_t[T - 1 : T, :]

    spread = expander(g)
    e = dot(et_s[...], spread)
    q = dot(qt_ref[...], spread)
    xh, xl = split2(x_s[g].astype(F32) * q)
    dh, dl = split2(dy_s[g].astype(F32) * e)
    xh_ref[0], xl_ref[0], dh_ref[0], dl_ref[0] = xh, xl, dh, dl
    b, c = b_s[g], c_s[g]
    bt_ref[0], ct_ref[0] = b, c
    b_tr = jnp.transpose(b * last_s[...])
    c_tr = jnp.transpose(c * first_s[...])
    e_last = e[T - 1 : T, :]
    forward = (dot(b_tr, xh) + dot(b_tr, xl)) * e_last
    reverse = dot(c_tr, dh) + dot(c_tr, dl)
    first, last = meta_s[0:1, :], meta_s[1:2, :]
    whole = (first == last).astype(F32)
    tail = jnp.concatenate([e_last * whole, first, last, e_last, jnp.zeros((4, W), F32)], axis=0)

    def put(f_ref, r_ref):
        f_ref[0, :N, :] = forward
        f_ref[0, N:, :] = tail
        r_ref[0, :N, :] = reverse
        r_ref[0, N:, :] = tail

    pl.when(i < 4)(lambda: put(fs_ref, rs_ref))
    pl.when(i >= 4)(lambda: put(fk_ref, rk_ref))


def whole_spec(shape):
    return pl.BlockSpec(shape, lambda i, pos: (0,) * len(shape))


def summaries(pos, dt, rate, seg, x, dy, b, c):
    at = lambda i, pos: (order(i, pos), 0, 0)
    sent = pl.BlockSpec((1, ROWS, W), lambda i, pos: (jnp.minimum(i, 3), 0, 0))
    kept = pl.BlockSpec((1, ROWS, W), lambda i, pos: (jnp.maximum(i - 4, 0), 0, 0))
    wide = pl.BlockSpec((1, T, W), at)
    slim = pl.BlockSpec((1, T, N), at)
    grid = pltpu.PrefetchScalarGridSpec(
        num_scalar_prefetch=1,
        grid=(G,),
        in_specs=[
            whole_spec((G, J, T)),
            pl.BlockSpec(memory_space=pltpu.SMEM),
            whole_spec((1, T)),
            whole_spec((T, G, W)),
            whole_spec((T, G, W)),
            whole_spec((T, G, N)),
            whole_spec((T, G, N)),
        ],
        out_specs=[wide] * 4 + [slim] * 2 + [whole_spec((T, N))] + [sent, kept, sent, kept],
        scratch_shapes=[
            pltpu.VMEM((G, T, W), BF16),
            pltpu.VMEM((G, T, W), BF16),
            pltpu.VMEM((G, T, N), BF16),
            pltpu.VMEM((G, T, N), BF16),
            pltpu.VMEM((32, T), F32),
            pltpu.VMEM((32, T), F32),
            pltpu.VMEM((T, N), BF16),
            pltpu.VMEM((T, N), BF16),
            pltpu.VMEM((T, N), BF16),
            pltpu.VMEM((8, T), F32),
        ],
    )
    big = jax.ShapeDtypeStruct((G, T, W), BF16)
    thin = jax.ShapeDtypeStruct((G, T, N), BF16)
    block = jax.ShapeDtypeStruct((4, ROWS, W), F32)
    return pl.pallas_call(
        summary_kernel,
        grid_spec=grid,
        out_shape=[big] * 4 + [thin] * 2 + [jax.ShapeDtypeStruct((T, N), BF16)] + [block] * 4,
        compiler_params=VMEM,
        cost_estimate=pl.CostEstimate(flops=8 * 10**9, bytes_accessed=10 * 2**20, transcendentals=0),
        name="summaries",
    )(pos, dt, rate, seg, x, dy, b, c)


def local_kernel(
    seg_ref, xh_ref, xl_ref, dh_ref, dl_ref, b_ref, c_ref,
    gc_ref, gb_ref, raw_ref, u_ref,
    low_s, high_s,
):
    @pl.when(pl.program_id(0) == 0)
    def _():
        low, high, _, _ = masks(seg_ref[...].astype(F32))
        low_s[...] = low.astype(F32)
        high_s[...] = high.astype(F32)

    xh, xl, dh, dl = xh_ref[0], xl_ref[0], dh_ref[0], dl_ref[0]
    b, c = b_ref[0], c_ref[0]
    sums = dot_t(dh, xh) + dot_t(dh, xl) + dot_t(dl, xh)
    sh, sl = split2(sums * low_s[...])
    gc_ref[0] = dot(sh, b) + dot(sl, b)
    c_tr = jnp.transpose(c)
    gb_ref[0] = jnp.transpose(dot(c_tr, sh) + dot(c_tr, sl))
    wh, wl = split2(dot_t(c, b) * low_s[...])
    out = dot(wh, xh) + dot(wh, xl) + dot(wl, xh)
    u_ref[0] = head_sums(head_ones(), out * (dh.astype(F32) + dl.astype(F32)))
    vh, vl = split2(dot_t(b, c) * high_s[...])
    raw_ref[0] = dot(vh, dh) + dot(vh, dl) + dot(vl, dh)


def local_grads(seg, xh, xl, dh, dl, b, c):
    at = lambda i: (i, 0, 0)
    wide = pl.BlockSpec((1, T, W), at)
    slim = pl.BlockSpec((1, T, N), at)
    return pl.pallas_call(
        local_kernel,
        grid=(G,),
        in_specs=[pl.BlockSpec((1, T), lambda i: (0, 0))] + [wide] * 4 + [slim] * 2,
        out_specs=[slim, slim, wide, pl.BlockSpec((1, 8, T), at)],
        out_shape=[
            jax.ShapeDtypeStruct((G, T, N), F32),
            jax.ShapeDtypeStruct((G, T, N), F32),
            jax.ShapeDtypeStruct((G, T, W), F32),
            jax.ShapeDtypeStruct((G, 8, T), F32),
        ],
        scratch_shapes=[pltpu.VMEM((T, T), F32), pltpu.VMEM((T, T), F32)],
        compiler_params=VMEM,
        cost_estimate=pl.CostEstimate(flops=10 * 10**9, bytes_accessed=12 * 2**20, transcendentals=0),
        name="local_grads",
    )(seg, xh, xl, dh, dl, b, c)


def linked(earlier, later):
    return (earlier[LAST : LAST + 1, :] == later[FIRST : FIRST + 1, :]).astype(F32)


def join(earlier, later, out, rev):
    link = linked(earlier, later)
    near, far = (earlier, later) if rev else (later, earlier)
    out[:N, :] = near[:N, :] + (near[DEC : DEC + 1, :] * link) * far[:N, :]
    both = earlier[DEC : DEC + 1, :] * later[DEC : DEC + 1, :] * link
    out[N:, :] = jnp.concatenate(
        [both, earlier[FIRST : FIRST + 1, :], later[LAST : LAST + 1, :], jnp.zeros((5, W), F32)], axis=0
    )


def small_call(body, name, n_out, shape, pos, args, scratch=()):
    vmem = pl.BlockSpec(memory_space=pltpu.VMEM)
    return pl.pallas_call(
        body,
        in_specs=[pl.BlockSpec(memory_space=pltpu.SMEM)] + [vmem] * len(args),
        out_specs=[vmem] * n_out,
        out_shape=[jax.ShapeDtypeStruct(shape, F32)] * n_out,
        scratch_shapes=list(scratch),
        compiler_params=VMEM,
        cost_estimate=pl.CostEstimate(flops=10**9, bytes_accessed=2 * 2**20, transcendentals=0),
        name=name,
    )(pos, *args)


def chip_join(pos, kept, got, rev):
    def body(pos, kept, got, *outs):
        def go(earlier, later):
            for s in range(4):
                join(earlier.at[s], later.at[s], outs[s], rev)

        pl.when(pos[0] == 0)(lambda: go(kept, got))
        pl.when(pos[0] == 1)(lambda: go(got, kept))

    return small_call(body, "chip_join", 4, (ROWS, W), pos, (kept, got))


def plane_join(pos, blocks, rev):
    def body(pos, *refs):
        blocks, out, order_s, one, two = refs[:4], refs[4], refs[5], refs[6], refs[7]
        for s in range(4):
            order_s[lax.rem(pos[1] + 4 - s, 4)] = blocks[s][...]
        join(order_s.at[0], order_s.at[1], one, rev)
        join(order_s.at[2], order_s.at[3], two, rev)
        join(one, two, out, rev)

    scratch = [pltpu.VMEM((4, ROWS, W), F32), pltpu.VMEM((ROWS, W), F32), pltpu.VMEM((ROWS, W), F32)]
    return small_call(body, "plane_join", 1, (ROWS, W), pos, blocks, scratch)[0]


def plane_enter(pos, blocks, near, far, rev):
    def body(pos, *refs):
        blocks, near, far, outs, order_s, enter_s = refs[:4], refs[4], refs[5], refs[6:10], refs[10], refs[11]
        for s in range(4):
            order_s[lax.rem(pos[1] + 4 - s, 4)] = blocks[s][...]

        def link(one, two):
            return linked(two, one) if rev else linked(one, two)

        start, ahead = (3, -1) if rev else (0, 1)
        own = order_s.at[start]
        carry = near[:N, :] + (near[DEC : DEC + 1, :] * link(far, near)) * far[:N, :]
        enter_s[start] = link(near, own) * carry
        for step in range(3):
            here, there = start + step * ahead, start + (step + 1) * ahead
            block = order_s.at[here]
            hop = link(block, order_s.at[there])
            enter_s[there] = hop * (block[:N, :] + block[DEC : DEC + 1, :] * enter_s[here])
        for s in range(4):
            outs[s][...] = enter_s[lax.rem(pos[1] + s, 4)]

    scratch = [pltpu.VMEM((4, ROWS, W), F32), pltpu.VMEM((4, N, W), F32)]
    return small_call(body, "plane_enter", 4, (N, W), pos, (*blocks, near, far), scratch)


def device_enter(pos, entering, kept, got, rev):
    def body(pos, *refs):
        entering, kept, got, mine, other = refs[:4], refs[4], refs[5], refs[6], refs[7]

        def go(zero, one, direct, passed):
            inner = one if rev else zero
            for s in range(4):
                k, slot = lax.rem(pos[1] + 4 - s, 4), (4 - s) % 4
                link = linked(zero.at[slot], one.at[slot])
                block = inner.at[slot]
                direct[k] = entering[s][...]
                passed[k] = link * (block[:N, :] + block[DEC : DEC + 1, :] * entering[s][...])

        pl.when(pos[0] == 0)(lambda: go(kept, got, *((other, mine) if rev else (mine, other))))
        pl.when(pos[0] == 1)(lambda: go(got, kept, *((mine, other) if rev else (other, mine))))

    return small_call(body, "device_enter", 2, (4, N, W), pos, (*entering, kept, got))


def ring(count, shift):
    return [(i, (i + shift) % count) for i in range(count)]


def swap(v):
    return lax.ppermute(v, C, ring(2, 1))


def along_y(v, shift):
    return lax.ppermute(v, Y, ring(4, shift))


def along_z(v, shift):
    return lax.ppermute(v, Z, ring(8, shift))


def along_x(v, shift):
    return lax.ppermute(v, X, ring(4, shift))


def carried(pos, sent, kept, rev):
    sign = -1 if rev else 1
    got = swap(sent)
    blocks = chip_join(pos, kept, got, rev)
    blocks = [blocks[0]] + [along_y(blocks[s], s) for s in (1, 2, 3)]
    plane = plane_join(pos, blocks, rev)
    near, far = along_z(plane, sign), along_z(plane, 2 * sign)
    entering = plane_enter(pos, blocks, near, far, rev)
    entering = [entering[0]] + [along_y(entering[s], s) for s in (1, 2, 3)]
    mine, other = device_enter(pos, entering, kept, got, rev)
    return mine, swap(other)


def turned(i, pos):
    return lax.rem(2 * pos[2] + i, G)


def put_by_turn(i, outs, value):
    for s in range(4):

        @pl.when(i // 2 == s)
        def _(s=s):
            outs[s][0] = value


def state_kernel(
    pos, seg_ref, dh_ref, dl_ref, c_ref, gc_ref, u_ref, mine_ref, got_ref,
    o0, o1, o2, o3, u_out,
    first_s,
):
    i = pl.program_id(0)
    g = turned(i, pos)

    @pl.when(i == 0)
    def _():
        first_s[...] = masks(seg_ref[...].astype(F32))[2].astype(F32)

    state = jnp.where(g // 4 == pos[0], mine_ref[0], got_ref[0])
    sh, sl = split2(state)
    dh, dl = dh_ref[0], dl_ref[0]
    carried_c = dot_t(dh, sh) + dot_t(dh, sl) + dot_t(dl, sh)
    put_by_turn(i, (o0, o1, o2, o3), gc_ref[0] + first_s[...] * carried_c)
    c = c_ref[0] * first_s[...].astype(BF16)
    out = dot(c, sh) + dot(c, sl)
    u_out[0] = u_ref[0] + head_sums(head_ones(), out * (dh.astype(F32) + dl.astype(F32)))


def turn_specs():
    def spec(s):
        return pl.BlockSpec((1, T, N), lambda i, pos: (jnp.clip(i - 2 * s, 0, 1), 0, 0))

    return [spec(s) for s in range(4)]


def half_spec(rows):
    return pl.BlockSpec((1, rows, W), lambda i, pos: (lax.rem(turned(i, pos), 4), 0, 0))


def state_grads(pos, seg, dh, dl, c, gc, u, mine, got):
    at = lambda i, pos: (turned(i, pos), 0, 0)
    wide = pl.BlockSpec((1, T, W), at)
    slim = pl.BlockSpec((1, T, N), at)
    heads = pl.BlockSpec((1, 8, T), at)
    grid = pltpu.PrefetchScalarGridSpec(
        num_scalar_prefetch=1,
        grid=(G,),
        in_specs=[whole_spec((1, T)), wide, wide, slim, slim, heads, half_spec(N), half_spec(N)],
        out_specs=turn_specs() + [heads],
        scratch_shapes=[pltpu.VMEM((T, N), F32)],
    )
    return pl.pallas_call(
        state_kernel,
        grid_spec=grid,
        out_shape=[jax.ShapeDtypeStruct((2, T, N), F32)] * 4 + [jax.ShapeDtypeStruct((G, 8, T), F32)],
        compiler_params=VMEM,
        cost_estimate=pl.CostEstimate(flops=4 * 10**9, bytes_accessed=6 * 2**20, transcendentals=0),
        name="state_grads",
    )(pos, seg, dh, dl, c, gc, u, mine, got)


def adjoint_kernel(
    pos, seg_ref, dt_ref, rate_ref, qt_ref, xh_ref, xl_ref, b_ref, gb_ref, raw_ref, u_ref,
    smine_ref, sgot_ref, amine_ref, agot_ref, rk_ref, rs_ref,
    o0, o1, o2, o3, gi_ref, gs_ref,
    last_s, low_s, gi_s, v_s, u_s, k_s, dt_s, rate_s,
):
    i = pl.program_id(0)
    g = turned(i, pos)

    @pl.when(i == 0)
    def _():
        low, _, _, last = masks(seg_ref[...].astype(F32))
        last_s[...] = last.astype(F32)
        low_s[...] = low.astype(BF16)
        for j in range(J):
            for k in range(G):
                row = slice(J * k + j, J * k + j + 1)
                dt_s[row, :] = dt_ref[k, j : j + 1, :]
                rate_s[row, :] = jnp.full((1, T), rate_ref[j, k], F32)

    ours = g // 4 == pos[0]
    adjoint = jnp.where(ours, amine_ref[0], agot_ref[0])
    state = jnp.where(ours, smine_ref[0], sgot_ref[0])
    reverse = jnp.where(ours, rk_ref[0], rs_ref[0])
    ones = head_ones()
    crossing = state * (reverse[:N] + reverse[DEC : DEC + 1] * adjoint)
    k_s[g] = head_sums(ones, crossing)
    ah, al = split2(adjoint * reverse[ELAST : ELAST + 1])
    xh, xl = xh_ref[0], xl_ref[0]
    carried_b = dot_t(xh, ah) + dot_t(xh, al) + dot_t(xl, ah)
    put_by_turn(i, (o0, o1, o2, o3), gb_ref[0] + last_s[...] * carried_b)
    b = b_ref[0] * last_s[...].astype(BF16)
    raw = raw_ref[0] + dot(b, ah) + dot(b, al)
    q = dot(qt_ref[...], expander(g))
    gi_s[g] = (q * raw).astype(BF16)
    v_s[g] = head_sums(ones, raw * (xh.astype(F32) + xl.astype(F32)))
    u_s[g] = u_ref[0]

    @pl.when(i == G - 1)
    def _():
        gi_ref[...] = jnp.swapaxes(gi_s[...], 0, 1)
        v = jnp.concatenate([v_s[k][:J] for k in range(G)], axis=0)
        u = jnp.concatenate([u_s[k][:J] for k in range(G)], axis=0)
        cross = jnp.concatenate([k_s[k][:J] for k in range(G)], axis=0)
        total = jnp.sum(cross, axis=1, keepdims=True)
        change = v - u + jnp.where(iota((32, T), 1) == 0, total, 0.0)
        run3 = dot_t(jnp.concatenate(split3(change), axis=0), low_s[...])
        inter = run3[:32] + run3[32:64] + run3[64:96] + u
        grad = v / dt_s[...] + rate_s[...] * (inter - v)
        for k in range(G):
            gs_ref[k] = grad[J * k : J * k + J]


def adjoint_grads(pos, seg, dt, rate, qt, xh, xl, b, gb, raw, u, smine, sgot, amine, agot, rk, rs):
    at = lambda i, pos: (turned(i, pos), 0, 0)
    wide = pl.BlockSpec((1, T, W), at)
    slim = pl.BlockSpec((1, T, N), at)
    heads = pl.BlockSpec((1, 8, T), at)
    slot = pl.BlockSpec((1, ROWS, W), lambda i, pos: (lax.rem(turned(i, pos) + 4 - pos[1], 4), 0, 0))
    grid = pltpu.PrefetchScalarGridSpec(
        num_scalar_prefetch=1,
        grid=(G,),
        in_specs=[
            whole_spec((1, T)),
            whole_spec((G, J, T)),
            pl.BlockSpec(memory_space=pltpu.SMEM),
            whole_spec((T, N)),
            wide, wide, slim, slim, wide, heads,
            half_spec(N), half_spec(N), half_spec(N), half_spec(N), slot, slot,
        ],
        out_specs=turn_specs() + [whole_spec((T, G, W)), whole_spec((G, J, T))],
        scratch_shapes=[
            pltpu.VMEM((T, N), F32),
            pltpu.VMEM((T, T), BF16),
            pltpu.VMEM((G, T, W), BF16),
            pltpu.VMEM((G, 8, T), F32),
            pltpu.VMEM((G, 8, T), F32),
            pltpu.VMEM((G, 8, N), F32),
            pltpu.VMEM((32, T), F32),
            pltpu.VMEM((32, T), F32),
        ],
    )
    return pl.pallas_call(
        adjoint_kernel,
        grid_spec=grid,
        out_shape=[jax.ShapeDtypeStruct((2, T, N), F32)] * 4
        + [jax.ShapeDtypeStruct((T, G, W), BF16), jax.ShapeDtypeStruct((G, J, T), F32)],
        compiler_params=VMEM,
        cost_estimate=pl.CostEstimate(flops=6 * 10**9, bytes_accessed=9 * 2**20, transcendentals=0),
        name="adjoint_grads",
    )(pos, seg, dt, rate, qt, xh, xl, b, gb, raw, u, smine, sgot, amine, agot, rk, rs)


def over_heads(parts):
    got = [along_x(parts[s], s) for s in (1, 2, 3)]
    return jnp.transpose(parts[0] + got[0] + got[1] + got[2], (1, 0, 2))


def per_device(inputs, step_size, decay_rate, b_proj, c_proj, grad_out, segment_ids):
    pos = jnp.stack([lax.axis_index(C), lax.axis_index(Y), lax.axis_index(X)]).astype(jnp.int32)
    seg = segment_ids.reshape(1, T)
    dt = jnp.transpose(step_size, (1, 2, 0))
    rate = jnp.transpose(decay_rate)
    xh, xl, dh, dl, b, c, qt, fs, fk, rs, rk = summaries(pos, dt, rate, seg, inputs, grad_out, b_proj, c_proj)
    gc, gb, raw, u = local_grads(seg, xh, xl, dh, dl, b, c)
    smine, sgot = carried(pos, fs, fk, False)
    amine, agot = carried(pos, rs, rk, True)
    *parts_c, u = state_grads(pos, seg, dh, dl, c, gc, u, smine, sgot)
    total_c = over_heads(parts_c)
    *parts_b, grad_in, grad_step = adjoint_grads(
        pos, seg, dt, rate, qt, xh, xl, b, gb, raw, u, smine, sgot, amine, agot, rk, rs
    )
    total_b = over_heads(parts_b)
    return grad_in, jnp.transpose(grad_step, (2, 0, 1)), total_b, total_c


def solution(mesh):
    fine = Mesh(mesh.devices.reshape(8, 4, 2, 4), (Z, Y, C, X))
    ctx = (Z, Y, C)
    placed = (
        P(ctx, None, X),
        P(ctx, None, X),
        P(None, X),
        P(ctx, None, None),
        P(ctx, None, None),
        P(ctx, None, X),
        P(ctx),
    )
    return jax.shard_map(
        per_device,
        mesh=fine,
        in_specs=placed,
        out_specs=(P(ctx, None, X), P(ctx, None, X), P(ctx, X, None), P(ctx, X, None)),
        check_vma=False,
    )
```

time: 1190 us -> 132 us (0.11); the launches traced: 1180 us -> 131 us
  loops' own time: 314 us -> 0 us
  other arithmetic: 267 us -> 1.68 us
  blocking collectives: 231 us -> 0 us
  local copies, waits for them, and re-layouts: 229 us -> 10.4 us
  Pallas kernels: 0 us -> 65.2 us
  matrix products: 54 us -> 0 us
  waiting for transfers between devices: 56.8 us -> 12.6 us
  starting transfers between devices: 0.12 us -> 40.6 us
  between operations: 23.1 us -> 0.82 us
    another operation x3 -> x0, loops' own time: 314 us -> none  [the longest x2 314 us: prefix(): return lax.fori_loop(0, count - 1, turn, total)]
    select_n x126 -> x0, other arithmetic: 185 us -> none  [turn(): jnp.where(position < mine, new, old)]
    unnamed x1 -> x0, blocking collectives: 127 us -> none
    all_gather x2 -> x0, blocking collectives: 104 us -> none  [prefix(): pieces = jax.tree.map(lambda part: lax.all_gather(part, axis), value)]
    dynamic_slice x136 -> x0, local copies, waits for them, and re-layouts: 82.5 us -> none  [the longest x126 75.2 us: turn(): longer = join(total, jax.tree.map(lambda part: part[position], pieces))]
    pallas_call x0 -> x12, Pallas kernels: none -> 65.2 us  [the longest x8 17.5 us: small_call(): pl.pallas_call(body, in_specs=[pl.BlockSpec(memory_space=pltpu.SMEM)] + [...]
    psum x1 -> x0, waiting for transfers between devices: 56.7 us -> none  [per_device(): whole_b, whole_c = lax.psum((part_b, part_c), 'head')]
    dot_general x24 -> x0, matrix products: 54 us -> none  [the longest x20 46.2 us: product(): return jnp.einsum(pattern, first_op, second_op, precision=PRECISE)]
  transfers between devices with their start and end apart: 3 -> 26, of which waited for: 1 -> 4; matrix products, arithmetic and copies ran while one was open for 15% -> 1% of each run, Pallas kernels for 0% -> 42%
where the time goes in v1:
time: 132 us; the launch traced here: 131 us
  Pallas kernels  65.2 us (49%)
  starting transfers between devices  40.6 us (31%)
  waiting for transfers between devices  12.6 us (10%)
  local copies, waits for them, and re-layouts  10.4 us (8%)
  other arithmetic  1.68 us (1%)
    pallas_call x8, Pallas kernels, small_call(): pl.pallas_call(body, in_specs=[pl.BlockSpec(memory_space=pltpu.SMEM)] + [...  17.5 us
    ppermute x12, starting transfers between devices, along_y(): return lax.ppermute(v, Y, ring(4, shift))  15.7 us
    pallas_call x1, Pallas kernels, local_grads(): pl.pallas_call(local_kernel, grid=(G,), in_specs=[pl.BlockSpec((1, T), la...  13.5 us
    pallas_call x1, Pallas kernels, adjoint_grads(): pl.pallas_call(adjoint_kernel, grid_spec=grid, out_shape=[jax.ShapeDtypeS...  13.3 us
    ppermute x6, waiting for transfers between devices, along_x(): return lax.ppermute(v, X, ring(4, shift))  10.8 us
    pallas_call x1, Pallas kernels, state_grads(): pl.pallas_call(state_kernel, grid_spec=grid, out_shape=[jax.ShapeDtypeStr...  10.6 us
    unnamed x44, local copies, waits for them, and re-layouts  10.4 us
    pallas_call x1, Pallas kernels, summaries(): pl.pallas_call(summary_kernel, grid_spec=grid, out_shape=[big] * 4 + [thi...  10.3 us
  transfers between devices with their start and end apart: 26, of which 4 were waited for; matrix products, arithmetic and copies ran while one was open for 1% of the time, Pallas kernels for 42%

profile of v1, /device:TPU:1, one launch (start us, length us, event | category | flops | bytes accessed | tf_op | source)
XLA Modules:
  0.0 131.3 jit_solution(5615810028562872203)
XLA Ops:
  1.2 10.3 %summaries.1 = (bf16[8,256,256]{2,1,0:T(8,128)(2,1)}, bf16[8,256,256]{2,1,0:T(8,128)(2,1)}, bf16[8,256,256]{2,1,0:T(8,128)(2,1)}, bf16[8,256,256]{2,1,0:T(8,128)...) custom-call(s32[3]{0:T(128)} %pad_add_fusion.pos, ...), custom_call_target="tpu_custom_call" | custom-call | flops 8000000000 | bytes 10485760 | tf_op jit(solution)/shard_map/summaries/pallas_call | solution.py:186
  11.5 3.3 %collective-permute-start = (f32[4,136,256]{2,1,0:T(8,128)}, f32[4,136,256]{2,1,0:T(8,128)S(1)}, u32[]{:S(2)}, u32[]{:S(2)}) collective-permute-start(f32[4,136,256]{2,1,0:T(8,128)} %get-tuple-element.62), channel_id=1, source_target_pairs={{0,4},{4,0},{1,5},{5,1},{2,6},{6,2},{3,7},{7,3},{8,12},{12,8},{9,1... | collective-permute-start | bytes 1671176 | tf_op jit(solution)/shard_map/ppermute | solution.py:345
  14.9 1.7 %collective-permute-done.got.refs_5_ = f32[4,136,256]{2,1,0:T(8,128)S(1)} collective-permute-done((f32[4,136,256]{2,1,0:T(8,128)}, f32[4,136,256]{2,1,0:T(8,128)S(1)}, u32[]{:S(2)}, u32[]{:S(2)}) %collective-permute-start) | collective-permute-done | bytes 557088 | tf_op jit(solution)/shard_map/ppermute | solution.py:345
  17.4 2.1 %chip_join.2 = (f32[136,256]{1,0:T(8,128)}, f32[136,256]{1,0:T(8,128)}, f32[136,256]{1,0:T(8,128)}, f32[136,256]{1,0:T(8,128)}) custom-call(s32[3]{0:T(128)} %pad_add_fusion.pos, f32[4,136,256]{2,1,0:T(8,128)} %get-tuple-element.61.kept.refs_4_, f32[4,136,256]{2,1,0:T(8,128)} %copy-done.2), custom_call_target="tpu_custom_call" | custom-call | flops 1000000000 | bytes 2097152 | tf_op jit(solution)/shard_map/chip_join/pallas_call | solution.py:259
  19.6 2.2 %collective-permute-start.2 = (f32[136,256]{1,0:T(8,128)}, f32[136,256]{1,0:T(8,128)S(1)}, u32[]{:S(2)}, u32[]{:S(2)}) collective-permute-start(f32[136,256]{1,0:T(8,128)} %get-tuple-element.65), channel_id=1, source_target_pairs={{0,16},{8,24},{16,0},{24,8},{1,17},{9,25},{17,1},{25,9},{2,18},{10... | collective-permute-start | bytes 417800 | tf_op jit(solution)/shard_map/ppermute | solution.py:349
  23.6 2.1 %chip_join.3 = (f32[136,256]{1,0:T(8,128)}, f32[136,256]{1,0:T(8,128)}, f32[136,256]{1,0:T(8,128)}, f32[136,256]{1,0:T(8,128)}) custom-call(s32[3]{0:T(128)} %pad_add_fusion.pos, f32[4,136,256]{2,1,0:T(8,128)} %get-tuple-element.74.kept.refs_4_.rk_ref, f32[4,136,256]{2,1,0:T(8,128)} %copy-done.1), custom_call_target="tpu_custom_call" | custom-call | flops 1000000000 | bytes 2097152 | tf_op jit(solution)/shard_map/chip_join/pallas_call | solution.py:259
  27.5 2.1 %collective-permute-start.13 = (f32[136,256]{1,0:T(8,128)}, f32[136,256]{1,0:T(8,128)S(1)}, u32[]{:S(2)}, u32[]{:S(2)}) collective-permute-start(f32[136,256]{1,0:T(8,128)} %get-tuple-element.79), channel_id=1, source_target_pairs={{0,24},{8,0},{16,8},{24,16},{1,25},{9,1},{17,9},{25,17},{2,26},{10... | collective-permute-start | bytes 417800 | tf_op jit(solution)/shard_map/ppermute | solution.py:349
  30.3 1.9 %plane_join.2 = f32[136,256]{1,0:T(8,128)} custom-call(s32[3]{0:T(128)} %pad_add_fusion.pos, f32[136,256]{1,0:T(8,128)} %get-tuple-element.63.refs_0_, f32[136,256]{1,0:T(8,128)} %copy-done.7, f32[136,256]{1,0:T(8,128)} %copy-done.9, f32[136,256]{1,0:T(8,128)} %copy-done.10), custom_call_target="tpu_custom_call" | custom-call | flops 1000000000 | bytes 2097152 | tf_op jit(solution)/shard_map/plane_join/pallas_call | solution.py:259
  32.8 3.0 %collective-permute-start.5 = (f32[136,256]{1,0:T(8,128)}, f32[136,256]{1,0:T(8,128)S(1)}, u32[]{:S(2)}, u32[]{:S(2)}) collective-permute-start(f32[136,256]{1,0:T(8,128)} %plane_join.2), channel_id=1, source_target_pairs={{0,64},{32,96},{64,128},{96,160},{128,192},{160,224},{192,0},{224,... | collective-permute-start | bytes 417800 | tf_op jit(solution)/shard_map/ppermute | solution.py:353
  36.5 1.9 %plane_join.3 = f32[136,256]{1,0:T(8,128)} custom-call(s32[3]{0:T(128)} %pad_add_fusion.pos, f32[136,256]{1,0:T(8,128)} %get-tuple-element.76.refs_0_, f32[136,256]{1,0:T(8,128)} %copy-done.5, f32[136,256]{1,0:T(8,128)} %copy-done.6, f32[136,256]{1,0:T(8,128)} %copy-done.8), custom_call_target="tpu_custom_call" | custom-call | flops 1000000000 | bytes 2097152 | tf_op jit(solution)/shard_map/plane_join/pallas_call | solution.py:259
  38.4 4.4 %collective-permute-start.14 = (f32[136,256]{1,0:T(8,128)}, f32[136,256]{1,0:T(8,128)S(1)}, u32[]{:S(2)}, u32[]{:S(2)}) collective-permute-start(f32[136,256]{1,0:T(8,128)} %plane_join.3), channel_id=1, source_target_pairs={{0,224},{32,0},{64,32},{96,64},{128,96},{160,128},{192,160},{224,1... | collective-permute-start | bytes 417800 | tf_op jit(solution)/shard_map/ppermute | solution.py:353
  45.3 2.2 %plane_enter.2 = (f32[128,256]{1,0:T(8,128)}, f32[128,256]{1,0:T(8,128)}, f32[128,256]{1,0:T(8,128)}, f32[128,256]{1,0:T(8,128)}) custom-call(s32[3]{0:T(128)} %pad_add_fusion.pos, f32[136,256]{1,0:T(8,128)} %get-tuple-element.63.refs_0_, f32[136,256]{1,0:T(8,128)} %copy-done.7, f32[136,256]{1,0:T(8,128)} %copy-done.9, f32[136,256]{1,0:T(8,128)} %copy-done.10, ...), custom_call_target="tpu_custom_call" | custom-call | flops 1000000000 | bytes 2097152 | tf_op jit(solution)/shard_map/plane_enter/pallas_call | solution.py:259
  48.7 3.4 %collective-permute-start.7 = (f32[128,256]{1,0:T(8,128)}, f32[128,256]{1,0:T(8,128)S(1)}, u32[]{:S(2)}, u32[]{:S(2)}) collective-permute-start(f32[128,256]{1,0:T(8,128)} %get-tuple-element.69), channel_id=1, source_target_pairs={{0,16},{8,24},{16,0},{24,8},{1,17},{9,25},{17,1},{25,9},{2,18},{10... | collective-permute-start | bytes 393224 | tf_op jit(solution)/shard_map/ppermute | solution.py:349
  53.4 2.2 %plane_enter.3 = (f32[128,256]{1,0:T(8,128)}, f32[128,256]{1,0:T(8,128)}, f32[128,256]{1,0:T(8,128)}, f32[128,256]{1,0:T(8,128)}) custom-call(s32[3]{0:T(128)} %pad_add_fusion.pos, f32[136,256]{1,0:T(8,128)} %get-tuple-element.76.refs_0_, f32[136,256]{1,0:T(8,128)} %copy-done.5, f32[136,256]{1,0:T(8,128)} %copy-done.6, f32[136,256]{1,0:T(8,128)} %copy-done.8, ...), custom_call_target="tpu_custom_call" | custom-call | flops 1000000000 | bytes 2097152 | tf_op jit(solution)/shard_map/plane_enter/pallas_call | solution.py:259
  60.2 2.6 %device_enter.2 = (f32[4,128,256]{2,1,0:T(8,128)}, f32[4,128,256]{2,1,0:T(8,128)}) custom-call(s32[3]{0:T(128)} %pad_add_fusion.pos, f32[128,256]{1,0:T(8,128)} %get-tuple-element.67.refs_0_, f32[128,256]{1,0:T(8,128)} %copy-done.15, f32[128,256]{1,0:T(8,128)} %copy-done.16, f32[128,256]{1,0:T(8,128)} %copy-done.18, ...), custom_call_target="tpu_custom_call" | custom-call | flops 1000000000 | bytes 2097152 | tf_op jit(solution)/shard_map/device_enter/pallas_call | solution.py:259
  62.8 3.0 %collective-permute-start.9 = (f32[4,128,256]{2,1,0:T(8,128)}, f32[4,128,256]{2,1,0:T(8,128)S(1)}, u32[]{:S(2)}, u32[]{:S(2)}) collective-permute-start(f32[4,128,256]{2,1,0:T(8,128)} %get-tuple-element.72), channel_id=1, source_target_pairs={{0,4},{4,0},{1,5},{5,1},{2,6},{6,2},{3,7},{7,3},{8,12},{12,8},{9,1... | collective-permute-start | bytes 1572872 | tf_op jit(solution)/shard_map/ppermute | solution.py:345
  66.5 2.6 %device_enter.3 = (f32[4,128,256]{2,1,0:T(8,128)}, f32[4,128,256]{2,1,0:T(8,128)}) custom-call(s32[3]{0:T(128)} %pad_add_fusion.pos, f32[128,256]{1,0:T(8,128)} %get-tuple-element.80.refs_0_, f32[128,256]{1,0:T(8,128)} %copy-done.17, f32[128,256]{1,0:T(8,128)} %copy-done.19, f32[128,256]{1,0:T(8,128)} %copy-done.20, ...), custom_call_target="tpu_custom_call" | custom-call | flops 1000000000 | bytes 2097152 | tf_op jit(solution)/shard_map/device_enter/pallas_call | solution.py:259
  69.1 1.7 %collective-permute-start.19 = (f32[4,128,256]{2,1,0:T(8,128)}, f32[4,128,256]{2,1,0:T(8,128)S(1)}, u32[]{:S(2)}, u32[]{:S(2)}) collective-permute-start(f32[4,128,256]{2,1,0:T(8,128)} %get-tuple-element.85), channel_id=1, source_target_pairs={{0,4},{4,0},{1,5},{5,1},{2,6},{6,2},{3,7},{7,3},{8,12},{12,8},{9,1... | collective-permute-start | bytes 1572872 | tf_op jit(solution)/shard_map/ppermute | solution.py:345
  70.8 13.5 %local_grads.1 = (f32[8,256,128]{2,1,0:T(8,128)}, f32[8,256,128]{2,1,0:T(8,128)}, f32[8,256,256]{2,1,0:T(8,128)}, f32[8,8,256]{2,1,0:T(8,128)}) custom-call(s32[1,256]{1,0:T(1,128)} %bitcast.16, bf16[8,256,256]{2,1,0:T(8,128)(2,1)} %get-tuple-element.51.xh_ref, bf16[8,256,256]{2,1,0:T(8,128)(2,1)} %get-tuple-element.52.xl_ref, ...), custom_call_target="tpu_custom_call" | custom-call | flops 10000000000 | bytes 12582912 | tf_op jit(solution)/shard_map/local_grads/pallas_call | solution.py:225
  85.1 10.6 %state_grads.1 = (f32[2,256,128]{2,1,0:T(8,128)}, f32[2,256,128]{2,1,0:T(8,128)}, f32[2,256,128]{2,1,0:T(8,128)}, f32[2,256,128]{2,1,0:T(8,128)}, f32[8,8,256]{2,1,0:T(8,128)}) custom-call(s32[3]{0:T(128)} %pad_add_fusion.pos, s32[1,256]{1,0:T(1,128)} %bitcast.17, bf16[8,256,256]{2,1,0:T(8,128)(2,1)} %get-tuple-element.54.dh_ref, ...), custom_call_target="tpu_custom_call" | custom-call | flops 4000000000 | bytes 6291456 | tf_op jit(solution)/shard_map/state_grads/pallas_call | solution.py:430
  96.9 2.5 %collective-permute-start.24 = (f32[2,256,128]{2,1,0:T(8,128)}, f32[2,256,128]{2,1,0:T(8,128)S(1)}, u32[]{:S(2)}, u32[]{:S(2)}) collective-permute-start(f32[2,256,128]{2,1,0:T(8,128)} %get-tuple-element.94), channel_id=1, source_target_pairs={{0,2},{1,3},{2,0},{3,1},{4,6},{5,7},{6,4},{7,5},{8,10},{9,11},{10,... | collective-permute-start | bytes 786440 | tf_op jit(solution)/shard_map/ppermute | solution.py:357
  101.4 13.3 %adjoint_grads.1 = (f32[2,256,128]{2,1,0:T(8,128)}, f32[2,256,128]{2,1,0:T(8,128)}, f32[2,256,128]{2,1,0:T(8,128)}, f32[2,256,128]{2,1,0:T(8,128)}, bf16[256,8,256]{2,1,0:T(8,128)(2,1)}, /*index=5*/f32[8,4,256]{2,1,0:T(4,128)}) custom-call(s32[3]{0:T(128)} %pad_add_fusion.pos, s32[1,256]{1,0:T(1,128)} %bitcast.18, f32[8,4,256]{2,1,0:T(4,128)} %bitcast.12, ...), custom_call_target="tpu_custom_call" | custom-call | flops 6000000000 | bytes 9437184 | tf_op jit(solution)/shard_map/adjoint_grads/pallas_call | solution.py:522
  116.0 1.6 %collective-permute-start.22 = (f32[2,256,128]{2,1,0:T(8,128)}, f32[2,256,128]{2,1,0:T(8,128)S(1)}, u32[]{:S(2)}, u32[]{:S(2)}) collective-permute-start(f32[2,256,128]{2,1,0:T(8,128)} %get-tuple-element.91), channel_id=1, source_target_pairs={{0,3},{1,0},{2,1},{3,2},{4,7},{5,4},{6,5},{7,6},{8,11},{9,8},{10,9... | collective-permute-start | bytes 786440 | tf_op jit(solution)/shard_map/ppermute | solution.py:357
  118.6 10.2 %collective-permute-done.20 = f32[2,256,128]{2,1,0:T(8,128)S(1)} collective-permute-done((f32[2,256,128]{2,1,0:T(8,128)}, f32[2,256,128]{2,1,0:T(8,128)S(1)}, u32[]{:S(2)}, u32[]{:S(2)}) %collective-permute-start.20) | collective-permute-done | bytes 262176 | tf_op jit(solution)/shard_map/ppermute | solution.py:357
  (87 shorter events, 26.2 us)
Async XLA Ops:
  14.8 8.0 %collective-permute-start.10 = (f32[4,136,256]{2,1,0:T(8,128)}, f32[4,136,256]{2,1,0:T(8,128)S(1)}, u32[]{:S(2)}, u32[]{:S(2)}) collective-permute-start(f32[4,136,256]{2,1,0:T(8,128)} %get-tuple-element.75.rs_ref), channel_id=1, source_target_pairs={{0,4},{4,0},{1,5},{5,1},{2,6},{6,2},{3,7},{7,3},{8,12},{12,8},{9,1... | collective-permute-start | bytes 1671176 | tf_op jit(solution)/shard_map/ppermute | solution.py:345
  19.6 8.0 %collective-permute-start.1 = (f32[136,256]{1,0:T(8,128)}, f32[136,256]{1,0:T(8,128)S(1)}, u32[]{:S(2)}, u32[]{:S(2)}) collective-permute-start(f32[136,256]{1,0:T(8,128)} %get-tuple-element.64), channel_id=1, source_target_pairs={{0,8},{8,16},{16,24},{24,0},{1,9},{9,17},{17,25},{25,1},{2,10},{10... | collective-permute-start | bytes 417800 | tf_op jit(solution)/shard_map/ppermute | solution.py:349
  19.6 10.1 %collective-permute-start.2 = (f32[136,256]{1,0:T(8,128)}, f32[136,256]{1,0:T(8,128)S(1)}, u32[]{:S(2)}, u32[]{:S(2)}) collective-permute-start(f32[136,256]{1,0:T(8,128)} %get-tuple-element.65), channel_id=1, source_target_pairs={{0,16},{8,24},{16,0},{24,8},{1,17},{9,25},{17,1},{25,9},{2,18},{10... | collective-permute-start | bytes 417800 | tf_op jit(solution)/shard_map/ppermute | solution.py:349
  21.7 7.9 %collective-permute-start.3 = (f32[136,256]{1,0:T(8,128)}, f32[136,256]{1,0:T(8,128)S(1)}, u32[]{:S(2)}, u32[]{:S(2)}) collective-permute-start(f32[136,256]{1,0:T(8,128)} %get-tuple-element.66), channel_id=1, source_target_pairs={{0,24},{8,0},{16,8},{24,16},{1,25},{9,1},{17,9},{25,17},{2,26},{10... | collective-permute-start | bytes 417800 | tf_op jit(solution)/shard_map/ppermute | solution.py:349
  25.7 10.0 %collective-permute-start.11 = (f32[136,256]{1,0:T(8,128)}, f32[136,256]{1,0:T(8,128)S(1)}, u32[]{:S(2)}, u32[]{:S(2)}) collective-permute-start(f32[136,256]{1,0:T(8,128)} %get-tuple-element.77), channel_id=1, source_target_pairs={{0,8},{8,16},{16,24},{24,0},{1,9},{9,17},{17,25},{25,1},{2,10},{10... | collective-permute-start | bytes 417800 | tf_op jit(solution)/shard_map/ppermute | solution.py:349
  26.1 9.6 %collective-permute-start.12 = (f32[136,256]{1,0:T(8,128)}, f32[136,256]{1,0:T(8,128)S(1)}, u32[]{:S(2)}, u32[]{:S(2)}) collective-permute-start(f32[136,256]{1,0:T(8,128)} %get-tuple-element.78), channel_id=1, source_target_pairs={{0,16},{8,24},{16,0},{24,8},{1,17},{9,25},{17,1},{25,9},{2,18},{10... | collective-permute-start | bytes 417800 | tf_op jit(solution)/shard_map/ppermute | solution.py:349
  27.5 8.2 %collective-permute-start.13 = (f32[136,256]{1,0:T(8,128)}, f32[136,256]{1,0:T(8,128)S(1)}, u32[]{:S(2)}, u32[]{:S(2)}) collective-permute-start(f32[136,256]{1,0:T(8,128)} %get-tuple-element.79), channel_id=1, source_target_pairs={{0,24},{8,0},{16,8},{24,16},{1,25},{9,1},{17,9},{25,17},{2,26},{10... | collective-permute-start | bytes 417800 | tf_op jit(solution)/shard_map/ppermute | solution.py:349
  32.2 11.7 %collective-permute-start.4 = (f32[136,256]{1,0:T(8,128)}, f32[136,256]{1,0:T(8,128)S(1)}, u32[]{:S(2)}, u32[]{:S(2)}) collective-permute-start(f32[136,256]{1,0:T(8,128)} %plane_join.2), channel_id=1, source_target_pairs={{0,32},{32,64},{64,96},{96,128},{128,160},{160,192},{192,224},{224... | collective-permute-start | bytes 417800 | tf_op jit(solution)/shard_map/ppermute | solution.py:353
  32.8 11.2 %collective-permute-start.5 = (f32[136,256]{1,0:T(8,128)}, f32[136,256]{1,0:T(8,128)S(1)}, u32[]{:S(2)}, u32[]{:S(2)}) collective-permute-start(f32[136,256]{1,0:T(8,128)} %plane_join.2), channel_id=1, source_target_pairs={{0,64},{32,96},{64,128},{96,160},{128,192},{160,224},{192,0},{224,... | collective-permute-start | bytes 417800 | tf_op jit(solution)/shard_map/ppermute | solution.py:353
  38.4 13.7 %collective-permute-start.14 = (f32[136,256]{1,0:T(8,128)}, f32[136,256]{1,0:T(8,128)S(1)}, u32[]{:S(2)}, u32[]{:S(2)}) collective-permute-start(f32[136,256]{1,0:T(8,128)} %plane_join.3), channel_id=1, source_target_pairs={{0,224},{32,0},{64,32},{96,64},{128,96},{160,128},{192,160},{224,1... | collective-permute-start | bytes 417800 | tf_op jit(solution)/shard_map/ppermute | solution.py:353
  42.7 9.3 %collective-permute-start.15 = (f32[136,256]{1,0:T(8,128)}, f32[136,256]{1,0:T(8,128)S(1)}, u32[]{:S(2)}, u32[]{:S(2)}) collective-permute-start(f32[136,256]{1,0:T(8,128)} %plane_join.3), channel_id=1, source_target_pairs={{0,192},{32,224},{64,0},{96,32},{128,64},{160,96},{192,128},{224,1... | collective-permute-start | bytes 417800 | tf_op jit(solution)/shard_map/ppermute | solution.py:353
  47.4 11.2 %collective-permute-start.6 = (f32[128,256]{1,0:T(8,128)}, f32[128,256]{1,0:T(8,128)S(1)}, u32[]{:S(2)}, u32[]{:S(2)}) collective-permute-start(f32[128,256]{1,0:T(8,128)} %get-tuple-element.68), channel_id=1, source_target_pairs={{0,8},{8,16},{16,24},{24,0},{1,9},{9,17},{17,25},{25,1},{2,10},{10... | collective-permute-start | bytes 393224 | tf_op jit(solution)/shard_map/ppermute | solution.py:349
  48.7 10.9 %collective-permute-start.7 = (f32[128,256]{1,0:T(8,128)}, f32[128,256]{1,0:T(8,128)S(1)}, u32[]{:S(2)}, u32[]{:S(2)}) collective-permute-start(f32[128,256]{1,0:T(8,128)} %get-tuple-element.69), channel_id=1, source_target_pairs={{0,16},{8,24},{16,0},{24,8},{1,17},{9,25},{17,1},{25,9},{2,18},{10... | collective-permute-start | bytes 393224 | tf_op jit(solution)/shard_map/ppermute | solution.py:349
  52.1 7.4 %collective-permute-start.8 = (f32[128,256]{1,0:T(8,128)}, f32[128,256]{1,0:T(8,128)S(1)}, u32[]{:S(2)}, u32[]{:S(2)}) collective-permute-start(f32[128,256]{1,0:T(8,128)} %get-tuple-element.70), channel_id=1, source_target_pairs={{0,24},{8,0},{16,8},{24,16},{1,25},{9,1},{17,9},{25,17},{2,26},{10... | collective-permute-start | bytes 393224 | tf_op jit(solution)/shard_map/ppermute | solution.py:349
  55.6 10.2 %collective-permute-start.16 = (f32[128,256]{1,0:T(8,128)}, f32[128,256]{1,0:T(8,128)S(1)}, u32[]{:S(2)}, u32[]{:S(2)}) collective-permute-start(f32[128,256]{1,0:T(8,128)} %get-tuple-element.81), channel_id=1, source_target_pairs={{0,8},{8,16},{16,24},{24,0},{1,9},{9,17},{17,25},{25,1},{2,10},{10... | collective-permute-start | bytes 393224 | tf_op jit(solution)/shard_map/ppermute | solution.py:349
  57.1 8.7 %collective-permute-start.17 = (f32[128,256]{1,0:T(8,128)}, f32[128,256]{1,0:T(8,128)S(1)}, u32[]{:S(2)}, u32[]{:S(2)}) collective-permute-start(f32[128,256]{1,0:T(8,128)} %get-tuple-element.82), channel_id=1, source_target_pairs={{0,16},{8,24},{16,0},{24,8},{1,17},{9,25},{17,1},{25,9},{2,18},{10... | collective-permute-start | bytes 393224 | tf_op jit(solution)/shard_map/ppermute | solution.py:349
  62.8 21.6 %collective-permute-start.9 = (f32[4,128,256]{2,1,0:T(8,128)}, f32[4,128,256]{2,1,0:T(8,128)S(1)}, u32[]{:S(2)}, u32[]{:S(2)}) collective-permute-start(f32[4,128,256]{2,1,0:T(8,128)} %get-tuple-element.72), channel_id=1, source_target_pairs={{0,4},{4,0},{1,5},{5,1},{2,6},{6,2},{3,7},{7,3},{8,12},{12,8},{9,1... | collective-permute-start | bytes 1572872 | tf_op jit(solution)/shard_map/ppermute | solution.py:345
  69.1 31.5 %collective-permute-start.19 = (f32[4,128,256]{2,1,0:T(8,128)}, f32[4,128,256]{2,1,0:T(8,128)S(1)}, u32[]{:S(2)}, u32[]{:S(2)}) collective-permute-start(f32[4,128,256]{2,1,0:T(8,128)} %get-tuple-element.85), channel_id=1, source_target_pairs={{0,4},{4,0},{1,5},{5,1},{2,6},{6,2},{3,7},{7,3},{8,12},{12,8},{9,1... | collective-permute-start | bytes 1572872 | tf_op jit(solution)/shard_map/ppermute | solution.py:345
  95.7 20.2 %collective-permute-start.23 = (f32[2,256,128]{2,1,0:T(8,128)}, f32[2,256,128]{2,1,0:T(8,128)S(1)}, u32[]{:S(2)}, u32[]{:S(2)}) collective-permute-start(f32[2,256,128]{2,1,0:T(8,128)} %get-tuple-element.93), channel_id=1, source_target_pairs={{0,1},{1,2},{2,3},{3,0},{4,5},{5,6},{6,7},{7,4},{8,9},{9,10},{10,1... | collective-permute-start | bytes 786440 | tf_op jit(solution)/shard_map/ppermute | solution.py:357
  96.9 20.7 %collective-permute-start.24 = (f32[2,256,128]{2,1,0:T(8,128)}, f32[2,256,128]{2,1,0:T(8,128)S(1)}, u32[]{:S(2)}, u32[]{:S(2)}) collective-permute-start(f32[2,256,128]{2,1,0:T(8,128)} %get-tuple-element.94), channel_id=1, source_target_pairs={{0,2},{1,3},{2,0},{3,1},{4,6},{5,7},{6,4},{7,5},{8,10},{9,11},{10,... | collective-permute-start | bytes 786440 | tf_op jit(solution)/shard_map/ppermute | solution.py:357
  99.5 18.1 %collective-permute-start.25 = (f32[2,256,128]{2,1,0:T(8,128)}, f32[2,256,128]{2,1,0:T(8,128)S(1)}, u32[]{:S(2)}, u32[]{:S(2)}) collective-permute-start(f32[2,256,128]{2,1,0:T(8,128)} %get-tuple-element.95), channel_id=1, source_target_pairs={{0,3},{1,0},{2,1},{3,2},{4,7},{5,4},{6,5},{7,6},{8,11},{9,8},{10,9... | collective-permute-start | bytes 786440 | tf_op jit(solution)/shard_map/ppermute | solution.py:357
  114.7 14.1 %collective-permute-start.20 = (f32[2,256,128]{2,1,0:T(8,128)}, f32[2,256,128]{2,1,0:T(8,128)S(1)}, u32[]{:S(2)}, u32[]{:S(2)}) collective-permute-start(f32[2,256,128]{2,1,0:T(8,128)} %get-tuple-element.89), channel_id=1, source_target_pairs={{0,1},{1,2},{2,3},{3,0},{4,5},{5,6},{6,7},{7,4},{8,9},{9,10},{10,1... | collective-permute-start | bytes 786440 | tf_op jit(solution)/shard_map/ppermute | solution.py:357
  115.1 13.7 %collective-permute-start.21 = (f32[2,256,128]{2,1,0:T(8,128)}, f32[2,256,128]{2,1,0:T(8,128)S(1)}, u32[]{:S(2)}, u32[]{:S(2)}) collective-permute-start(f32[2,256,128]{2,1,0:T(8,128)} %get-tuple-element.90), channel_id=1, source_target_pairs={{0,2},{1,3},{2,0},{3,1},{4,6},{5,7},{6,4},{7,5},{8,10},{9,11},{10,... | collective-permute-start | bytes 786440 | tf_op jit(solution)/shard_map/ppermute | solution.py:357
  116.0 13.4 %collective-permute-start.22 = (f32[2,256,128]{2,1,0:T(8,128)}, f32[2,256,128]{2,1,0:T(8,128)S(1)}, u32[]{:S(2)}, u32[]{:S(2)}) collective-permute-start(f32[2,256,128]{2,1,0:T(8,128)} %get-tuple-element.91), channel_id=1, source_target_pairs={{0,3},{1,0},{2,1},{3,2},{4,7},{5,4},{6,5},{7,6},{8,11},{9,8},{10,9... | collective-permute-start | bytes 786440 | tf_op jit(solution)/shard_map/ppermute | solution.py:357
  (23 other events, 44.0 us)

commit v2 on v0

v2 whole, which is shorter than its diff:
```python
import functools

import jax
import jax.numpy as jnp
from jax import lax
from jax.experimental import pallas as pl
from jax.experimental.pallas import tpu as pltpu
from jax.sharding import Mesh, PartitionSpec as P

F32 = jnp.float32
BF16 = jnp.bfloat16
T = 256
G = 8
J = 4
W = 256
N = 128
ROWS = N + 8
DEC, FIRST, LAST, ELAST = N, N + 1, N + 2, N + 3
HBM = pl.BlockSpec(memory_space=pltpu.HBM)
VMEM = pl.BlockSpec(memory_space=pltpu.VMEM)
SMEM = pl.BlockSpec(memory_space=pltpu.SMEM)
Z, Y, C, X = "z", "y", "core", "head"


def dot(a, b):
    return lax.dot_general(a, b, (((1,), (0,)), ((), ())), preferred_element_type=F32)


def dot_t(a, b):
    return lax.dot_general(a, b, (((1,), (1,)), ((), ())), preferred_element_type=F32)


def split2(v):
    hi = v.astype(BF16)
    return hi, (v - hi.astype(F32)).astype(BF16)


def split3(v):
    hi = v.astype(BF16)
    rest = v - hi.astype(F32)
    mid = rest.astype(BF16)
    return hi, mid, (rest - mid.astype(F32)).astype(BF16)


def iota(shape, dim):
    return lax.broadcasted_iota(jnp.int32, shape, dim)


def head_ones():
    return (iota((8, W), 0) == iota((8, W), 1) // 64).astype(BF16)


def expander(g):
    k = iota((128, W), 0)
    return ((k < 96) & (k % 32 == J * g + iota((128, W), 1) // 64)).astype(BF16)


def head_sums(ones, z):
    hi, lo = split2(z)
    return dot_t(ones, hi) + dot_t(ones, lo)


def token_rows(seg_row):
    padded = jnp.concatenate([seg_row, jnp.zeros((7, T), F32)], axis=0).astype(BF16)
    ones = jnp.ones((8, T), BF16)
    return lax.dot_general(padded, ones, (((0,), (0,)), ((), ())), preferred_element_type=F32)


def lows(seg_t, seg_row):
    return (seg_t == seg_row) & (iota((T, T), 1) <= iota((T, T), 0))


def highs(seg_t, seg_row):
    return (seg_t == seg_row) & (iota((T, T), 1) >= iota((T, T), 0))


def firsts(seg_t):
    return seg_t[:, :N] == seg_t[0:1, :N]


def lasts(seg_t):
    return seg_t[:, :N] == seg_t[T - 1 : T, :N]


def place():
    return lax.axis_index(C), lax.axis_index(Y), lax.axis_index(X)


def copy(source, target, sem):
    return pltpu.make_async_copy(source, target, sem)


def start(*copies):
    for one in copies:
        one.start()


def wait(*copies):
    for one in copies:
        one.wait()


def sds(*shape, dtype=F32):
    return jax.ShapeDtypeStruct(shape, dtype)


def call(kernel, args, specs, outs, scratch, name, mega, mib, out_spec=HBM, **more):
    return pl.pallas_call(
        kernel,
        in_specs=specs,
        out_specs=[out_spec] * len(outs),
        out_shape=outs,
        scratch_shapes=scratch,
        compiler_params=pltpu.CompilerParams(vmem_limit_bytes=mib * 2**20),
        cost_estimate=pl.CostEstimate(flops=mega * 10**3, bytes_accessed=2**10, transcendentals=0),
        name=name,
        **more,
    )(*args)


def columns(v):
    pieces = [piece.astype(F32) for piece in split3(v)] + [jnp.zeros((32, T), F32)]
    return jnp.transpose(jnp.concatenate(pieces, axis=0)).astype(BF16)


def summary_kernel(
    rate_hbm, dt_hbm, seg_hbm, x_hbm, dy_hbm, b_hbm, c_hbm,
    xh_hbm, xl_hbm, dh_hbm, dl_hbm, bt_hbm, ct_hbm, qt_hbm, fs_hbm, fk_hbm, rs_hbm, rk_hbm,
    rate, dt_v, seg_v, x_v, dy_v, b_v, c_v, bt_s, ct_s, xh_s, xl_s, dh_s, dl_s, f_s, r_s,
    a_s, dt_s, et_s, qt_s, in_sem, bc_sem, xd_sem, st_sem,
):
    core, y, _ = place()
    loads = [
        copy(source, target, in_sem.at[k])
        for k, (source, target) in enumerate(
            [
                (rate_hbm, rate), (dt_hbm, dt_v), (seg_hbm, seg_v),
                (b_hbm, b_v), (x_hbm, x_v), (c_hbm, c_v), (dy_hbm, dy_v),
            ]
        )
    ]
    start(*loads)
    wait(*loads[:3])
    for j in range(J):
        for k in range(G):
            row = slice(J * k + j, J * k + j + 1)
            dt_s[row, :] = dt_v[k, j : j + 1, :]
            a_s[row, :] = dt_v[k, j : j + 1, :] * rate[j, k]
    upto = (iota((T, T), 0) <= iota((T, T), 1)).astype(BF16)
    cum3 = dot(jnp.concatenate(split3(a_s[...]), axis=0), upto)
    cum = cum3[:32] + cum3[32:64] + cum3[64:96]
    et_s[...] = columns(jnp.exp(cum))
    qt_s[...] = columns(jnp.exp(-cum) * dt_s[...])
    seg_t = token_rows(seg_v[...].astype(F32))
    first_mask, last_mask = firsts(seg_t).astype(BF16), lasts(seg_t).astype(BF16)
    first, last = seg_t[0:1, :], seg_t[T - 1 : T, :]
    whole = (first == last).astype(F32)
    outs = [copy(qt_s, qt_hbm, bc_sem.at[2])]

    def order(i):
        return 4 * (1 - core if i < 4 else core) + lax.rem(y + i % 4, 4)

    def side(load_w, load_v, w_v, v_v, wt_s, wt_hbm, k, col, mask, hi_s, lo_s, hi_hbm, lo_hbm, out_s, sent, kept):
        load_w.wait()
        wt_s[...] = jnp.swapaxes(w_v[...], 0, 1)
        outs.append(copy(wt_s, wt_hbm, bc_sem.at[k]))
        outs[-1].start()
        load_v.wait()
        hi_s[...] = jnp.swapaxes(v_v[...], 0, 1)
        for i in range(G):
            g = order(i)
            spread = expander(g)
            scale = dot(col[...], spread)
            e_last = dot(et_s[T - 16 :, :], spread)[15:16]
            hi, lo = split2(hi_s[g].astype(F32) * scale)
            hi_s[g], lo_s[g] = hi, lo
            w = jnp.transpose(wt_s[g] * mask)
            block = dot(w, hi) + dot(w, lo)
            out_s[i, :N, :] = block if k else block * e_last
            out_s[i, N:, :] = jnp.concatenate(
                [e_last * whole, first, last, e_last, jnp.zeros((4, W), F32)], axis=0
            )
            started = copy(out_s.at[i], (sent if i < 4 else kept).at[i % 4], st_sem.at[8 * k + i])
            started.start()
            outs.append(started)
        outs.append(copy(hi_s, hi_hbm, xd_sem.at[2 * k]))
        outs.append(copy(lo_s, lo_hbm, xd_sem.at[2 * k + 1]))
        start(*outs[-2:])

    outs[0].start()
    side(
        loads[3], loads[4], b_v, x_v, bt_s, bt_hbm, 0, qt_s, last_mask,
        xh_s, xl_s, xh_hbm, xl_hbm, f_s, fs_hbm, fk_hbm,
    )
    side(
        loads[5], loads[6], c_v, dy_v, ct_s, ct_hbm, 1, et_s, first_mask,
        dh_s, dl_s, dh_hbm, dl_hbm, r_s, rs_hbm, rk_hbm,
    )
    wait(*outs)


def summaries(dt, rate, seg, x, dy, b, c):
    big, thin, block = sds(G, T, W, dtype=BF16), sds(G, T, N, dtype=BF16), sds(4, ROWS, W)
    tall = pltpu.VMEM((G, T, W), BF16)
    return call(
        summary_kernel,
        (rate, dt, seg, x, dy, b, c),
        [HBM] * 7,
        [big] * 4 + [thin] * 2 + [sds(T, N, dtype=BF16)] + [block] * 4,
        [
            pltpu.SMEM((J, G), F32), pltpu.VMEM((G, J, T), F32), pltpu.VMEM((1, T), jnp.int32),
            pltpu.VMEM((T, G, W), BF16), pltpu.VMEM((T, G, W), BF16),
            pltpu.VMEM((T, G, N), BF16), pltpu.VMEM((T, G, N), BF16),
            pltpu.VMEM((G, T, N), BF16), pltpu.VMEM((G, T, N), BF16),
            tall, tall, tall, tall,
            pltpu.VMEM((G, ROWS, W), F32), pltpu.VMEM((G, ROWS, W), F32),
            pltpu.VMEM((32, T), F32), pltpu.VMEM((32, T), F32),
            pltpu.VMEM((T, N), BF16), pltpu.VMEM((T, N), BF16),
            pltpu.SemaphoreType.DMA((7,)), pltpu.SemaphoreType.DMA((3,)),
            pltpu.SemaphoreType.DMA((4,)), pltpu.SemaphoreType.DMA((16,)),
        ],
        "summaries",
        8000,
        60,
    )


def local_kernel(g0, count, seg_ref, *refs):
    ins, outs = refs[:6], refs[-4:]
    seg_row = seg_ref[...].astype(F32)
    seg_t = token_rows(seg_row)
    low, high = lows(seg_t, seg_row).astype(F32), highs(seg_t, seg_row).astype(F32)
    ones = head_ones()
    for i in range(count):
        xh, xl, dh, dl, b, c = [ref[g0 + i] for ref in ins]
        sums = dot_t(dh, xh) + dot_t(dh, xl) + dot_t(dl, xh)
        sh, sl = split2(sums * low)
        outs[0][i] = dot(sh, b) + dot(sl, b)
        c_tr = jnp.transpose(c)
        outs[1][i] = jnp.transpose(dot(c_tr, sh) + dot(c_tr, sl))
        wh, wl = split2(dot_t(c, b) * low)
        out = dot(wh, xh) + dot(wh, xl) + dot(wl, xh)
        outs[3][i] = head_sums(ones, out * (dh.astype(F32) + dl.astype(F32)))
        vh, vl = split2(dot_t(b, c) * high)
        outs[2][i] = dot(vh, dh) + dot(vh, dl) + dot(vl, dh)


def local_grads(g0, count, seg, data, after):
    return call(
        functools.partial(local_kernel, g0, count),
        (seg, *data, *after),
        [VMEM] * 7 + [HBM] * len(after),
        [sds(count, T, N), sds(count, T, N), sds(count, T, W), sds(count, 8, T)],
        [],
        "local_grads",
        3000,
        12,
        VMEM,
    )


def piece(parts, g):
    for part in parts:
        if g < part.shape[0]:
            return part.at[g]
        g -= part.shape[0]


def linked(earlier, later):
    return (earlier[LAST : LAST + 1, :] == later[FIRST : FIRST + 1, :]).astype(F32)


def join(earlier, later, out, rev):
    link = linked(earlier, later)
    near, far = (earlier, later) if rev else (later, earlier)
    out[:N, :] = near[:N, :] + (near[DEC : DEC + 1, :] * link) * far[:N, :]
    both = earlier[DEC : DEC + 1, :] * later[DEC : DEC + 1, :] * link
    out[N:, :] = jnp.concatenate(
        [both, earlier[FIRST : FIRST + 1, :], later[LAST : LAST + 1, :], jnp.zeros((5, W), F32)], axis=0
    )


def load_all(pairs, sems):
    loads = [copy(source, target, sems.at[k]) for k, (source, target) in enumerate(pairs)]
    start(*loads)
    return loads


def block(*lead):
    return pltpu.VMEM((*lead, ROWS, W), F32)


def sems(count):
    return pltpu.SemaphoreType.DMA((count,))


def small_call(body, args, after, outs, scratch, name):
    def kernel(*refs):
        body(*refs[: len(args)], *refs[len(args) + len(after) :])

    specs = [VMEM] * len(args) + [HBM] * len(after)
    return call(kernel, (*args, *after), specs, outs, scratch, name, 1000, 8, VMEM)


def chip_join(kept, got, rev, after=()):
    def body(kept, got, *outs):
        def go(earlier, later):
            for s in range(4):
                join(earlier.at[s], later.at[s], outs[s], rev)

        pl.when(place()[0] == 0)(lambda: go(kept, got))
        pl.when(place()[0] == 1)(lambda: go(got, kept))

    return small_call(body, (kept, got), after, [sds(ROWS, W)] * 4, [], "chip_join")


def by_y(blocks, go):
    y = place()[1]
    for k in range(4):
        pl.when(y == k)(lambda k=k: go([blocks[(k - there) % 4] for there in range(4)], k))


def plane_join(blocks, rev, after=()):
    def body(*refs):
        blocks, out, one, two = refs[:4], refs[4], refs[5], refs[6]

        def go(order, _):
            join(order[0], order[1], one, rev)
            join(order[2], order[3], two, rev)
            join(one, two, out, rev)

        by_y(blocks, go)

    return small_call(body, blocks, after, [sds(ROWS, W)], [block(), block()], "plane_join")[0]


def plane_enter(blocks, near, far, rev, after=()):
    def body(*refs):
        blocks, near, far, outs = refs[:4], refs[4], refs[5], refs[6:]

        def link(one, two):
            return linked(two, one) if rev else linked(one, two)

        def go(order, y):
            first, ahead = (3, -1) if rev else (0, 1)
            carry = near[:N, :] + (near[DEC : DEC + 1, :] * link(far, near)) * far[:N, :]
            carry = link(near, order[first]) * carry
            for step in range(4):
                here = first + step * ahead
                outs[(here - y) % 4][...] = carry
                if step < 3:
                    one = order[here]
                    carry = link(one, order[here + ahead]) * (one[:N, :] + one[DEC : DEC + 1, :] * carry)

        by_y(blocks, go)

    return small_call(body, (*blocks, near, far), after, [sds(N, W)] * 4, [], "plane_enter")


def device_enter(entering, kept, got, rev, after=()):
    inner = 1 if rev else 0

    def body(*refs):
        entering, kept, got, mine, other = refs[:4], refs[4], refs[5], refs[6], refs[7]
        core, y, _ = place()

        def go(near, far, direct, passed):
            for s in range(4):
                k, slot = lax.rem(y + 4 - s, 4), (4 - s) % 4
                one, two = near.at[slot], far.at[slot]
                link = linked(two, one) if rev else linked(one, two)
                direct[k] = entering[s][...]
                passed[k] = link * (one[:N, :] + one[DEC : DEC + 1, :] * entering[s][...])

        pl.when(core == inner)(lambda: go(kept, got, mine, other))
        pl.when(core != inner)(lambda: go(got, kept, other, mine))

    args = (*entering, kept, got)
    return small_call(body, args, after, [sds(4, N, W)] * 2, [], "device_enter")


def ring(count, shift):
    return [(i, (i + shift) % count) for i in range(count)]


def swap(v):
    return lax.ppermute(v, C, ring(2, 1))


def along_y(v, shift):
    return lax.ppermute(v, Y, ring(4, shift))


def along_z(v, shift):
    return lax.ppermute(v, Z, ring(8, shift))


def along_x(v, shift):
    return lax.ppermute(v, X, ring(4, shift))


def of_half(core, g, mine, got):
    return jnp.where(core == g // 4, mine[g % 4], got[g % 4])


def reverse_block(core, y, g, kept, sent, rows):
    slot = lax.rem(g % 4 + 4 - y, 4)
    return jnp.where(core == g // 4, kept[slot, rows, :], sent[slot, rows, :])


def sum_kernel(rev, n_parts, seg_ref, hi_ref, lo_ref, mine, got, *refs):
    if rev:
        kept, sent, refs = refs[0], refs[1], refs[2:]
    parts, outs = refs[:n_parts], refs[-4:]
    core, y, x = place()
    seg_t = token_rows(seg_ref[...].astype(F32))
    mask = (lasts(seg_t) if rev else firsts(seg_t)).astype(F32)
    for g in range(G):
        state = of_half(core, g, mine, got)
        if rev:
            state = state * reverse_block(core, y, g, kept, sent, slice(N, ROWS))[ELAST - N : ELAST - N + 1]
        sh, sl = split2(state)
        hi, lo = hi_ref[g], lo_ref[g]
        whole = piece(parts, g)[...] + mask * (dot_t(hi, sh) + dot_t(hi, sl) + dot_t(lo, sh))
        shift = lax.rem(g // 2 + 4 - x, 4)
        for s in range(4):

            @pl.when(shift == s)
            def _(s=s, whole=whole):
                outs[s][g % 2] = whole


def summed(rev, seg, hi, lo, mine, got, more, parts, after):
    args = (seg, hi, lo, mine, got, *more, *parts, *after)
    return call(
        functools.partial(sum_kernel, rev, len(parts)),
        args,
        [VMEM] * (len(args) - len(after)) + [HBM] * len(after),
        [sds(2, T, N)] * 4,
        [],
        "summed",
        3000,
        12,
        VMEM,
    )


def token_kernel(
    n_parts, rate, seg_ref, dt_ref, qt_ref, xh_ref, xl_ref, dh_ref, dl_ref, b_ref, c_ref,
    smine, sgot, amine, agot, kept, sent, *refs,
):
    raws, us = refs[:n_parts], refs[n_parts : 2 * n_parts]
    gi_ref, gs_ref, gi_s, v_s, u_s, k_s, dt_s, rate_s = refs[-8:]
    core, y, _ = place()
    for j in range(J):
        for k in range(G):
            row = slice(J * k + j, J * k + j + 1)
            dt_s[row, :] = dt_ref[k, j : j + 1, :]
            rate_s[row, :] = jnp.full((1, T), rate[j, k], F32)
    seg_row = seg_ref[...].astype(F32)
    seg_t = token_rows(seg_row)
    first, last = firsts(seg_t).astype(BF16), lasts(seg_t).astype(BF16)
    ones = head_ones()
    for g in range(G):
        state, adjoint = of_half(core, g, smine, sgot), of_half(core, g, amine, agot)
        reverse = reverse_block(core, y, g, kept, sent, slice(0, ROWS))
        crossing = state * (reverse[:N] + reverse[DEC : DEC + 1] * adjoint)
        k_s[g] = head_sums(ones, crossing)
        sh, sl = split2(state)
        c = c_ref[g] * first
        out = dot(c, sh) + dot(c, sl)
        u_s[g] = piece(us, g)[...] + head_sums(ones, out * (dh_ref[g].astype(F32) + dl_ref[g].astype(F32)))
        ah, al = split2(adjoint * reverse[ELAST : ELAST + 1])
        b = b_ref[g] * last
        raw = piece(raws, g)[...] + dot(b, ah) + dot(b, al)
        q = dot(qt_ref[...], expander(g))
        gi_s[g] = (q * raw).astype(BF16)
        v_s[g] = head_sums(ones, raw * (xh_ref[g].astype(F32) + xl_ref[g].astype(F32)))
    gi_ref[...] = jnp.swapaxes(gi_s[...], 0, 1)
    v = jnp.concatenate([v_s[k][:J] for k in range(G)], axis=0)
    u = jnp.concatenate([u_s[k][:J] for k in range(G)], axis=0)
    cross = jnp.concatenate([k_s[k][:J] for k in range(G)], axis=0)
    total = jnp.sum(cross, axis=1, keepdims=True)
    change = v - u + jnp.where(iota((32, T), 1) == 0, total, 0.0)
    run3 = dot_t(jnp.concatenate(split3(change), axis=0), lows(seg_t, seg_row).astype(BF16))
    inter = run3[:32] + run3[32:64] + run3[64:96] + u
    grad = v / dt_s[...] + rate_s[...] * (inter - v)
    for k in range(G):
        gs_ref[k] = grad[J * k : J * k + J]


def token_grads(args, raws, us, after):
    args = (*args, *raws, *us, *after)
    heads = pltpu.VMEM((G, 8, T), F32)
    return call(
        functools.partial(token_kernel, len(raws)),
        args,
        [SMEM] + [VMEM] * (len(args) - 1 - len(after)) + [HBM] * len(after),
        [sds(T, G, W, dtype=BF16), sds(G, J, T)],
        [
            pltpu.VMEM((G, T, W), BF16), heads, heads, pltpu.VMEM((G, 8, N), F32),
            pltpu.VMEM((32, T), F32), pltpu.VMEM((32, T), F32),
        ],
        "token_grads", 6000, 16, VMEM,
    )


def over_heads(parts):
    return [along_x(parts[s], s) for s in (1, 2, 3)]


def total(own, got):
    return jnp.transpose(own + got[0] + got[1] + got[2], (1, 0, 2))


def per_device(inputs, step_size, decay_rate, b_proj, c_proj, grad_out, segment_ids):
    seg = segment_ids.reshape(1, T)
    dt = jnp.transpose(step_size, (1, 2, 0))
    rate = jnp.transpose(decay_rate)
    xh, xl, dh, dl, b, c, qt, fs, fk, rs, rk = summaries(dt, rate, seg, inputs, grad_out, b_proj, c_proj)
    data = (xh, xl, dh, dl, b, c)

    def spread_y(blocks):
        return [blocks[0]] + [along_y(blocks[s], s) for s in (1, 2, 3)]

    def local(g0, count, *after):
        return local_grads(g0, count, seg, data, after)

    fgot, rgot = swap(fs), swap(rs)
    fjoined = chip_join(fk, fgot, 0)
    rjoined = chip_join(rk, rgot, 1, (fjoined[0],))
    held = [local(0, 3, rjoined[0])]
    fblocks, rblocks = spread_y(fjoined), spread_y(rjoined)
    fplane = plane_join(fblocks, 0, (held[0][3],))
    held.append(local(3, 2, fplane))
    rplane = plane_join(rblocks, 1, (held[1][3],))
    held.append(local(5, 3, rplane))
    fenter = plane_enter(fblocks, along_z(fplane, 1), along_z(fplane, 2), 0, (held[2][3],))
    renter = plane_enter(rblocks, along_z(rplane, -1), along_z(rplane, -2), 1, (fenter[0],))
    gc, gb, raw, u = zip(*held)
    smine, fother = device_enter(spread_y(fenter), fk, fgot, 0)
    sgot = swap(fother)
    parts_c = summed(False, seg, dh, dl, smine, sgot, (), gc, ())
    got_c = over_heads(parts_c)
    amine, rother = device_enter(spread_y(renter), rk, rgot, 1, (smine,))
    agot = swap(rother)
    parts_b = summed(True, seg, xh, xl, amine, agot, (rk, rs), gb, (parts_c[0],))
    got_b = over_heads(parts_b)
    grad_in, grad_step = token_grads(
        (rate, seg, dt, qt, xh, xl, dh, dl, b, c, smine, sgot, amine, agot, rk, rs), raw, u, (parts_b[0],)
    )
    total_c, total_b = total(parts_c[0], got_c), total(parts_b[0], got_b)
    return grad_in, jnp.transpose(grad_step, (2, 0, 1)), total_b, total_c


def solution(mesh):
    fine = Mesh(mesh.devices.reshape(8, 4, 2, 4), (Z, Y, C, X))
    ctx = (Z, Y, C)
    placed = (
        P(ctx, None, X),
        P(ctx, None, X),
        P(None, X),
        P(ctx, None, None),
        P(ctx, None, None),
        P(ctx, None, X),
        P(ctx),
    )
    return jax.shard_map(
        per_device,
        mesh=fine,
        in_specs=placed,
        out_specs=(P(ctx, None, X), P(ctx, None, X), P(ctx, X, None), P(ctx, X, None)),
        check_vma=False,
    )
```

time: 1190 us -> 95.7 us (0.08); the launches traced: 1180 us -> 95.3 us
  loops' own time: 314 us -> 0 us
  other arithmetic: 267 us -> 0.15 us
  blocking collectives: 231 us -> 0 us
  local copies, waits for them, and re-layouts: 229 us -> 9.81 us
  matrix products: 54 us -> 0 us
  waiting for transfers between devices: 56.8 us -> 18.1 us
  starting transfers between devices: 0.12 us -> 38.2 us
  Pallas kernels: 0 us -> 28.1 us
  between operations: 23.1 us -> 0.92 us
    another operation x3 -> x0, loops' own time: 314 us -> none  [the longest x2 314 us: prefix(): return lax.fori_loop(0, count - 1, turn, total)]
    select_n x126 -> x0, other arithmetic: 185 us -> none  [turn(): jnp.where(position < mine, new, old)]
    unnamed x1 -> x0, blocking collectives: 127 us -> none
    all_gather x2 -> x0, blocking collectives: 104 us -> none  [prefix(): pieces = jax.tree.map(lambda part: lax.all_gather(part, axis), value)]
    dynamic_slice x136 -> x0, local copies, waits for them, and re-layouts: 82.5 us -> none  [the longest x126 75.2 us: turn(): longer = join(total, jax.tree.map(lambda part: part[position], pieces))]
    psum x1 -> x0, waiting for transfers between devices: 56.7 us -> none  [per_device(): whole_b, whole_c = lax.psum((part_b, part_c), 'head')]
    dot_general x24 -> x0, matrix products: 54 us -> none  [the longest x20 46.2 us: product(): return jnp.einsum(pattern, first_op, second_op, precision=PRECISE)]
    another operation x8 -> x0, other arithmetic: 51.3 us -> none  [the longest x4 46.9 us: span_weights(): cumlog = jnp.cumsum(step_size * decay_rate[None], axis=0)]
  transfers between devices with their start and end apart: 3 -> 26, of which waited for: 1 -> 10; matrix products, arithmetic and copies ran while one was open for 15% -> 1% of each run, Pallas kernels for 0% -> 20%
where the time goes in v2:
time: 95.7 us; the launch traced here: 95.3 us
  starting transfers between devices  38.2 us (40%)
  Pallas kernels  28.1 us (29%)
  waiting for transfers between devices  18.1 us (19%)
  local copies, waits for them, and re-layouts  9.81 us (10%)
    pallas_call x15, Pallas kernels, call(): pl.pallas_call(kernel, in_specs=specs, out_specs=[out_spec] * len(outs),...  28.1 us
    ppermute x12, starting transfers between devices, along_y(): return lax.ppermute(v, Y, ring(4, shift))  13.6 us
    ppermute x6, waiting for transfers between devices, along_x(): return lax.ppermute(v, X, ring(4, shift))  11.5 us
    ppermute x4, starting transfers between devices, swap(): return lax.ppermute(v, C, ring(2, 1))  9.99 us
    unnamed x40, local copies, waits for them, and re-layouts  9.81 us
    ppermute x6, starting transfers between devices, along_x(): return lax.ppermute(v, X, ring(4, shift))  7.33 us
    ppermute x4, starting transfers between devices, along_z(): return lax.ppermute(v, Z, ring(8, shift))  7.3 us
    ppermute x12, waiting for transfers between devices, along_y(): return lax.ppermute(v, Y, ring(4, shift))  3.48 us
  transfers between devices with their start and end apart: 26, of which 10 were waited for; matrix products, arithmetic and copies ran while one was open for 1% of the time, Pallas kernels for 20%

profile of v2, /device:TPU:1, one launch (start us, length us, event | category | flops | bytes accessed | tf_op | source)
XLA Modules:
  0.0 95.3 jit_solution(15955071654897184184)
XLA Ops:
  0.6 6.0 %summaries.1 = (bf16[8,256,256]{2,1,0:T(8,128)(2,1)}, bf16[8,256,256]{2,1,0:T(8,128)(2,1)}, bf16[8,256,256]{2,1,0:T(8,128)(2,1)}, bf16[8,256,256]{2,1,0:T(8,128)...) custom-call(f32[4,8]{1,0:T(4,128)} %bitcast.17, ...), custom_call_target="tpu_custom_call" | custom-call | flops 8000000 | bytes 1024 | tf_op jit(solution)/shard_map/summaries/pallas_call | solution.py:108
  6.6 3.3 %collective-permute-start = (f32[4,136,256]{2,1,0:T(8,128)}, f32[4,136,256]{2,1,0:T(8,128)S(1)}, u32[]{:S(2)}, u32[]{:S(2)}) collective-permute-start(f32[4,136,256]{2,1,0:T(8,128)} %get-tuple-element.65), channel_id=1, source_target_pairs={{0,4},{4,0},{1,5},{5,1},{2,6},{6,2},{3,7},{7,3},{8,12},{12,8},{9,1... | collective-permute-start | bytes 1671176 | tf_op jit(solution)/shard_map/ppermute | solution.py:387
  10.0 1.7 %collective-permute-done.refs_1_.refs_5_ = f32[4,136,256]{2,1,0:T(8,128)S(1)} collective-permute-done((f32[4,136,256]{2,1,0:T(8,128)}, f32[4,136,256]{2,1,0:T(8,128)S(1)}, u32[]{:S(2)}, u32[]{:S(2)}) %collective-permute-start) | collective-permute-done | bytes 557088 | tf_op jit(solution)/shard_map/ppermute | solution.py:387
  13.0 2.2 %collective-permute-start.2 = (f32[136,256]{1,0:T(8,128)S(1)}, f32[136,256]{1,0:T(8,128)S(1)}, u32[]{:S(2)}, u32[]{:S(2)}) collective-permute-start(f32[136,256]{1,0:T(8,128)S(1)} %get-tuple-element.68), channel_id=1, source_target_pairs={{0,16},{8,24},{16,0},{24,8},{1,17},{9,25},{17,1},{25,9},{2,18},{10... | collective-permute-start | bytes 417800 | tf_op jit(solution)/shard_map/ppermute | solution.py:391
  17.8 1.5 %collective-permute-start.8 = (f32[136,256]{1,0:T(8,128)S(1)}, f32[136,256]{1,0:T(8,128)S(1)}, u32[]{:S(2)}, u32[]{:S(2)}) collective-permute-start(f32[136,256]{1,0:T(8,128)S(1)} %get-tuple-element.75), channel_id=1, source_target_pairs={{0,16},{8,24},{16,0},{24,8},{1,17},{9,25},{17,1},{25,9},{2,18},{10... | collective-permute-start | bytes 417800 | tf_op jit(solution)/shard_map/ppermute | solution.py:391
  19.6 1.7 %collective-permute-start.9 = (f32[136,256]{1,0:T(8,128)S(1)}, f32[136,256]{1,0:T(8,128)S(1)}, u32[]{:S(2)}, u32[]{:S(2)}) collective-permute-start(f32[136,256]{1,0:T(8,128)S(1)} %get-tuple-element.76), channel_id=1, source_target_pairs={{0,24},{8,0},{16,8},{24,16},{1,25},{9,1},{17,9},{25,17},{2,26},{10... | collective-permute-start | bytes 417800 | tf_op jit(solution)/shard_map/ppermute | solution.py:391
  26.5 3.3 %local_grads.3 = (f32[3,256,128]{2,1,0:T(8,128)S(1)}, f32[3,256,128]{2,1,0:T(8,128)S(1)}, f32[3,256,256]{2,1,0:T(8,128)S(1)}, f32[3,8,256]{2,1,0:T(8,128)S(1)}) custom-call(s32[1,256]{1,0:T(1,128)S(1)} %bitcast.11, bf16[8,256,256]{2,1,0:T(8,128)(2,1)S(1)} %copy-done.2, bf16[8,256,256]{2,1,0:T(8,128)(2,1)S(1)} %copy-done.4, bf16[8,256,256]{2,1,0:T(8,128)(2,1)S(1)} %copy-done, ...), custom_call_target="tpu_custom_call" | custom-call | flops 3000000 | bytes 1024 | tf_op jit(solution)/shard_map/local_grads/pallas_call | solution.py:108
  29.9 2.3 %collective-permute-start.6 = (f32[136,256]{1,0:T(8,128)S(1)}, f32[136,256]{1,0:T(8,128)S(1)}, u32[]{:S(2)}, u32[]{:S(2)}) collective-permute-start(f32[136,256]{1,0:T(8,128)S(1)} %plane_join.2.refs_6_), channel_id=1, source_target_pairs={{0,64},{32,96},{64,128},{96,160},{128,192},{160,224},{192,0},{224,... | collective-permute-start | bytes 417800 | tf_op jit(solution)/shard_map/ppermute | solution.py:395
  32.2 1.6 %collective-permute-start.5 = (f32[136,256]{1,0:T(8,128)S(1)}, f32[136,256]{1,0:T(8,128)S(1)}, u32[]{:S(2)}, u32[]{:S(2)}) collective-permute-start(f32[136,256]{1,0:T(8,128)S(1)} %plane_join.2.refs_6_), channel_id=1, source_target_pairs={{0,32},{32,64},{64,96},{96,128},{128,160},{160,192},{192,224},{224... | collective-permute-start | bytes 417800 | tf_op jit(solution)/shard_map/ppermute | solution.py:395
  33.8 2.3 %local_grads.4 = (f32[2,256,128]{2,1,0:T(8,128)S(1)}, f32[2,256,128]{2,1,0:T(8,128)S(1)}, f32[2,256,256]{2,1,0:T(8,128)S(1)}, f32[2,8,256]{2,1,0:T(8,128)S(1)}) custom-call(s32[1,256]{1,0:T(1,128)S(1)} %bitcast.12, bf16[8,256,256]{2,1,0:T(8,128)(2,1)S(1)} %copy-done.2, bf16[8,256,256]{2,1,0:T(8,128)(2,1)S(1)} %copy-done.4, bf16[8,256,256]{2,1,0:T(8,128)(2,1)S(1)} %copy-done, ...), custom_call_target="tpu_custom_call" | custom-call | flops 3000000 | bytes 1024 | tf_op jit(solution)/shard_map/local_grads/pallas_call | solution.py:108
  36.2 2.3 %collective-permute-start.15 = (f32[136,256]{1,0:T(8,128)S(1)}, f32[136,256]{1,0:T(8,128)S(1)}, u32[]{:S(2)}, u32[]{:S(2)}) collective-permute-start(f32[136,256]{1,0:T(8,128)S(1)} %plane_join.3.refs_6_), channel_id=1, source_target_pairs={{0,192},{32,224},{64,0},{96,32},{128,64},{160,96},{192,128},{224,1... | collective-permute-start | bytes 417800 | tf_op jit(solution)/shard_map/ppermute | solution.py:395
  39.6 3.3 %local_grads.5 = (f32[3,256,128]{2,1,0:T(8,128)S(1)}, f32[3,256,128]{2,1,0:T(8,128)S(1)}, f32[3,256,256]{2,1,0:T(8,128)S(1)}, f32[3,8,256]{2,1,0:T(8,128)S(1)}) custom-call(s32[1,256]{1,0:T(1,128)S(1)} %bitcast.13, bf16[8,256,256]{2,1,0:T(8,128)(2,1)S(1)} %copy-done.2, bf16[8,256,256]{2,1,0:T(8,128)(2,1)S(1)} %copy-done.4, bf16[8,256,256]{2,1,0:T(8,128)(2,1)S(1)} %copy-done, ...), custom_call_target="tpu_custom_call" | custom-call | flops 3000000 | bytes 1024 | tf_op jit(solution)/shard_map/local_grads/pallas_call | solution.py:108
  44.9 1.7 %collective-permute-start.11 = (f32[128,256]{1,0:T(8,128)S(1)}, f32[128,256]{1,0:T(8,128)S(1)}, u32[]{:S(2)}, u32[]{:S(2)}) collective-permute-start(f32[128,256]{1,0:T(8,128)S(1)} %get-tuple-element.81), channel_id=1, source_target_pairs={{0,16},{8,24},{16,0},{24,8},{1,17},{9,25},{17,1},{25,9},{2,18},{10... | collective-permute-start | bytes 393224 | tf_op jit(solution)/shard_map/ppermute | solution.py:391
  46.6 2.0 %collective-permute-start.12 = (f32[128,256]{1,0:T(8,128)S(1)}, f32[128,256]{1,0:T(8,128)S(1)}, u32[]{:S(2)}, u32[]{:S(2)}) collective-permute-start(f32[128,256]{1,0:T(8,128)S(1)} %get-tuple-element.82), channel_id=1, source_target_pairs={{0,24},{8,0},{16,8},{24,16},{1,25},{9,1},{17,9},{25,17},{2,26},{10... | collective-permute-start | bytes 393224 | tf_op jit(solution)/shard_map/ppermute | solution.py:391
  48.8 1.6 %collective-permute-start.17 = (f32[128,256]{1,0:T(8,128)S(1)}, f32[128,256]{1,0:T(8,128)S(1)}, u32[]{:S(2)}, u32[]{:S(2)}) collective-permute-start(f32[128,256]{1,0:T(8,128)S(1)} %get-tuple-element.87), channel_id=1, source_target_pairs={{0,16},{8,24},{16,0},{24,8},{1,17},{9,25},{17,1},{25,9},{2,18},{10... | collective-permute-start | bytes 393224 | tf_op jit(solution)/shard_map/ppermute | solution.py:391
  52.7 3.9 %collective-permute-start.13 = (f32[4,128,256]{2,1,0:T(8,128)S(1)}, f32[4,128,256]{2,1,0:T(8,128)S(1)}, u32[]{:S(2)}, u32[]{:S(2)}) collective-permute-start(f32[4,128,256]{2,1,0:T(8,128)S(1)} %get-tuple-element.84), channel_id=1, source_target_pairs={{0,4},{4,0},{1,5},{5,1},{2,6},{6,2},{3,7},{7,3},{8,12},{12,8},{9,1... | collective-permute-start | bytes 1572872 | tf_op jit(solution)/shard_map/ppermute | solution.py:387
  58.5 2.6 %collective-permute-start.19 = (f32[4,128,256]{2,1,0:T(8,128)S(1)}, f32[4,128,256]{2,1,0:T(8,128)S(1)}, u32[]{:S(2)}, u32[]{:S(2)}) collective-permute-start(f32[4,128,256]{2,1,0:T(8,128)S(1)} %get-tuple-element.90), channel_id=1, source_target_pairs={{0,4},{4,0},{1,5},{5,1},{2,6},{6,2},{3,7},{7,3},{8,12},{12,8},{9,1... | collective-permute-start | bytes 1572872 | tf_op jit(solution)/shard_map/ppermute | solution.py:387
  61.1 3.0 %summed.2 = (f32[2,256,128]{2,1,0:T(8,128)S(1)}, f32[2,256,128]{2,1,0:T(8,128)S(1)}, f32[2,256,128]{2,1,0:T(8,128)S(1)}, f32[2,256,128]{2,1,0:T(8,128)S(1)}) custom-call(s32[1,256]{1,0:T(1,128)S(1)} %bitcast.14, bf16[8,256,256]{2,1,0:T(8,128)(2,1)S(1)} %copy-done, bf16[8,256,256]{2,1,0:T(8,128)(2,1)S(1)} %copy-done.1, ...), custom_call_target="tpu_custom_call" | custom-call | flops 3000000 | bytes 1024 | tf_op jit(solution)/shard_map/summed/pallas_call | solution.py:108
  64.2 3.0 %summed.3 = (f32[2,256,128]{2,1,0:T(8,128)S(1)}, f32[2,256,128]{2,1,0:T(8,128)S(1)}, f32[2,256,128]{2,1,0:T(8,128)S(1)}, f32[2,256,128]{2,1,0:T(8,128)S(1)}) custom-call(s32[1,256]{1,0:T(1,128)S(1)} %bitcast.15, bf16[8,256,256]{2,1,0:T(8,128)(2,1)S(1)} %copy-done.2, bf16[8,256,256]{2,1,0:T(8,128)(2,1)S(1)} %copy-done.4, ...), custom_call_target="tpu_custom_call" | custom-call | flops 3000000 | bytes 1024 | tf_op jit(solution)/shard_map/summed/pallas_call | solution.py:108
  68.5 2.4 %collective-permute-start.21 = (f32[2,256,128]{2,1,0:T(8,128)S(1)}, f32[2,256,128]{2,1,0:T(8,128)S(1)}, u32[]{:S(2)}, u32[]{:S(2)}) collective-permute-start(f32[2,256,128]{2,1,0:T(8,128)S(1)} %get-tuple-element.105), channel_id=1, source_target_pairs={{0,2},{1,3},{2,0},{3,1},{4,6},{5,7},{6,4},{7,5},{8,10},{9,11},{10,... | collective-permute-start | bytes 786440 | tf_op jit(solution)/shard_map/ppermute | solution.py:399
  73.3 3.1 %collective-permute-done.20 = f32[2,256,128]{2,1,0:T(8,128)S(1)} collective-permute-done((f32[2,256,128]{2,1,0:T(8,128)S(1)}, f32[2,256,128]{2,1,0:T(8,128)S(1)}, u32[]{:S(2)}, u32[]{:S(2)}) %collective-permute-start.20) | collective-permute-done | bytes 262176 | tf_op jit(solution)/shard_map/ppermute | solution.py:399
  78.4 6.6 %token_grads.1 = (bf16[256,8,256]{2,1,0:T(8,128)(2,1)}, f32[8,4,256]{2,1,0:T(4,128)}) custom-call(f32[4,8]{1,0:T(4,128)S(1)} %bitcast.18, s32[1,256]{1,0:T(1,128)S(1)} %bitcast.16, f32[8,4,256]{2,1,0:T(4,128)S(1)} %bitcast.9, bf16[256,128]{1,0:T(8,128)(2,1)S(1)} %copy-done.16, bf16[8,256,256]{2,1,0:T(8,128)(2,1)S(1)} %copy-done.3, ...), custom_call_target="tpu_custom_call" | custom-call | flops 6000000 | bytes 1024 | tf_op jit(solution)/shard_map/token_grads/pallas_call | solution.py:108
  85.9 1.6 %collective-permute-done.23 = f32[2,256,128]{2,1,0:T(8,128)S(1)} collective-permute-done((f32[2,256,128]{2,1,0:T(8,128)S(1)}, f32[2,256,128]{2,1,0:T(8,128)S(1)}, u32[]{:S(2)}, u32[]{:S(2)}) %collective-permute-start.23) | collective-permute-done | bytes 262176 | tf_op jit(solution)/shard_map/ppermute | solution.py:399
  87.5 6.8 %collective-permute-done.24 = f32[2,256,128]{2,1,0:T(8,128)S(1)} collective-permute-done((f32[2,256,128]{2,1,0:T(8,128)S(1)}, f32[2,256,128]{2,1,0:T(8,128)S(1)}, u32[]{:S(2)}, u32[]{:S(2)}) %collective-permute-start.24) | collective-permute-done | bytes 262176 | tf_op jit(solution)/shard_map/ppermute | solution.py:399
  (85 shorter events, 24.6 us)
Async XLA Ops:
  9.9 6.3 %collective-permute-start.4 = (f32[4,136,256]{2,1,0:T(8,128)}, f32[4,136,256]{2,1,0:T(8,128)S(1)}, u32[]{:S(2)}, u32[]{:S(2)}) collective-permute-start(f32[4,136,256]{2,1,0:T(8,128)} %get-tuple-element.71.refs_1_.sent), channel_id=1, source_target_pairs={{0,4},{4,0},{1,5},{5,1},{2,6},{6,2},{3,7},{7,3},{8,12},{12,8},{9,1... | collective-permute-start | bytes 1671176 | tf_op jit(solution)/shard_map/ppermute | solution.py:387
  12.9 6.7 %collective-permute-start.1 = (f32[136,256]{1,0:T(8,128)S(1)}, f32[136,256]{1,0:T(8,128)S(1)}, u32[]{:S(2)}, u32[]{:S(2)}) collective-permute-start(f32[136,256]{1,0:T(8,128)S(1)} %get-tuple-element.67), channel_id=1, source_target_pairs={{0,8},{8,16},{16,24},{24,0},{1,9},{9,17},{17,25},{25,1},{2,10},{10... | collective-permute-start | bytes 417800 | tf_op jit(solution)/shard_map/ppermute | solution.py:391
  13.0 16.8 %collective-permute-start.2 = (f32[136,256]{1,0:T(8,128)S(1)}, f32[136,256]{1,0:T(8,128)S(1)}, u32[]{:S(2)}, u32[]{:S(2)}) collective-permute-start(f32[136,256]{1,0:T(8,128)S(1)} %get-tuple-element.68), channel_id=1, source_target_pairs={{0,16},{8,24},{16,0},{24,8},{1,17},{9,25},{17,1},{25,9},{2,18},{10... | collective-permute-start | bytes 417800 | tf_op jit(solution)/shard_map/ppermute | solution.py:391
  15.2 14.7 %collective-permute-start.3 = (f32[136,256]{1,0:T(8,128)S(1)}, f32[136,256]{1,0:T(8,128)S(1)}, u32[]{:S(2)}, u32[]{:S(2)}) collective-permute-start(f32[136,256]{1,0:T(8,128)S(1)} %get-tuple-element.69), channel_id=1, source_target_pairs={{0,24},{8,0},{16,8},{24,16},{1,25},{9,1},{17,9},{25,17},{2,26},{10... | collective-permute-start | bytes 417800 | tf_op jit(solution)/shard_map/ppermute | solution.py:391
  17.4 18.8 %collective-permute-start.7 = (f32[136,256]{1,0:T(8,128)S(1)}, f32[136,256]{1,0:T(8,128)S(1)}, u32[]{:S(2)}, u32[]{:S(2)}) collective-permute-start(f32[136,256]{1,0:T(8,128)S(1)} %get-tuple-element.74), channel_id=1, source_target_pairs={{0,8},{8,16},{16,24},{24,0},{1,9},{9,17},{17,25},{25,1},{2,10},{10... | collective-permute-start | bytes 417800 | tf_op jit(solution)/shard_map/ppermute | solution.py:391
  17.8 18.3 %collective-permute-start.8 = (f32[136,256]{1,0:T(8,128)S(1)}, f32[136,256]{1,0:T(8,128)S(1)}, u32[]{:S(2)}, u32[]{:S(2)}) collective-permute-start(f32[136,256]{1,0:T(8,128)S(1)} %get-tuple-element.75), channel_id=1, source_target_pairs={{0,16},{8,24},{16,0},{24,8},{1,17},{9,25},{17,1},{25,9},{2,18},{10... | collective-permute-start | bytes 417800 | tf_op jit(solution)/shard_map/ppermute | solution.py:391
  19.6 16.6 %collective-permute-start.9 = (f32[136,256]{1,0:T(8,128)S(1)}, f32[136,256]{1,0:T(8,128)S(1)}, u32[]{:S(2)}, u32[]{:S(2)}) collective-permute-start(f32[136,256]{1,0:T(8,128)S(1)} %get-tuple-element.76), channel_id=1, source_target_pairs={{0,24},{8,0},{16,8},{24,16},{1,25},{9,1},{17,9},{25,17},{2,26},{10... | collective-permute-start | bytes 417800 | tf_op jit(solution)/shard_map/ppermute | solution.py:391
  29.9 13.0 %collective-permute-start.6 = (f32[136,256]{1,0:T(8,128)S(1)}, f32[136,256]{1,0:T(8,128)S(1)}, u32[]{:S(2)}, u32[]{:S(2)}) collective-permute-start(f32[136,256]{1,0:T(8,128)S(1)} %plane_join.2.refs_6_), channel_id=1, source_target_pairs={{0,64},{32,96},{64,128},{96,160},{128,192},{160,224},{192,0},{224,... | collective-permute-start | bytes 417800 | tf_op jit(solution)/shard_map/ppermute | solution.py:395
  32.2 12.2 %collective-permute-start.5 = (f32[136,256]{1,0:T(8,128)S(1)}, f32[136,256]{1,0:T(8,128)S(1)}, u32[]{:S(2)}, u32[]{:S(2)}) collective-permute-start(f32[136,256]{1,0:T(8,128)S(1)} %plane_join.2.refs_6_), channel_id=1, source_target_pairs={{0,32},{32,64},{64,96},{96,128},{128,160},{160,192},{192,224},{224... | collective-permute-start | bytes 417800 | tf_op jit(solution)/shard_map/ppermute | solution.py:395
  36.2 12.3 %collective-permute-start.15 = (f32[136,256]{1,0:T(8,128)S(1)}, f32[136,256]{1,0:T(8,128)S(1)}, u32[]{:S(2)}, u32[]{:S(2)}) collective-permute-start(f32[136,256]{1,0:T(8,128)S(1)} %plane_join.3.refs_6_), channel_id=1, source_target_pairs={{0,192},{32,224},{64,0},{96,32},{128,64},{160,96},{192,128},{224,1... | collective-permute-start | bytes 417800 | tf_op jit(solution)/shard_map/ppermute | solution.py:395
  38.5 10.0 %collective-permute-start.14 = (f32[136,256]{1,0:T(8,128)S(1)}, f32[136,256]{1,0:T(8,128)S(1)}, u32[]{:S(2)}, u32[]{:S(2)}) collective-permute-start(f32[136,256]{1,0:T(8,128)S(1)} %plane_join.3.refs_6_), channel_id=1, source_target_pairs={{0,224},{32,0},{64,32},{96,64},{128,96},{160,128},{192,160},{224,1... | collective-permute-start | bytes 417800 | tf_op jit(solution)/shard_map/ppermute | solution.py:395
  44.5 7.3 %collective-permute-start.10 = (f32[128,256]{1,0:T(8,128)S(1)}, f32[128,256]{1,0:T(8,128)S(1)}, u32[]{:S(2)}, u32[]{:S(2)}) collective-permute-start(f32[128,256]{1,0:T(8,128)S(1)} %get-tuple-element.80), channel_id=1, source_target_pairs={{0,8},{8,16},{16,24},{24,0},{1,9},{9,17},{17,25},{25,1},{2,10},{10... | collective-permute-start | bytes 393224 | tf_op jit(solution)/shard_map/ppermute | solution.py:391
  44.9 7.5 %collective-permute-start.11 = (f32[128,256]{1,0:T(8,128)S(1)}, f32[128,256]{1,0:T(8,128)S(1)}, u32[]{:S(2)}, u32[]{:S(2)}) collective-permute-start(f32[128,256]{1,0:T(8,128)S(1)} %get-tuple-element.81), channel_id=1, source_target_pairs={{0,16},{8,24},{16,0},{24,8},{1,17},{9,25},{17,1},{25,9},{2,18},{10... | collective-permute-start | bytes 393224 | tf_op jit(solution)/shard_map/ppermute | solution.py:391
  46.6 6.0 %collective-permute-start.12 = (f32[128,256]{1,0:T(8,128)S(1)}, f32[128,256]{1,0:T(8,128)S(1)}, u32[]{:S(2)}, u32[]{:S(2)}) collective-permute-start(f32[128,256]{1,0:T(8,128)S(1)} %get-tuple-element.82), channel_id=1, source_target_pairs={{0,24},{8,0},{16,8},{24,16},{1,25},{9,1},{17,9},{25,17},{2,26},{10... | collective-permute-start | bytes 393224 | tf_op jit(solution)/shard_map/ppermute | solution.py:391
  48.7 8.5 %collective-permute-start.16 = (f32[128,256]{1,0:T(8,128)S(1)}, f32[128,256]{1,0:T(8,128)S(1)}, u32[]{:S(2)}, u32[]{:S(2)}) collective-permute-start(f32[128,256]{1,0:T(8,128)S(1)} %get-tuple-element.86), channel_id=1, source_target_pairs={{0,8},{8,16},{16,24},{24,0},{1,9},{9,17},{17,25},{25,1},{2,10},{10... | collective-permute-start | bytes 393224 | tf_op jit(solution)/shard_map/ppermute | solution.py:391
  48.8 8.4 %collective-permute-start.17 = (f32[128,256]{1,0:T(8,128)S(1)}, f32[128,256]{1,0:T(8,128)S(1)}, u32[]{:S(2)}, u32[]{:S(2)}) collective-permute-start(f32[128,256]{1,0:T(8,128)S(1)} %get-tuple-element.87), channel_id=1, source_target_pairs={{0,16},{8,24},{16,0},{24,8},{1,17},{9,25},{17,1},{25,9},{2,18},{10... | collective-permute-start | bytes 393224 | tf_op jit(solution)/shard_map/ppermute | solution.py:391
  51.8 6.6 %collective-permute-start.18 = (f32[128,256]{1,0:T(8,128)S(1)}, f32[128,256]{1,0:T(8,128)S(1)}, u32[]{:S(2)}, u32[]{:S(2)}) collective-permute-start(f32[128,256]{1,0:T(8,128)S(1)} %get-tuple-element.88), channel_id=1, source_target_pairs={{0,24},{8,0},{16,8},{24,16},{1,25},{9,1},{17,9},{25,17},{2,26},{10... | collective-permute-start | bytes 393224 | tf_op jit(solution)/shard_map/ppermute | solution.py:391
  52.7 8.4 %collective-permute-start.13 = (f32[4,128,256]{2,1,0:T(8,128)S(1)}, f32[4,128,256]{2,1,0:T(8,128)S(1)}, u32[]{:S(2)}, u32[]{:S(2)}) collective-permute-start(f32[4,128,256]{2,1,0:T(8,128)S(1)} %get-tuple-element.84), channel_id=1, source_target_pairs={{0,4},{4,0},{1,5},{5,1},{2,6},{6,2},{3,7},{7,3},{8,12},{12,8},{9,1... | collective-permute-start | bytes 1572872 | tf_op jit(solution)/shard_map/ppermute | solution.py:387
  67.3 9.2 %collective-permute-start.20 = (f32[2,256,128]{2,1,0:T(8,128)S(1)}, f32[2,256,128]{2,1,0:T(8,128)S(1)}, u32[]{:S(2)}, u32[]{:S(2)}) collective-permute-start(f32[2,256,128]{2,1,0:T(8,128)S(1)} %get-tuple-element.104), channel_id=1, source_target_pairs={{0,1},{1,2},{2,3},{3,0},{4,5},{5,6},{6,7},{7,4},{8,9},{9,10},{10,1... | collective-permute-start | bytes 786440 | tf_op jit(solution)/shard_map/ppermute | solution.py:399
  68.5 16.4 %collective-permute-start.21 = (f32[2,256,128]{2,1,0:T(8,128)S(1)}, f32[2,256,128]{2,1,0:T(8,128)S(1)}, u32[]{:S(2)}, u32[]{:S(2)}) collective-permute-start(f32[2,256,128]{2,1,0:T(8,128)S(1)} %get-tuple-element.105), channel_id=1, source_target_pairs={{0,2},{1,3},{2,0},{3,1},{4,6},{5,7},{6,4},{7,5},{8,10},{9,11},{10,... | collective-permute-start | bytes 786440 | tf_op jit(solution)/shard_map/ppermute | solution.py:399
  71.0 14.0 %collective-permute-start.22 = (f32[2,256,128]{2,1,0:T(8,128)S(1)}, f32[2,256,128]{2,1,0:T(8,128)S(1)}, u32[]{:S(2)}, u32[]{:S(2)}) collective-permute-start(f32[2,256,128]{2,1,0:T(8,128)S(1)} %get-tuple-element.106), channel_id=1, source_target_pairs={{0,3},{1,0},{2,1},{3,2},{4,7},{5,4},{6,5},{7,6},{8,11},{9,8},{10,9... | collective-permute-start | bytes 786440 | tf_op jit(solution)/shard_map/ppermute | solution.py:399
  72.2 15.3 %collective-permute-start.23 = (f32[2,256,128]{2,1,0:T(8,128)S(1)}, f32[2,256,128]{2,1,0:T(8,128)S(1)}, u32[]{:S(2)}, u32[]{:S(2)}) collective-permute-start(f32[2,256,128]{2,1,0:T(8,128)S(1)} %get-tuple-element.107), channel_id=1, source_target_pairs={{0,1},{1,2},{2,3},{3,0},{4,5},{5,6},{6,7},{7,4},{8,9},{9,10},{10,1... | collective-permute-start | bytes 786440 | tf_op jit(solution)/shard_map/ppermute | solution.py:399
  72.4 21.9 %collective-permute-start.24 = (f32[2,256,128]{2,1,0:T(8,128)S(1)}, f32[2,256,128]{2,1,0:T(8,128)S(1)}, u32[]{:S(2)}, u32[]{:S(2)}) collective-permute-start(f32[2,256,128]{2,1,0:T(8,128)S(1)} %get-tuple-element.108), channel_id=1, source_target_pairs={{0,2},{1,3},{2,0},{3,1},{4,6},{5,7},{6,4},{7,5},{8,10},{9,11},{10,... | collective-permute-start | bytes 786440 | tf_op jit(solution)/shard_map/ppermute | solution.py:399
  76.5 17.9 %collective-permute-start.25 = (f32[2,256,128]{2,1,0:T(8,128)S(1)}, f32[2,256,128]{2,1,0:T(8,128)S(1)}, u32[]{:S(2)}, u32[]{:S(2)}) collective-permute-start(f32[2,256,128]{2,1,0:T(8,128)S(1)} %get-tuple-element.109), channel_id=1, source_target_pairs={{0,3},{1,0},{2,1},{3,2},{4,7},{5,4},{6,5},{7,6},{8,11},{9,8},{10,9... | collective-permute-start | bytes 786440 | tf_op jit(solution)/shard_map/ppermute | solution.py:399
  (21 other events, 134.9 us)

commit v3 on v2

--- a/solution.py
+++ b/solution.py
@@ -225,45 +225,31 @@
     )
 
 
-def local_kernel(g0, count, seg_ref, *refs):
-    ins, outs = refs[:6], refs[-4:]
+def local_kernel(seg_ref, xh_ref, xl_ref, dh_ref, dl_ref, b_ref, c_ref, *refs):
+    gc_ref, gb_ref = refs[-2:]
     seg_row = seg_ref[...].astype(F32)
-    seg_t = token_rows(seg_row)
-    low, high = lows(seg_t, seg_row).astype(F32), highs(seg_t, seg_row).astype(F32)
-    ones = head_ones()
-    for i in range(count):
-        xh, xl, dh, dl, b, c = [ref[g0 + i] for ref in ins]
-        sums = dot_t(dh, xh) + dot_t(dh, xl) + dot_t(dl, xh)
+    low = lows(token_rows(seg_row), seg_row).astype(F32)
+    for g in range(G):
+        xh, dh = xh_ref[g], dh_ref[g]
+        sums = dot_t(dh, xh) + dot_t(dh, xl_ref[g]) + dot_t(dl_ref[g], xh)
         sh, sl = split2(sums * low)
-        outs[0][i] = dot(sh, b) + dot(sl, b)
-        c_tr = jnp.transpose(c)
-        outs[1][i] = jnp.transpose(dot(c_tr, sh) + dot(c_tr, sl))
-        wh, wl = split2(dot_t(c, b) * low)
-        out = dot(wh, xh) + dot(wh, xl) + dot(wl, xh)
-        outs[3][i] = head_sums(ones, out * (dh.astype(F32) + dl.astype(F32)))
-        vh, vl = split2(dot_t(b, c) * high)
-        outs[2][i] = dot(vh, dh) + dot(vh, dl) + dot(vl, dh)
-
-
-def local_grads(g0, count, seg, data, after):
+        gc_ref[g] = dot(sh, b_ref[g]) + dot(sl, b_ref[g])
+        c_tr = jnp.transpose(c_ref[g])
+        gb_ref[g] = jnp.transpose(dot(c_tr, sh) + dot(c_tr, sl))
+
+
+def local_grads(seg, data, after):
     return call(
-        functools.partial(local_kernel, g0, count),
+        local_kernel,
         (seg, *data, *after),
         [VMEM] * 7 + [HBM] * len(after),
-        [sds(count, T, N), sds(count, T, N), sds(count, T, W), sds(count, 8, T)],
+        [sds(G, T, N)] * 2,
         [],
         "local_grads",
         3000,
         12,
         VMEM,
     )
-
-
-def piece(parts, g):
-    for part in parts:
-        if g < part.shape[0]:
-            return part.at[g]
-        g -= part.shape[0]
 
 
 def linked(earlier, later):
@@ -408,48 +394,32 @@
     return jnp.where(core == g // 4, kept[slot, rows, :], sent[slot, rows, :])
 
 
-def sum_kernel(rev, n_parts, seg_ref, hi_ref, lo_ref, mine, got, *refs):
-    if rev:
-        kept, sent, refs = refs[0], refs[1], refs[2:]
-    parts, outs = refs[:n_parts], refs[-4:]
+def sum_kernel(
+    seg_ref, dh_ref, dl_ref, xh_ref, xl_ref, smine, sgot, amine, agot, kept, sent, gc_ref, gb_ref, *outs
+):
     core, y, x = place()
     seg_t = token_rows(seg_ref[...].astype(F32))
-    mask = (lasts(seg_t) if rev else firsts(seg_t)).astype(F32)
-    for g in range(G):
-        state = of_half(core, g, mine, got)
-        if rev:
-            state = state * reverse_block(core, y, g, kept, sent, slice(N, ROWS))[ELAST - N : ELAST - N + 1]
-        sh, sl = split2(state)
-        hi, lo = hi_ref[g], lo_ref[g]
-        whole = piece(parts, g)[...] + mask * (dot_t(hi, sh) + dot_t(hi, sl) + dot_t(lo, sh))
-        shift = lax.rem(g // 2 + 4 - x, 4)
-        for s in range(4):
-
-            @pl.when(shift == s)
-            def _(s=s, whole=whole):
-                outs[s][g % 2] = whole
-
-
-def summed(rev, seg, hi, lo, mine, got, more, parts, after):
-    args = (seg, hi, lo, mine, got, *more, *parts, *after)
-    return call(
-        functools.partial(sum_kernel, rev, len(parts)),
-        args,
-        [VMEM] * (len(args) - len(after)) + [HBM] * len(after),
-        [sds(2, T, N)] * 4,
-        [],
-        "summed",
-        3000,
-        12,
-        VMEM,
-    )
+    first, last = firsts(seg_t).astype(F32), lasts(seg_t).astype(F32)
+    for i in range(G):
+        g = lax.rem(2 * x + i, G)
+        out, at = outs[i // 2], i % 2
+        sh, sl = split2(of_half(core, g, smine, sgot))
+        hi, lo = dh_ref[g], dl_ref[g]
+        out[at] = gc_ref[g] + first * (dot_t(hi, sh) + dot_t(hi, sl) + dot_t(lo, sh))
+        scale = reverse_block(core, y, g, kept, sent, slice(N, ROWS))[ELAST - N : ELAST - N + 1]
+        ah, al = split2(of_half(core, g, amine, agot) * scale)
+        hi, lo = xh_ref[g], xl_ref[g]
+        out[2 + at] = gb_ref[g] + last * (dot_t(hi, ah) + dot_t(hi, al) + dot_t(lo, ah))
+
+
+def summed(*args):
+    return call(sum_kernel, args, [VMEM] * len(args), [sds(4, T, N)] * 4, [], "summed", 3000, 16, VMEM)
 
 
 def token_kernel(
-    n_parts, rate, seg_ref, dt_ref, qt_ref, xh_ref, xl_ref, dh_ref, dl_ref, b_ref, c_ref,
+    rate, seg_ref, dt_ref, qt_ref, xh_ref, xl_ref, dh_ref, dl_ref, b_ref, c_ref,
     smine, sgot, amine, agot, kept, sent, *refs,
 ):
-    raws, us = refs[:n_parts], refs[n_parts : 2 * n_parts]
     gi_ref, gs_ref, gi_s, v_s, u_s, k_s, dt_s, rate_s = refs[-8:]
     core, y, _ = place()
     for j in range(J):
@@ -460,22 +430,26 @@
     seg_row = seg_ref[...].astype(F32)
     seg_t = token_rows(seg_row)
     first, last = firsts(seg_t).astype(BF16), lasts(seg_t).astype(BF16)
+    low, high = lows(seg_t, seg_row).astype(F32), highs(seg_t, seg_row).astype(F32)
     ones = head_ones()
     for g in range(G):
+        xh, xl, dh, dl, b, c = [ref[g] for ref in (xh_ref, xl_ref, dh_ref, dl_ref, b_ref, c_ref)]
         state, adjoint = of_half(core, g, smine, sgot), of_half(core, g, amine, agot)
         reverse = reverse_block(core, y, g, kept, sent, slice(0, ROWS))
         crossing = state * (reverse[:N] + reverse[DEC : DEC + 1] * adjoint)
         k_s[g] = head_sums(ones, crossing)
         sh, sl = split2(state)
-        c = c_ref[g] * first
-        out = dot(c, sh) + dot(c, sl)
-        u_s[g] = piece(us, g)[...] + head_sums(ones, out * (dh_ref[g].astype(F32) + dl_ref[g].astype(F32)))
+        wh, wl = split2(dot_t(c, b) * low)
+        edge = c * first
+        out = dot(wh, xh) + dot(wh, xl) + dot(wl, xh) + dot(edge, sh) + dot(edge, sl)
+        u_s[g] = head_sums(ones, out * (dh.astype(F32) + dl.astype(F32)))
         ah, al = split2(adjoint * reverse[ELAST : ELAST + 1])
-        b = b_ref[g] * last
-        raw = piece(raws, g)[...] + dot(b, ah) + dot(b, al)
+        vh, vl = split2(dot_t(b, c) * high)
+        edge = b * last
+        raw = dot(vh, dh) + dot(vh, dl) + dot(vl, dh) + dot(edge, ah) + dot(edge, al)
         q = dot(qt_ref[...], expander(g))
         gi_s[g] = (q * raw).astype(BF16)
-        v_s[g] = head_sums(ones, raw * (xh_ref[g].astype(F32) + xl_ref[g].astype(F32)))
+        v_s[g] = head_sums(ones, raw * (xh.astype(F32) + xl.astype(F32)))
     gi_ref[...] = jnp.swapaxes(gi_s[...], 0, 1)
     v = jnp.concatenate([v_s[k][:J] for k in range(G)], axis=0)
     u = jnp.concatenate([u_s[k][:J] for k in range(G)], axis=0)
@@ -489,11 +463,11 @@
         gs_ref[k] = grad[J * k : J * k + J]
 
 
-def token_grads(args, raws, us, after):
-    args = (*args, *raws, *us, *after)
+def token_grads(args, after):
+    args = (*args, *after)
     heads = pltpu.VMEM((G, 8, T), F32)
     return call(
-        functools.partial(token_kernel, len(raws)),
+        token_kernel,
         args,
         [SMEM] + [VMEM] * (len(args) - 1 - len(after)) + [HBM] * len(after),
         [sds(T, G, W, dtype=BF16), sds(G, J, T)],
@@ -509,10 +483,6 @@
     return [along_x(parts[s], s) for s in (1, 2, 3)]
 
 
-def total(own, got):
-    return jnp.transpose(own + got[0] + got[1] + got[2], (1, 0, 2))
-
-
 def per_device(inputs, step_size, decay_rate, b_proj, c_proj, grad_out, segment_ids):
     seg = segment_ids.reshape(1, T)
     dt = jnp.transpose(step_size, (1, 2, 0))
@@ -523,33 +493,26 @@
     def spread_y(blocks):
         return [blocks[0]] + [along_y(blocks[s], s) for s in (1, 2, 3)]
 
-    def local(g0, count, *after):
-        return local_grads(g0, count, seg, data, after)
-
     fgot, rgot = swap(fs), swap(rs)
     fjoined = chip_join(fk, fgot, 0)
     rjoined = chip_join(rk, rgot, 1, (fjoined[0],))
-    held = [local(0, 3, rjoined[0])]
     fblocks, rblocks = spread_y(fjoined), spread_y(rjoined)
-    fplane = plane_join(fblocks, 0, (held[0][3],))
-    held.append(local(3, 2, fplane))
-    rplane = plane_join(rblocks, 1, (held[1][3],))
-    held.append(local(5, 3, rplane))
-    fenter = plane_enter(fblocks, along_z(fplane, 1), along_z(fplane, 2), 0, (held[2][3],))
+    fplane = plane_join(fblocks, 0)
+    rplane = plane_join(rblocks, 1, (fplane,))
+    gc, gb = local_grads(seg, data, (rplane,))
+    fenter = plane_enter(fblocks, along_z(fplane, 1), along_z(fplane, 2), 0, (gc,))
     renter = plane_enter(rblocks, along_z(rplane, -1), along_z(rplane, -2), 1, (fenter[0],))
-    gc, gb, raw, u = zip(*held)
     smine, fother = device_enter(spread_y(fenter), fk, fgot, 0)
     sgot = swap(fother)
-    parts_c = summed(False, seg, dh, dl, smine, sgot, (), gc, ())
-    got_c = over_heads(parts_c)
     amine, rother = device_enter(spread_y(renter), rk, rgot, 1, (smine,))
     agot = swap(rother)
-    parts_b = summed(True, seg, xh, xl, amine, agot, (rk, rs), gb, (parts_c[0],))
-    got_b = over_heads(parts_b)
+    parts = summed(seg, dh, dl, xh, xl, smine, sgot, amine, agot, rk, rs, gc, gb)
+    got = over_heads(parts)
     grad_in, grad_step = token_grads(
-        (rate, seg, dt, qt, xh, xl, dh, dl, b, c, smine, sgot, amine, agot, rk, rs), raw, u, (parts_b[0],)
-    )
-    total_c, total_b = total(parts_c[0], got_c), total(parts_b[0], got_b)
+        (rate, seg, dt, qt, xh, xl, dh, dl, b, c, smine, sgot, amine, agot, rk, rs), (parts[1],)
+    )
+    whole = parts[0] + got[0] + got[1] + got[2]
+    total_c, total_b = jnp.transpose(whole[:2], (1, 0, 2)), jnp.transpose(whole[2:], (1, 0, 2))
     return grad_in, jnp.transpose(grad_step, (2, 0, 1)), total_b, total_c
 
 

time: 95.7 us -> 89.5 us (0.935)
  waiting for transfers between devices: 18.1 us -> 24.4 us
  Pallas kernels: 28.1 us -> 23.5 us
  starting transfers between devices: 38.2 us -> 33.6 us
  local copies, waits for them, and re-layouts: 9.81 us -> 6.93 us
    ppermute x12, waiting for transfers between devices: 3.48 us -> 10.7 us  [along_y(): return lax.ppermute(v, Y, ring(4, shift))]
    pallas_call x15 -> x12, Pallas kernels: 28.1 us -> 23.5 us  [call(): pl.pallas_call(kernel, in_specs=specs, out_specs=[out_spec] * len(outs),...]
    ppermute x4, starting transfers between devices: 9.99 us -> 5.31 us  [swap(): return lax.ppermute(v, C, ring(2, 1))]
    ppermute x6 -> x3, starting transfers between devices: 7.33 us -> 4.3 us  [along_x(): return lax.ppermute(v, X, ring(4, shift))]
    unnamed x40 -> x36, local copies, waits for them, and re-layouts: 9.81 us -> 6.89 us
    ppermute x4, waiting for transfers between devices: 1.7 us -> 3.88 us  [swap(): return lax.ppermute(v, C, ring(2, 1))]
    ppermute x4, starting transfers between devices: 7.3 us -> 9.33 us  [along_z(): return lax.ppermute(v, Z, ring(8, shift))]
    ppermute x6 -> x3, waiting for transfers between devices: 11.5 us -> 9.78 us  [along_x(): return lax.ppermute(v, X, ring(4, shift))]
  transfers between devices with their start and end apart: 26 -> 23, of which waited for: 10 -> 12; matrix products, arithmetic and copies ran while one was open for 1% -> 0% of each run, Pallas kernels for 20% -> 17%
where the time goes in v3:
time: 89.5 us; the launch traced here: 89.2 us
  starting transfers between devices  33.6 us (38%)
  waiting for transfers between devices  24.4 us (27%)
  Pallas kernels  23.5 us (26%)
  local copies, waits for them, and re-layouts  6.93 us (8%)
    pallas_call x12, Pallas kernels, call(): pl.pallas_call(kernel, in_specs=specs, out_specs=[out_spec] * len(outs),...  23.5 us
    ppermute x12, starting transfers between devices, along_y(): return lax.ppermute(v, Y, ring(4, shift))  14.6 us
    ppermute x12, waiting for transfers between devices, along_y(): return lax.ppermute(v, Y, ring(4, shift))  10.7 us
    ppermute x3, waiting for transfers between devices, along_x(): return lax.ppermute(v, X, ring(4, shift))  9.78 us
    ppermute x4, starting transfers between devices, along_z(): return lax.ppermute(v, Z, ring(8, shift))  9.33 us
    unnamed x36, local copies, waits for them, and re-layouts  6.89 us
    ppermute x4, starting transfers between devices, swap(): return lax.ppermute(v, C, ring(2, 1))  5.31 us
    ppermute x3, starting transfers between devices, along_x(): return lax.ppermute(v, X, ring(4, shift))  4.3 us
  transfers between devices with their start and end apart: 23, of which 12 were waited for; matrix products, arithmetic and copies ran while one was open for 0% of the time, Pallas kernels for 17%

profile of v3, /device:TPU:1, one launch (start us, length us, event | category | flops | bytes accessed | tf_op | source)
XLA Modules:
  0.0 89.2 jit_solution(9267494550938821303)
XLA Ops:
  0.6 6.0 %summaries.1 = (bf16[8,256,256]{2,1,0:T(8,128)(2,1)}, bf16[8,256,256]{2,1,0:T(8,128)(2,1)}, bf16[8,256,256]{2,1,0:T(8,128)(2,1)}, bf16[8,256,256]{2,1,0:T(8,128)...) custom-call(f32[4,8]{1,0:T(4,128)} %bitcast.14, ...), custom_call_target="tpu_custom_call" | custom-call | flops 8000000 | bytes 1024 | tf_op jit(solution)/shard_map/summaries/pallas_call | solution.py:108
  6.6 3.3 %collective-permute-start = (f32[4,136,256]{2,1,0:T(8,128)}, f32[4,136,256]{2,1,0:T(8,128)S(1)}, u32[]{:S(2)}, u32[]{:S(2)}) collective-permute-start(f32[4,136,256]{2,1,0:T(8,128)} %get-tuple-element.51), channel_id=1, source_target_pairs={{0,4},{4,0},{1,5},{5,1},{2,6},{6,2},{3,7},{7,3},{8,12},{12,8},{9,1... | collective-permute-start | bytes 1671176 | tf_op jit(solution)/shard_map/ppermute | solution.py:373
  10.1 1.7 %collective-permute-done.refs_1_.refs_5_ = f32[4,136,256]{2,1,0:T(8,128)S(1)} collective-permute-done((f32[4,136,256]{2,1,0:T(8,128)}, f32[4,136,256]{2,1,0:T(8,128)S(1)}, u32[]{:S(2)}, u32[]{:S(2)}) %collective-permute-start) | collective-permute-done | bytes 557088 | tf_op jit(solution)/shard_map/ppermute | solution.py:373
  13.0 2.2 %collective-permute-start.2 = (f32[136,256]{1,0:T(8,128)S(1)}, f32[136,256]{1,0:T(8,128)S(1)}, u32[]{:S(2)}, u32[]{:S(2)}) collective-permute-start(f32[136,256]{1,0:T(8,128)S(1)} %get-tuple-element.54), channel_id=1, source_target_pairs={{0,16},{8,24},{16,0},{24,8},{1,17},{9,25},{17,1},{25,9},{2,18},{10... | collective-permute-start | bytes 417800 | tf_op jit(solution)/shard_map/ppermute | solution.py:377
  15.2 1.1 %collective-permute-start.3 = (f32[136,256]{1,0:T(8,128)S(1)}, f32[136,256]{1,0:T(8,128)S(1)}, u32[]{:S(2)}, u32[]{:S(2)}) collective-permute-start(f32[136,256]{1,0:T(8,128)S(1)} %get-tuple-element.55), channel_id=1, source_target_pairs={{0,24},{8,0},{16,8},{24,16},{1,25},{9,1},{17,9},{25,17},{2,26},{10... | collective-permute-start | bytes 417800 | tf_op jit(solution)/shard_map/ppermute | solution.py:377
  17.9 1.5 %collective-permute-start.8 = (f32[136,256]{1,0:T(8,128)S(1)}, f32[136,256]{1,0:T(8,128)S(1)}, u32[]{:S(2)}, u32[]{:S(2)}) collective-permute-start(f32[136,256]{1,0:T(8,128)S(1)} %get-tuple-element.60), channel_id=1, source_target_pairs={{0,16},{8,24},{16,0},{24,8},{1,17},{9,25},{17,1},{25,9},{2,18},{10... | collective-permute-start | bytes 417800 | tf_op jit(solution)/shard_map/ppermute | solution.py:377
  19.6 1.7 %collective-permute-start.9 = (f32[136,256]{1,0:T(8,128)S(1)}, f32[136,256]{1,0:T(8,128)S(1)}, u32[]{:S(2)}, u32[]{:S(2)}) collective-permute-start(f32[136,256]{1,0:T(8,128)S(1)} %get-tuple-element.61), channel_id=1, source_target_pairs={{0,24},{8,0},{16,8},{24,16},{1,25},{9,1},{17,9},{25,17},{2,26},{10... | collective-permute-start | bytes 417800 | tf_op jit(solution)/shard_map/ppermute | solution.py:377
  21.6 1.2 %collective-permute-done.3.refs_3_ = f32[136,256]{1,0:T(8,128)S(1)} collective-permute-done((f32[136,256]{1,0:T(8,128)S(1)}, f32[136,256]{1,0:T(8,128)S(1)}, u32[]{:S(2)}, u32[]{:S(2)}) %collective-permute-start.3) | collective-permute-done | bytes 139296 | tf_op jit(solution)/shard_map/ppermute | solution.py:377
  22.9 1.8 %collective-permute-start.5 = (f32[136,256]{1,0:T(8,128)S(1)}, f32[136,256]{1,0:T(8,128)S(1)}, u32[]{:S(2)}, u32[]{:S(2)}) collective-permute-start(f32[136,256]{1,0:T(8,128)S(1)} %plane_join.2.refs_4_), channel_id=1, source_target_pairs={{0,64},{32,96},{64,128},{96,160},{128,192},{160,224},{192,0},{224,... | collective-permute-start | bytes 417800 | tf_op jit(solution)/shard_map/ppermute | solution.py:381
  24.8 1.6 %collective-permute-start.4 = (f32[136,256]{1,0:T(8,128)S(1)}, f32[136,256]{1,0:T(8,128)S(1)}, u32[]{:S(2)}, u32[]{:S(2)}) collective-permute-start(f32[136,256]{1,0:T(8,128)S(1)} %plane_join.2.refs_4_), channel_id=1, source_target_pairs={{0,32},{32,64},{64,96},{96,128},{128,160},{160,192},{192,224},{224... | collective-permute-start | bytes 417800 | tf_op jit(solution)/shard_map/ppermute | solution.py:381
  26.4 2.1 %collective-permute-done.7.refs_1_ = f32[136,256]{1,0:T(8,128)S(1)} collective-permute-done((f32[136,256]{1,0:T(8,128)S(1)}, f32[136,256]{1,0:T(8,128)S(1)}, u32[]{:S(2)}, u32[]{:S(2)}) %collective-permute-start.7) | collective-permute-done | bytes 139296 | tf_op jit(solution)/shard_map/ppermute | solution.py:377
  28.6 5.1 %collective-permute-start.15 = (f32[136,256]{1,0:T(8,128)S(1)}, f32[136,256]{1,0:T(8,128)S(1)}, u32[]{:S(2)}, u32[]{:S(2)}) collective-permute-start(f32[136,256]{1,0:T(8,128)S(1)} %plane_join.3.refs_0_), channel_id=1, source_target_pairs={{0,192},{32,224},{64,0},{96,32},{128,64},{160,96},{192,128},{224,1... | collective-permute-start | bytes 417800 | tf_op jit(solution)/shard_map/ppermute | solution.py:381
  35.2 1.2 %copy-done.3 = bf16[8,256,256]{2,1,0:T(8,128)(2,1)S(1)} copy-done((bf16[8,256,256]{2,1,0:T(8,128)(2,1)S(1)}, bf16[8,256,256]{2,1,0:T(8,128)(2,1)}, u32[]{:S(2)}) %copy-start.3) | copy-done | bytes 1048600
  37.4 2.2 %local_grads.1 = (f32[8,256,128]{2,1,0:T(8,128)S(1)}, f32[8,256,128]{2,1,0:T(8,128)S(1)}) custom-call(s32[1,256]{1,0:T(1,128)S(1)} %bitcast.11, bf16[8,256,256]{2,1,0:T(8,128)(2,1)S(1)} %copy-done, bf16[8,256,256]{2,1,0:T(8,128)(2,1)S(1)} %copy-done.1, bf16[8,256,256]{2,1,0:T(8,128)(2,1)S(1)} %copy-done.2, bf16[8,256,256]{2,1,0:T(8,128)(2,1)S(1)} %copy-done.3, ...), custom_call_target="tpu_custom_call" | custom-call | flops 3000000 | bytes 1024 | tf_op jit(solution)/shard_map/local_grads/pallas_call | solution.py:108
  40.7 2.5 %collective-permute-start.11 = (f32[128,256]{1,0:T(8,128)S(1)}, f32[128,256]{1,0:T(8,128)S(1)}, u32[]{:S(2)}, u32[]{:S(2)}) collective-permute-start(f32[128,256]{1,0:T(8,128)S(1)} %get-tuple-element.65), channel_id=1, source_target_pairs={{0,16},{8,24},{16,0},{24,8},{1,17},{9,25},{17,1},{25,9},{2,18},{10... | collective-permute-start | bytes 393224 | tf_op jit(solution)/shard_map/ppermute | solution.py:377
  44.8 2.6 %collective-permute-start.17 = (f32[128,256]{1,0:T(8,128)S(1)}, f32[128,256]{1,0:T(8,128)S(1)}, u32[]{:S(2)}, u32[]{:S(2)}) collective-permute-start(f32[128,256]{1,0:T(8,128)S(1)} %get-tuple-element.71), channel_id=1, source_target_pairs={{0,16},{8,24},{16,0},{24,8},{1,17},{9,25},{17,1},{25,9},{2,18},{10... | collective-permute-start | bytes 393224 | tf_op jit(solution)/shard_map/ppermute | solution.py:377
  47.8 3.6 %collective-permute-done.16.refs_1_ = f32[128,256]{1,0:T(8,128)S(1)} collective-permute-done((f32[128,256]{1,0:T(8,128)S(1)}, f32[128,256]{1,0:T(8,128)S(1)}, u32[]{:S(2)}, u32[]{:S(2)}) %collective-permute-start.16) | collective-permute-done | bytes 131104 | tf_op jit(solution)/shard_map/ppermute | solution.py:377
  51.4 2.9 %collective-permute-done.17.refs_2_ = f32[128,256]{1,0:T(8,128)S(1)} collective-permute-done((f32[128,256]{1,0:T(8,128)S(1)}, f32[128,256]{1,0:T(8,128)S(1)}, u32[]{:S(2)}, u32[]{:S(2)}) %collective-permute-start.17) | collective-permute-done | bytes 131104 | tf_op jit(solution)/shard_map/ppermute | solution.py:377
  54.5 1.8 %collective-permute-start.19 = (f32[4,128,256]{2,1,0:T(8,128)S(1)}, f32[4,128,256]{2,1,0:T(8,128)S(1)}, u32[]{:S(2)}, u32[]{:S(2)}) collective-permute-start(f32[4,128,256]{2,1,0:T(8,128)S(1)} %get-tuple-element.74), channel_id=1, source_target_pairs={{0,4},{4,0},{1,5},{5,1},{2,6},{6,2},{3,7},{7,3},{8,12},{12,8},{9,1... | collective-permute-start | bytes 1572872 | tf_op jit(solution)/shard_map/ppermute | solution.py:373
  56.4 1.4 %collective-permute-done.19.agot = f32[4,128,256]{2,1,0:T(8,128)S(1)} collective-permute-done((f32[4,128,256]{2,1,0:T(8,128)S(1)}, f32[4,128,256]{2,1,0:T(8,128)S(1)}, u32[]{:S(2)}, u32[]{:S(2)}) %collective-permute-start.19) | collective-permute-done | bytes 524320 | tf_op jit(solution)/shard_map/ppermute | solution.py:373
  58.6 2.0 %summed.1 = (f32[4,256,128]{2,1,0:T(8,128)S(1)}, f32[4,256,128]{2,1,0:T(8,128)S(1)}, f32[4,256,128]{2,1,0:T(8,128)S(1)}, f32[4,256,128]{2,1,0:T(8,128)S(1)}) custom-call(s32[1,256]{1,0:T(1,128)S(1)} %bitcast.12, bf16[8,256,256]{2,1,0:T(8,128)(2,1)S(1)} %copy-done.2, bf16[8,256,256]{2,1,0:T(8,128)(2,1)S(1)} %copy-done.4, bf16[8,256,256]{2,1,0:T(8,128)(2,1)S(1)} %copy-done, ...), custom_call_target="tpu_custom_call" | custom-call | flops 3000000 | bytes 1024 | tf_op jit(solution)/shard_map/summed/pallas_call | solution.py:108
  60.6 2.8 %collective-permute-start.21 = (f32[4,256,128]{2,1,0:T(8,128)S(1)}, f32[4,256,128]{2,1,0:T(8,128)S(1)}, u32[]{:S(2)}, u32[]{:S(2)}) collective-permute-start(f32[4,256,128]{2,1,0:T(8,128)S(1)} %get-tuple-element.80), channel_id=1, source_target_pairs={{0,2},{1,3},{2,0},{3,1},{4,6},{5,7},{6,4},{7,5},{8,10},{9,11},{10,... | collective-permute-start | bytes 1572872 | tf_op jit(solution)/shard_map/ppermute | solution.py:385
  64.9 12.6 %token_grads.1 = (bf16[256,8,256]{2,1,0:T(8,128)(2,1)}, f32[8,4,256]{2,1,0:T(4,128)}) custom-call(f32[4,8]{1,0:T(4,128)S(1)} %bitcast.15, s32[1,256]{1,0:T(1,128)S(1)} %bitcast.13, f32[8,4,256]{2,1,0:T(4,128)S(1)} %bitcast.9, bf16[256,128]{1,0:T(8,128)(2,1)S(1)} %copy-done.14, bf16[8,256,256]{2,1,0:T(8,128)(2,1)S(1)} %copy-done, ...), custom_call_target="tpu_custom_call" | custom-call | flops 6000000 | bytes 1024 | tf_op jit(solution)/shard_map/token_grads/pallas_call | solution.py:108
  77.5 9.2 %collective-permute-done.22 = f32[4,256,128]{2,1,0:T(8,128)S(1)} collective-permute-done((f32[4,256,128]{2,1,0:T(8,128)S(1)}, f32[4,256,128]{2,1,0:T(8,128)S(1)}, u32[]{:S(2)}, u32[]{:S(2)}) %collective-permute-start.22) | collective-permute-done | bytes 524320 | tf_op jit(solution)/shard_map/ppermute | solution.py:385
  (72 shorter events, 14.1 us)
Async XLA Ops:
  6.6 5.1 %collective-permute-start = (f32[4,136,256]{2,1,0:T(8,128)}, f32[4,136,256]{2,1,0:T(8,128)S(1)}, u32[]{:S(2)}, u32[]{:S(2)}) collective-permute-start(f32[4,136,256]{2,1,0:T(8,128)} %get-tuple-element.51), channel_id=1, source_target_pairs={{0,4},{4,0},{1,5},{5,1},{2,6},{6,2},{3,7},{7,3},{8,12},{12,8},{9,1... | collective-permute-start | bytes 1671176 | tf_op jit(solution)/shard_map/ppermute | solution.py:373
  10.0 6.3 %collective-permute-start.6 = (f32[4,136,256]{2,1,0:T(8,128)}, f32[4,136,256]{2,1,0:T(8,128)S(1)}, u32[]{:S(2)}, u32[]{:S(2)}) collective-permute-start(f32[4,136,256]{2,1,0:T(8,128)} %get-tuple-element.57.sent), channel_id=1, source_target_pairs={{0,4},{4,0},{1,5},{5,1},{2,6},{6,2},{3,7},{7,3},{8,12},{12,8},{9,1... | collective-permute-start | bytes 1671176 | tf_op jit(solution)/shard_map/ppermute | solution.py:373
  12.8 21.7 %copy-start.2 = (bf16[8,256,256]{2,1,0:T(8,128)(2,1)S(1)}, bf16[8,256,256]{2,1,0:T(8,128)(2,1)}, u32[]{:S(2)}) copy-start(bf16[8,256,256]{2,1,0:T(8,128)(2,1)} %get-tuple-element.46.dh_ref) | copy-start | bytes 3145732
  12.9 6.7 %collective-permute-start.1 = (f32[136,256]{1,0:T(8,128)S(1)}, f32[136,256]{1,0:T(8,128)S(1)}, u32[]{:S(2)}, u32[]{:S(2)}) collective-permute-start(f32[136,256]{1,0:T(8,128)S(1)} %get-tuple-element.53), channel_id=1, source_target_pairs={{0,8},{8,16},{16,24},{24,0},{1,9},{9,17},{17,25},{25,1},{2,10},{10... | collective-permute-start | bytes 417800 | tf_op jit(solution)/shard_map/ppermute | solution.py:377
  13.0 8.6 %collective-permute-start.2 = (f32[136,256]{1,0:T(8,128)S(1)}, f32[136,256]{1,0:T(8,128)S(1)}, u32[]{:S(2)}, u32[]{:S(2)}) collective-permute-start(f32[136,256]{1,0:T(8,128)S(1)} %get-tuple-element.54), channel_id=1, source_target_pairs={{0,16},{8,24},{16,0},{24,8},{1,17},{9,25},{17,1},{25,9},{2,18},{10... | collective-permute-start | bytes 417800 | tf_op jit(solution)/shard_map/ppermute | solution.py:377
  15.2 7.7 %collective-permute-start.3 = (f32[136,256]{1,0:T(8,128)S(1)}, f32[136,256]{1,0:T(8,128)S(1)}, u32[]{:S(2)}, u32[]{:S(2)}) collective-permute-start(f32[136,256]{1,0:T(8,128)S(1)} %get-tuple-element.55), channel_id=1, source_target_pairs={{0,24},{8,0},{16,8},{24,16},{1,25},{9,1},{17,9},{25,17},{2,26},{10... | collective-permute-start | bytes 417800 | tf_op jit(solution)/shard_map/ppermute | solution.py:377
  17.4 11.1 %collective-permute-start.7 = (f32[136,256]{1,0:T(8,128)S(1)}, f32[136,256]{1,0:T(8,128)S(1)}, u32[]{:S(2)}, u32[]{:S(2)}) collective-permute-start(f32[136,256]{1,0:T(8,128)S(1)} %get-tuple-element.59), channel_id=1, source_target_pairs={{0,8},{8,16},{16,24},{24,0},{1,9},{9,17},{17,25},{25,1},{2,10},{10... | collective-permute-start | bytes 417800 | tf_op jit(solution)/shard_map/ppermute | solution.py:377
  17.9 10.7 %collective-permute-start.8 = (f32[136,256]{1,0:T(8,128)S(1)}, f32[136,256]{1,0:T(8,128)S(1)}, u32[]{:S(2)}, u32[]{:S(2)}) collective-permute-start(f32[136,256]{1,0:T(8,128)S(1)} %get-tuple-element.60), channel_id=1, source_target_pairs={{0,16},{8,24},{16,0},{24,8},{1,17},{9,25},{17,1},{25,9},{2,18},{10... | collective-permute-start | bytes 417800 | tf_op jit(solution)/shard_map/ppermute | solution.py:377
  19.6 8.9 %collective-permute-start.9 = (f32[136,256]{1,0:T(8,128)S(1)}, f32[136,256]{1,0:T(8,128)S(1)}, u32[]{:S(2)}, u32[]{:S(2)}) collective-permute-start(f32[136,256]{1,0:T(8,128)S(1)} %get-tuple-element.61), channel_id=1, source_target_pairs={{0,24},{8,0},{16,8},{24,16},{1,25},{9,1},{17,9},{25,17},{2,26},{10... | collective-permute-start | bytes 417800 | tf_op jit(solution)/shard_map/ppermute | solution.py:377
  22.9 16.7 %collective-permute-start.5 = (f32[136,256]{1,0:T(8,128)S(1)}, f32[136,256]{1,0:T(8,128)S(1)}, u32[]{:S(2)}, u32[]{:S(2)}) collective-permute-start(f32[136,256]{1,0:T(8,128)S(1)} %plane_join.2.refs_4_), channel_id=1, source_target_pairs={{0,64},{32,96},{64,128},{96,160},{128,192},{160,224},{192,0},{224,... | collective-permute-start | bytes 417800 | tf_op jit(solution)/shard_map/ppermute | solution.py:381
  24.8 14.9 %collective-permute-start.4 = (f32[136,256]{1,0:T(8,128)S(1)}, f32[136,256]{1,0:T(8,128)S(1)}, u32[]{:S(2)}, u32[]{:S(2)}) collective-permute-start(f32[136,256]{1,0:T(8,128)S(1)} %plane_join.2.refs_4_), channel_id=1, source_target_pairs={{0,32},{32,64},{64,96},{96,128},{128,160},{160,192},{192,224},{224... | collective-permute-start | bytes 417800 | tf_op jit(solution)/shard_map/ppermute | solution.py:381
  28.6 15.3 %collective-permute-start.15 = (f32[136,256]{1,0:T(8,128)S(1)}, f32[136,256]{1,0:T(8,128)S(1)}, u32[]{:S(2)}, u32[]{:S(2)}) collective-permute-start(f32[136,256]{1,0:T(8,128)S(1)} %plane_join.3.refs_0_), channel_id=1, source_target_pairs={{0,192},{32,224},{64,0},{96,32},{128,64},{160,96},{192,128},{224,1... | collective-permute-start | bytes 417800 | tf_op jit(solution)/shard_map/ppermute | solution.py:381
  33.7 10.2 %collective-permute-start.14 = (f32[136,256]{1,0:T(8,128)S(1)}, f32[136,256]{1,0:T(8,128)S(1)}, u32[]{:S(2)}, u32[]{:S(2)}) collective-permute-start(f32[136,256]{1,0:T(8,128)S(1)} %plane_join.3.refs_0_), channel_id=1, source_target_pairs={{0,224},{32,0},{64,32},{96,64},{128,96},{160,128},{192,160},{224,1... | collective-permute-start | bytes 417800 | tf_op jit(solution)/shard_map/ppermute | solution.py:381
  39.8 7.7 %collective-permute-start.10 = (f32[128,256]{1,0:T(8,128)S(1)}, f32[128,256]{1,0:T(8,128)S(1)}, u32[]{:S(2)}, u32[]{:S(2)}) collective-permute-start(f32[128,256]{1,0:T(8,128)S(1)} %get-tuple-element.64), channel_id=1, source_target_pairs={{0,8},{8,16},{16,24},{24,0},{1,9},{9,17},{17,25},{25,1},{2,10},{10... | collective-permute-start | bytes 393224 | tf_op jit(solution)/shard_map/ppermute | solution.py:377
  40.7 7.0 %collective-permute-start.11 = (f32[128,256]{1,0:T(8,128)S(1)}, f32[128,256]{1,0:T(8,128)S(1)}, u32[]{:S(2)}, u32[]{:S(2)}) collective-permute-start(f32[128,256]{1,0:T(8,128)S(1)} %get-tuple-element.65), channel_id=1, source_target_pairs={{0,16},{8,24},{16,0},{24,8},{1,17},{9,25},{17,1},{25,9},{2,18},{10... | collective-permute-start | bytes 393224 | tf_op jit(solution)/shard_map/ppermute | solution.py:377
  43.2 4.6 %collective-permute-start.12 = (f32[128,256]{1,0:T(8,128)S(1)}, f32[128,256]{1,0:T(8,128)S(1)}, u32[]{:S(2)}, u32[]{:S(2)}) collective-permute-start(f32[128,256]{1,0:T(8,128)S(1)} %get-tuple-element.66), channel_id=1, source_target_pairs={{0,24},{8,0},{16,8},{24,16},{1,25},{9,1},{17,9},{25,17},{2,26},{10... | collective-permute-start | bytes 393224 | tf_op jit(solution)/shard_map/ppermute | solution.py:377
  44.0 7.4 %collective-permute-start.16 = (f32[128,256]{1,0:T(8,128)S(1)}, f32[128,256]{1,0:T(8,128)S(1)}, u32[]{:S(2)}, u32[]{:S(2)}) collective-permute-start(f32[128,256]{1,0:T(8,128)S(1)} %get-tuple-element.70), channel_id=1, source_target_pairs={{0,8},{8,16},{16,24},{24,0},{1,9},{9,17},{17,25},{25,1},{2,10},{10... | collective-permute-start | bytes 393224 | tf_op jit(solution)/shard_map/ppermute | solution.py:377
  44.8 9.6 %collective-permute-start.17 = (f32[128,256]{1,0:T(8,128)S(1)}, f32[128,256]{1,0:T(8,128)S(1)}, u32[]{:S(2)}, u32[]{:S(2)}) collective-permute-start(f32[128,256]{1,0:T(8,128)S(1)} %get-tuple-element.71), channel_id=1, source_target_pairs={{0,16},{8,24},{16,0},{24,8},{1,17},{9,25},{17,1},{25,9},{2,18},{10... | collective-permute-start | bytes 393224 | tf_op jit(solution)/shard_map/ppermute | solution.py:377
  47.4 6.9 %collective-permute-start.18 = (f32[128,256]{1,0:T(8,128)S(1)}, f32[128,256]{1,0:T(8,128)S(1)}, u32[]{:S(2)}, u32[]{:S(2)}) collective-permute-start(f32[128,256]{1,0:T(8,128)S(1)} %get-tuple-element.72), channel_id=1, source_target_pairs={{0,24},{8,0},{16,8},{24,16},{1,25},{9,1},{17,9},{25,17},{2,26},{10... | collective-permute-start | bytes 393224 | tf_op jit(solution)/shard_map/ppermute | solution.py:377
  54.5 3.3 %collective-permute-start.19 = (f32[4,128,256]{2,1,0:T(8,128)S(1)}, f32[4,128,256]{2,1,0:T(8,128)S(1)}, u32[]{:S(2)}, u32[]{:S(2)}) collective-permute-start(f32[4,128,256]{2,1,0:T(8,128)S(1)} %get-tuple-element.74), channel_id=1, source_target_pairs={{0,4},{4,0},{1,5},{5,1},{2,6},{6,2},{3,7},{7,3},{8,12},{12,8},{9,1... | collective-permute-start | bytes 1572872 | tf_op jit(solution)/shard_map/ppermute | solution.py:373
  56.3 2.3 %collective-permute-start.13 = (f32[4,128,256]{2,1,0:T(8,128)S(1)}, f32[4,128,256]{2,1,0:T(8,128)S(1)}, u32[]{:S(2)}, u32[]{:S(2)}) collective-permute-start(f32[4,128,256]{2,1,0:T(8,128)S(1)} %get-tuple-element.68), channel_id=1, source_target_pairs={{0,4},{4,0},{1,5},{5,1},{2,6},{6,2},{3,7},{7,3},{8,12},{12,8},{9,1... | collective-permute-start | bytes 1572872 | tf_op jit(solution)/shard_map/ppermute | solution.py:373
  60.6 16.9 %collective-permute-start.21 = (f32[4,256,128]{2,1,0:T(8,128)S(1)}, f32[4,256,128]{2,1,0:T(8,128)S(1)}, u32[]{:S(2)}, u32[]{:S(2)}) collective-permute-start(f32[4,256,128]{2,1,0:T(8,128)S(1)} %get-tuple-element.80), channel_id=1, source_target_pairs={{0,2},{1,3},{2,0},{3,1},{4,6},{5,7},{6,4},{7,5},{8,10},{9,11},{10,... | collective-permute-start | bytes 1572872 | tf_op jit(solution)/shard_map/ppermute | solution.py:385
  63.4 23.3 %collective-permute-start.22 = (f32[4,256,128]{2,1,0:T(8,128)S(1)}, f32[4,256,128]{2,1,0:T(8,128)S(1)}, u32[]{:S(2)}, u32[]{:S(2)}) collective-permute-start(f32[4,256,128]{2,1,0:T(8,128)S(1)} %get-tuple-element.81), channel_id=1, source_target_pairs={{0,3},{1,0},{2,1},{3,2},{4,7},{5,4},{6,5},{7,6},{8,11},{9,8},{10,9... | collective-permute-start | bytes 1572872 | tf_op jit(solution)/shard_map/ppermute | solution.py:385
  64.3 23.0 %collective-permute-start.20 = (f32[4,256,128]{2,1,0:T(8,128)S(1)}, f32[4,256,128]{2,1,0:T(8,128)S(1)}, u32[]{:S(2)}, u32[]{:S(2)}) collective-permute-start(f32[4,256,128]{2,1,0:T(8,128)S(1)} %get-tuple-element.76.refs_0_), channel_id=1, source_target_pairs={{0,1},{1,2},{2,3},{3,0},{4,5},{5,6},{6,7},{7,4},{8,9},{9,10},{10,1... | collective-permute-start | bytes 1572872 | tf_op jit(solution)/shard_map/ppermute | solution.py:385
  (16 other events, 100.3 us)

commit v4 on v3

--- a/solution.py
+++ b/solution.py
@@ -483,6 +483,17 @@
     return [along_x(parts[s], s) for s in (1, 2, 3)]
 
 
+def finish(parts):
+    def body(*refs):
+        parts, outs = refs[:4], refs[4:]
+        for k in range(2):
+            own = slice(2 * k, 2 * k + 2)
+            whole = parts[0][own] + parts[1][own] + parts[2][own] + parts[3][own]
+            outs[k][...] = jnp.swapaxes(whole, 0, 1)
+
+    return call(body, parts, [VMEM] * 4, [sds(T, 2, N)] * 2, [], "finish", 1, 12, VMEM)
+
+
 def per_device(inputs, step_size, decay_rate, b_proj, c_proj, grad_out, segment_ids):
     seg = segment_ids.reshape(1, T)
     dt = jnp.transpose(step_size, (1, 2, 0))
@@ -499,20 +510,19 @@
     fblocks, rblocks = spread_y(fjoined), spread_y(rjoined)
     fplane = plane_join(fblocks, 0)
     rplane = plane_join(rblocks, 1, (fplane,))
-    gc, gb = local_grads(seg, data, (rplane,))
-    fenter = plane_enter(fblocks, along_z(fplane, 1), along_z(fplane, 2), 0, (gc,))
+    fenter = plane_enter(fblocks, along_z(fplane, 1), along_z(fplane, 2), 0)
     renter = plane_enter(rblocks, along_z(rplane, -1), along_z(rplane, -2), 1, (fenter[0],))
+    gc, gb = local_grads(seg, data, (renter[0],))
     smine, fother = device_enter(spread_y(fenter), fk, fgot, 0)
     sgot = swap(fother)
-    amine, rother = device_enter(spread_y(renter), rk, rgot, 1, (smine,))
+    amine, rother = device_enter(spread_y(renter), rk, rgot, 1, (smine, gc))
     agot = swap(rother)
     parts = summed(seg, dh, dl, xh, xl, smine, sgot, amine, agot, rk, rs, gc, gb)
     got = over_heads(parts)
     grad_in, grad_step = token_grads(
         (rate, seg, dt, qt, xh, xl, dh, dl, b, c, smine, sgot, amine, agot, rk, rs), (parts[1],)
     )
-    whole = parts[0] + got[0] + got[1] + got[2]
-    total_c, total_b = jnp.transpose(whole[:2], (1, 0, 2)), jnp.transpose(whole[2:], (1, 0, 2))
+    total_c, total_b = finish((parts[0], *got))
     return grad_in, jnp.transpose(grad_step, (2, 0, 1)), total_b, total_c
 
 

time: 89.5 us -> 85.6 us (0.956)
  local copies, waits for them, and re-layouts: 6.93 us -> 2.76 us
  waiting for transfers between devices: 24.4 us -> 23.5 us
    ppermute x12, waiting for transfers between devices: 10.7 us -> 5.97 us  [along_y(): return lax.ppermute(v, Y, ring(4, shift))]
    unnamed x36 -> x28, local copies, waits for them, and re-layouts: 6.89 us -> 2.76 us
    ppermute x4, waiting for transfers between devices: 0.01 us -> 3.63 us  [along_z(): return lax.ppermute(v, Z, ring(8, shift))]
    ppermute x4, starting transfers between devices: 5.31 us -> 6.68 us  [swap(): return lax.ppermute(v, C, ring(2, 1))]
    pallas_call x12 -> x13, Pallas kernels: 23.5 us -> 24.3 us  [call(): pl.pallas_call(kernel, in_specs=specs, out_specs=[out_spec] * len(outs),...]
  transfers between devices with their start and end apart: 23 -> 23, of which waited for: 12 -> 10; matrix products, arithmetic and copies ran while one was open for 0% -> 0% of each run, Pallas kernels for 17% -> 18%
where the time goes in v4:
time: 85.6 us; the launch traced here: 85.4 us
  starting transfers between devices  34.1 us (40%)
  Pallas kernels  24.3 us (28%)
  waiting for transfers between devices  23.5 us (27%)
  local copies, waits for them, and re-layouts  2.76 us (3%)
    pallas_call x13, Pallas kernels, call(): pl.pallas_call(kernel, in_specs=specs, out_specs=[out_spec] * len(outs),...  24.3 us
    ppermute x12, starting transfers between devices, along_y(): return lax.ppermute(v, Y, ring(4, shift))  14.7 us
    ppermute x3, waiting for transfers between devices, along_x(): return lax.ppermute(v, X, ring(4, shift))  10.6 us
    ppermute x4, starting transfers between devices, along_z(): return lax.ppermute(v, Z, ring(8, shift))  9.24 us
    ppermute x4, starting transfers between devices, swap(): return lax.ppermute(v, C, ring(2, 1))  6.68 us
    ppermute x12, waiting for transfers between devices, along_y(): return lax.ppermute(v, Y, ring(4, shift))  5.97 us
    ppermute x4, waiting for transfers between devices, along_z(): return lax.ppermute(v, Z, ring(8, shift))  3.63 us
    ppermute x3, starting transfers between devices, along_x(): return lax.ppermute(v, X, ring(4, shift))  3.49 us
  transfers between devices with their start and end apart: 23, of which 10 were waited for; matrix products, arithmetic and copies ran while one was open for 0% of the time, Pallas kernels for 18%

profile of v4, /device:TPU:1, one launch (start us, length us, event | category | flops | bytes accessed | tf_op | source)
XLA Modules:
  0.0 85.4 jit_solution(15210635495974201060)
XLA Ops:
  0.6 6.0 %summaries.1 = (bf16[8,256,256]{2,1,0:T(8,128)(2,1)}, bf16[8,256,256]{2,1,0:T(8,128)(2,1)}, bf16[8,256,256]{2,1,0:T(8,128)(2,1)}, bf16[8,256,256]{2,1,0:T(8,128)...) custom-call(f32[4,8]{1,0:T(4,128)} %bitcast.10, ...), custom_call_target="tpu_custom_call" | custom-call | flops 8000000 | bytes 1024 | tf_op jit(solution)/shard_map/summaries/pallas_call | solution.py:108
  6.6 3.3 %collective-permute-start = (f32[4,136,256]{2,1,0:T(8,128)}, f32[4,136,256]{2,1,0:T(8,128)S(1)}, u32[]{:S(2)}, u32[]{:S(2)}) collective-permute-start(f32[4,136,256]{2,1,0:T(8,128)} %get-tuple-element.53), channel_id=1, source_target_pairs={{0,4},{4,0},{1,5},{5,1},{2,6},{6,2},{3,7},{7,3},{8,12},{12,8},{9,1... | collective-permute-start | bytes 1671176 | tf_op jit(solution)/shard_map/ppermute | solution.py:373
  10.1 1.7 %collective-permute-done.refs_1_.refs_5_ = f32[4,136,256]{2,1,0:T(8,128)S(1)} collective-permute-done((f32[4,136,256]{2,1,0:T(8,128)}, f32[4,136,256]{2,1,0:T(8,128)S(1)}, u32[]{:S(2)}, u32[]{:S(2)}) %collective-permute-start) | collective-permute-done | bytes 557088 | tf_op jit(solution)/shard_map/ppermute | solution.py:373
  13.0 2.2 %collective-permute-start.2 = (f32[136,256]{1,0:T(8,128)S(1)}, f32[136,256]{1,0:T(8,128)S(1)}, u32[]{:S(2)}, u32[]{:S(2)}) collective-permute-start(f32[136,256]{1,0:T(8,128)S(1)} %get-tuple-element.56), channel_id=1, source_target_pairs={{0,16},{8,24},{16,0},{24,8},{1,17},{9,25},{17,1},{25,9},{2,18},{10... | collective-permute-start | bytes 417800 | tf_op jit(solution)/shard_map/ppermute | solution.py:377
  16.8 1.5 %collective-permute-start.12 = (f32[136,256]{1,0:T(8,128)S(1)}, f32[136,256]{1,0:T(8,128)S(1)}, u32[]{:S(2)}, u32[]{:S(2)}) collective-permute-start(f32[136,256]{1,0:T(8,128)S(1)} %get-tuple-element.68), channel_id=1, source_target_pairs={{0,16},{8,24},{16,0},{24,8},{1,17},{9,25},{17,1},{25,9},{2,18},{10... | collective-permute-start | bytes 417800 | tf_op jit(solution)/shard_map/ppermute | solution.py:377
  22.9 1.8 %collective-permute-start.5 = (f32[136,256]{1,0:T(8,128)S(1)}, f32[136,256]{1,0:T(8,128)S(1)}, u32[]{:S(2)}, u32[]{:S(2)}) collective-permute-start(f32[136,256]{1,0:T(8,128)S(1)} %plane_join.2.refs_4_), channel_id=1, source_target_pairs={{0,64},{32,96},{64,128},{96,160},{128,192},{160,224},{192,0},{224,... | collective-permute-start | bytes 417800 | tf_op jit(solution)/shard_map/ppermute | solution.py:381
  24.7 1.6 %collective-permute-start.4 = (f32[136,256]{1,0:T(8,128)S(1)}, f32[136,256]{1,0:T(8,128)S(1)}, u32[]{:S(2)}, u32[]{:S(2)}) collective-permute-start(f32[136,256]{1,0:T(8,128)S(1)} %plane_join.2.refs_4_), channel_id=1, source_target_pairs={{0,32},{32,64},{64,96},{96,128},{128,160},{160,192},{192,224},{224... | collective-permute-start | bytes 417800 | tf_op jit(solution)/shard_map/ppermute | solution.py:381
  26.3 2.2 %collective-permute-done.11.refs_1_ = f32[136,256]{1,0:T(8,128)S(1)} collective-permute-done((f32[136,256]{1,0:T(8,128)S(1)}, f32[136,256]{1,0:T(8,128)S(1)}, u32[]{:S(2)}, u32[]{:S(2)}) %collective-permute-start.11) | collective-permute-done | bytes 139296 | tf_op jit(solution)/shard_map/ppermute | solution.py:377
  28.6 5.1 %collective-permute-start.15 = (f32[136,256]{1,0:T(8,128)S(1)}, f32[136,256]{1,0:T(8,128)S(1)}, u32[]{:S(2)}, u32[]{:S(2)}) collective-permute-start(f32[136,256]{1,0:T(8,128)S(1)} %plane_join.3), channel_id=1, source_target_pairs={{0,192},{32,224},{64,0},{96,32},{128,64},{160,96},{192,128},{224,1... | collective-permute-start | bytes 417800 | tf_op jit(solution)/shard_map/ppermute | solution.py:381
  34.4 1.9 %collective-permute-done.4.refs_4_ = f32[136,256]{1,0:T(8,128)S(1)} collective-permute-done((f32[136,256]{1,0:T(8,128)S(1)}, f32[136,256]{1,0:T(8,128)S(1)}, u32[]{:S(2)}, u32[]{:S(2)}) %collective-permute-start.4) | collective-permute-done | bytes 139296 | tf_op jit(solution)/shard_map/ppermute | solution.py:381
  36.5 1.9 %collective-permute-start.7 = (f32[128,256]{1,0:T(8,128)S(1)}, f32[128,256]{1,0:T(8,128)S(1)}, u32[]{:S(2)}, u32[]{:S(2)}) collective-permute-start(f32[128,256]{1,0:T(8,128)S(1)} %get-tuple-element.60), channel_id=1, source_target_pairs={{0,16},{8,24},{16,0},{24,8},{1,17},{9,25},{17,1},{25,9},{2,18},{10... | collective-permute-start | bytes 393224 | tf_op jit(solution)/shard_map/ppermute | solution.py:377
  38.4 2.0 %collective-permute-start.8 = (f32[128,256]{1,0:T(8,128)S(1)}, f32[128,256]{1,0:T(8,128)S(1)}, u32[]{:S(2)}, u32[]{:S(2)}) collective-permute-start(f32[128,256]{1,0:T(8,128)S(1)} %get-tuple-element.61), channel_id=1, source_target_pairs={{0,24},{8,0},{16,8},{24,16},{1,25},{9,1},{17,9},{25,17},{2,26},{10... | collective-permute-start | bytes 393224 | tf_op jit(solution)/shard_map/ppermute | solution.py:377
  40.4 1.7 %collective-permute-done.14.refs_4_ = f32[136,256]{1,0:T(8,128)S(1)} collective-permute-done((f32[136,256]{1,0:T(8,128)S(1)}, f32[136,256]{1,0:T(8,128)S(1)}, u32[]{:S(2)}, u32[]{:S(2)}) %collective-permute-start.14) | collective-permute-done | bytes 139296 | tf_op jit(solution)/shard_map/ppermute | solution.py:381
  42.2 1.6 %collective-permute-start.16 = (f32[128,256]{1,0:T(8,128)S(1)}, f32[128,256]{1,0:T(8,128)S(1)}, u32[]{:S(2)}, u32[]{:S(2)}) collective-permute-start(f32[128,256]{1,0:T(8,128)S(1)} %get-tuple-element.71), channel_id=1, source_target_pairs={{0,8},{8,16},{16,24},{24,0},{1,9},{9,17},{17,25},{25,1},{2,10},{10... | collective-permute-start | bytes 393224 | tf_op jit(solution)/shard_map/ppermute | solution.py:377
  43.8 3.1 %collective-permute-start.17 = (f32[128,256]{1,0:T(8,128)S(1)}, f32[128,256]{1,0:T(8,128)S(1)}, u32[]{:S(2)}, u32[]{:S(2)}) collective-permute-start(f32[128,256]{1,0:T(8,128)S(1)} %get-tuple-element.72), channel_id=1, source_target_pairs={{0,16},{8,24},{16,0},{24,8},{1,17},{9,25},{17,1},{25,9},{2,18},{10... | collective-permute-start | bytes 393224 | tf_op jit(solution)/shard_map/ppermute | solution.py:377
  48.6 2.2 %local_grads.1 = (f32[8,256,128]{2,1,0:T(8,128)S(1)}, f32[8,256,128]{2,1,0:T(8,128)S(1)}) custom-call(s32[1,256]{1,0:T(1,128)S(1)} %bitcast.7, bf16[8,256,256]{2,1,0:T(8,128)(2,1)S(1)} %copy-done, bf16[8,256,256]{2,1,0:T(8,128)(2,1)S(1)} %copy-done.1, bf16[8,256,256]{2,1,0:T(8,128)(2,1)S(1)} %copy-done.2, bf16[8,256,256]{2,1,0:T(8,128)(2,1)S(1)} %copy-done.3, ...), custom_call_target="tpu_custom_call" | custom-call | flops 3000000 | bytes 1024 | tf_op jit(solution)/shard_map/local_grads/pallas_call | solution.py:108
  50.9 1.8 %collective-permute-start.9 = (f32[4,128,256]{2,1,0:T(8,128)S(1)}, f32[4,128,256]{2,1,0:T(8,128)S(1)}, u32[]{:S(2)}, u32[]{:S(2)}) collective-permute-start(f32[4,128,256]{2,1,0:T(8,128)S(1)} %get-tuple-element.63), channel_id=1, source_target_pairs={{0,4},{4,0},{1,5},{5,1},{2,6},{6,2},{3,7},{7,3},{8,12},{12,8},{9,1... | collective-permute-start | bytes 1572872 | tf_op jit(solution)/shard_map/ppermute | solution.py:373
  52.9 1.4 %collective-permute-start.19 = (f32[4,128,256]{2,1,0:T(8,128)S(1)}, f32[4,128,256]{2,1,0:T(8,128)S(1)}, u32[]{:S(2)}, u32[]{:S(2)}) collective-permute-start(f32[4,128,256]{2,1,0:T(8,128)S(1)} %get-tuple-element.76), channel_id=1, source_target_pairs={{0,4},{4,0},{1,5},{5,1},{2,6},{6,2},{3,7},{7,3},{8,12},{12,8},{9,1... | collective-permute-start | bytes 1572872 | tf_op jit(solution)/shard_map/ppermute | solution.py:373
  54.3 1.5 %collective-permute-done.19.agot = f32[4,128,256]{2,1,0:T(8,128)S(1)} collective-permute-done((f32[4,128,256]{2,1,0:T(8,128)S(1)}, f32[4,128,256]{2,1,0:T(8,128)S(1)}, u32[]{:S(2)}, u32[]{:S(2)}) %collective-permute-start.19) | collective-permute-done | bytes 524320 | tf_op jit(solution)/shard_map/ppermute | solution.py:373
  55.9 2.0 %summed.1 = (f32[4,256,128]{2,1,0:T(8,128)S(1)}, f32[4,256,128]{2,1,0:T(8,128)S(1)}, f32[4,256,128]{2,1,0:T(8,128)S(1)}, f32[4,256,128]{2,1,0:T(8,128)S(1)}) custom-call(s32[1,256]{1,0:T(1,128)S(1)} %bitcast.8, bf16[8,256,256]{2,1,0:T(8,128)(2,1)S(1)} %copy-done.2, bf16[8,256,256]{2,1,0:T(8,128)(2,1)S(1)} %copy-done.3, bf16[8,256,256]{2,1,0:T(8,128)(2,1)S(1)} %copy-done, ...), custom_call_target="tpu_custom_call" | custom-call | flops 3000000 | bytes 1024 | tf_op jit(solution)/shard_map/summed/pallas_call | solution.py:108
  57.8 2.0 %collective-permute-start.21 = (f32[4,256,128]{2,1,0:T(8,128)S(1)}, f32[4,256,128]{2,1,0:T(8,128)S(1)}, u32[]{:S(2)}, u32[]{:S(2)}) collective-permute-start(f32[4,256,128]{2,1,0:T(8,128)S(1)} %get-tuple-element.82), channel_id=1, source_target_pairs={{0,2},{1,3},{2,0},{3,1},{4,6},{5,7},{6,4},{7,5},{8,10},{9,11},{10,... | collective-permute-start | bytes 1572872 | tf_op jit(solution)/shard_map/ppermute | solution.py:385
  61.3 12.5 %token_grads.1 = (bf16[256,8,256]{2,1,0:T(8,128)(2,1)}, f32[8,4,256]{2,1,0:T(4,128)}) custom-call(f32[4,8]{1,0:T(4,128)S(1)} %bitcast.11, s32[1,256]{1,0:T(1,128)S(1)} %bitcast.9, f32[8,4,256]{2,1,0:T(4,128)S(1)} %bitcast.5, bf16[256,128]{1,0:T(8,128)(2,1)S(1)} %copy-done.11, bf16[8,256,256]{2,1,0:T(8,128)(2,1)S(1)} %copy-done, ...), custom_call_target="tpu_custom_call" | custom-call | flops 6000000 | bytes 1024 | tf_op jit(solution)/shard_map/token_grads/pallas_call | solution.py:108
  73.9 9.3 %collective-permute-done.22.refs_3_ = f32[4,256,128]{2,1,0:T(8,128)S(1)} collective-permute-done((f32[4,256,128]{2,1,0:T(8,128)S(1)}, f32[4,256,128]{2,1,0:T(8,128)S(1)}, u32[]{:S(2)}, u32[]{:S(2)}) %collective-permute-start.22) | collective-permute-done | bytes 524320 | tf_op jit(solution)/shard_map/ppermute | solution.py:385
  83.1 1.4 %collective-permute-done.20.refs_1_ = f32[4,256,128]{2,1,0:T(8,128)S(1)} collective-permute-done((f32[4,256,128]{2,1,0:T(8,128)S(1)}, f32[4,256,128]{2,1,0:T(8,128)S(1)}, u32[]{:S(2)}, u32[]{:S(2)}) %collective-permute-start.20) | collective-permute-done | bytes 524320 | tf_op jit(solution)/shard_map/ppermute | solution.py:385
  (63 shorter events, 13.0 us)
Async XLA Ops:
  6.6 5.1 %collective-permute-start = (f32[4,136,256]{2,1,0:T(8,128)}, f32[4,136,256]{2,1,0:T(8,128)S(1)}, u32[]{:S(2)}, u32[]{:S(2)}) collective-permute-start(f32[4,136,256]{2,1,0:T(8,128)} %get-tuple-element.53), channel_id=1, source_target_pairs={{0,4},{4,0},{1,5},{5,1},{2,6},{6,2},{3,7},{7,3},{8,12},{12,8},{9,1... | collective-permute-start | bytes 1671176 | tf_op jit(solution)/shard_map/ppermute | solution.py:373
  9.9 6.3 %collective-permute-start.10 = (f32[4,136,256]{2,1,0:T(8,128)}, f32[4,136,256]{2,1,0:T(8,128)S(1)}, u32[]{:S(2)}, u32[]{:S(2)}) collective-permute-start(f32[4,136,256]{2,1,0:T(8,128)} %get-tuple-element.65.sent), channel_id=1, source_target_pairs={{0,4},{4,0},{1,5},{5,1},{2,6},{6,2},{3,7},{7,3},{8,12},{12,8},{9,1... | collective-permute-start | bytes 1671176 | tf_op jit(solution)/shard_map/ppermute | solution.py:373
  12.8 34.1 %copy-start.8 = (bf16[8,256,128]{2,1,0:T(8,128)(2,1)S(1)}, bf16[8,256,128]{2,1,0:T(8,128)(2,1)}, u32[]{:S(2)}) copy-start(bf16[8,256,128]{2,1,0:T(8,128)(2,1)} %get-tuple-element.50.b_ref) | copy-start | bytes 1572868
  12.9 6.7 %collective-permute-start.1 = (f32[136,256]{1,0:T(8,128)S(1)}, f32[136,256]{1,0:T(8,128)S(1)}, u32[]{:S(2)}, u32[]{:S(2)}) collective-permute-start(f32[136,256]{1,0:T(8,128)S(1)} %get-tuple-element.55), channel_id=1, source_target_pairs={{0,8},{8,16},{16,24},{24,0},{1,9},{9,17},{17,25},{25,1},{2,10},{10... | collective-permute-start | bytes 417800 | tf_op jit(solution)/shard_map/ppermute | solution.py:377
  13.0 8.6 %collective-permute-start.2 = (f32[136,256]{1,0:T(8,128)S(1)}, f32[136,256]{1,0:T(8,128)S(1)}, u32[]{:S(2)}, u32[]{:S(2)}) collective-permute-start(f32[136,256]{1,0:T(8,128)S(1)} %get-tuple-element.56), channel_id=1, source_target_pairs={{0,16},{8,24},{16,0},{24,8},{1,17},{9,25},{17,1},{25,9},{2,18},{10... | collective-permute-start | bytes 417800 | tf_op jit(solution)/shard_map/ppermute | solution.py:377
  15.1 7.7 %collective-permute-start.3 = (f32[136,256]{1,0:T(8,128)S(1)}, f32[136,256]{1,0:T(8,128)S(1)}, u32[]{:S(2)}, u32[]{:S(2)}) collective-permute-start(f32[136,256]{1,0:T(8,128)S(1)} %get-tuple-element.57), channel_id=1, source_target_pairs={{0,24},{8,0},{16,8},{24,16},{1,25},{9,1},{17,9},{25,17},{2,26},{10... | collective-permute-start | bytes 417800 | tf_op jit(solution)/shard_map/ppermute | solution.py:377
  16.3 12.2 %collective-permute-start.11 = (f32[136,256]{1,0:T(8,128)S(1)}, f32[136,256]{1,0:T(8,128)S(1)}, u32[]{:S(2)}, u32[]{:S(2)}) collective-permute-start(f32[136,256]{1,0:T(8,128)S(1)} %get-tuple-element.67), channel_id=1, source_target_pairs={{0,8},{8,16},{16,24},{24,0},{1,9},{9,17},{17,25},{25,1},{2,10},{10... | collective-permute-start | bytes 417800 | tf_op jit(solution)/shard_map/ppermute | solution.py:377
  16.8 11.7 %collective-permute-start.12 = (f32[136,256]{1,0:T(8,128)S(1)}, f32[136,256]{1,0:T(8,128)S(1)}, u32[]{:S(2)}, u32[]{:S(2)}) collective-permute-start(f32[136,256]{1,0:T(8,128)S(1)} %get-tuple-element.68), channel_id=1, source_target_pairs={{0,16},{8,24},{16,0},{24,8},{1,17},{9,25},{17,1},{25,9},{2,18},{10... | collective-permute-start | bytes 417800 | tf_op jit(solution)/shard_map/ppermute | solution.py:377
  19.5 8.9 %collective-permute-start.13 = (f32[136,256]{1,0:T(8,128)S(1)}, f32[136,256]{1,0:T(8,128)S(1)}, u32[]{:S(2)}, u32[]{:S(2)}) collective-permute-start(f32[136,256]{1,0:T(8,128)S(1)} %get-tuple-element.69), channel_id=1, source_target_pairs={{0,24},{8,0},{16,8},{24,16},{1,25},{9,1},{17,9},{25,17},{2,26},{10... | collective-permute-start | bytes 417800 | tf_op jit(solution)/shard_map/ppermute | solution.py:377
  22.9 11.5 %collective-permute-start.5 = (f32[136,256]{1,0:T(8,128)S(1)}, f32[136,256]{1,0:T(8,128)S(1)}, u32[]{:S(2)}, u32[]{:S(2)}) collective-permute-start(f32[136,256]{1,0:T(8,128)S(1)} %plane_join.2.refs_4_), channel_id=1, source_target_pairs={{0,64},{32,96},{64,128},{96,160},{128,192},{160,224},{192,0},{224,... | collective-permute-start | bytes 417800 | tf_op jit(solution)/shard_map/ppermute | solution.py:381
  24.7 11.6 %collective-permute-start.4 = (f32[136,256]{1,0:T(8,128)S(1)}, f32[136,256]{1,0:T(8,128)S(1)}, u32[]{:S(2)}, u32[]{:S(2)}) collective-permute-start(f32[136,256]{1,0:T(8,128)S(1)} %plane_join.2.refs_4_), channel_id=1, source_target_pairs={{0,32},{32,64},{64,96},{96,128},{128,160},{160,192},{192,224},{224... | collective-permute-start | bytes 417800 | tf_op jit(solution)/shard_map/ppermute | solution.py:381
  28.6 11.8 %collective-permute-start.15 = (f32[136,256]{1,0:T(8,128)S(1)}, f32[136,256]{1,0:T(8,128)S(1)}, u32[]{:S(2)}, u32[]{:S(2)}) collective-permute-start(f32[136,256]{1,0:T(8,128)S(1)} %plane_join.3), channel_id=1, source_target_pairs={{0,192},{32,224},{64,0},{96,32},{128,64},{160,96},{192,128},{224,1... | collective-permute-start | bytes 417800 | tf_op jit(solution)/shard_map/ppermute | solution.py:381
  33.7 8.4 %collective-permute-start.14 = (f32[136,256]{1,0:T(8,128)S(1)}, f32[136,256]{1,0:T(8,128)S(1)}, u32[]{:S(2)}, u32[]{:S(2)}) collective-permute-start(f32[136,256]{1,0:T(8,128)S(1)} %plane_join.3), channel_id=1, source_target_pairs={{0,224},{32,0},{64,32},{96,64},{128,96},{160,128},{192,160},{224,1... | collective-permute-start | bytes 417800 | tf_op jit(solution)/shard_map/ppermute | solution.py:381
  36.4 10.5 %collective-permute-start.6 = (f32[128,256]{1,0:T(8,128)S(1)}, f32[128,256]{1,0:T(8,128)S(1)}, u32[]{:S(2)}, u32[]{:S(2)}) collective-permute-start(f32[128,256]{1,0:T(8,128)S(1)} %get-tuple-element.59), channel_id=1, source_target_pairs={{0,8},{8,16},{16,24},{24,0},{1,9},{9,17},{17,25},{25,1},{2,10},{10... | collective-permute-start | bytes 393224 | tf_op jit(solution)/shard_map/ppermute | solution.py:377
  36.5 14.2 %collective-permute-start.7 = (f32[128,256]{1,0:T(8,128)S(1)}, f32[128,256]{1,0:T(8,128)S(1)}, u32[]{:S(2)}, u32[]{:S(2)}) collective-permute-start(f32[128,256]{1,0:T(8,128)S(1)} %get-tuple-element.60), channel_id=1, source_target_pairs={{0,16},{8,24},{16,0},{24,8},{1,17},{9,25},{17,1},{25,9},{2,18},{10... | collective-permute-start | bytes 393224 | tf_op jit(solution)/shard_map/ppermute | solution.py:377
  38.4 12.4 %collective-permute-start.8 = (f32[128,256]{1,0:T(8,128)S(1)}, f32[128,256]{1,0:T(8,128)S(1)}, u32[]{:S(2)}, u32[]{:S(2)}) collective-permute-start(f32[128,256]{1,0:T(8,128)S(1)} %get-tuple-element.61), channel_id=1, source_target_pairs={{0,24},{8,0},{16,8},{24,16},{1,25},{9,1},{17,9},{25,17},{2,26},{10... | collective-permute-start | bytes 393224 | tf_op jit(solution)/shard_map/ppermute | solution.py:377
  42.2 10.6 %collective-permute-start.16 = (f32[128,256]{1,0:T(8,128)S(1)}, f32[128,256]{1,0:T(8,128)S(1)}, u32[]{:S(2)}, u32[]{:S(2)}) collective-permute-start(f32[128,256]{1,0:T(8,128)S(1)} %get-tuple-element.71), channel_id=1, source_target_pairs={{0,8},{8,16},{16,24},{24,0},{1,9},{9,17},{17,25},{25,1},{2,10},{10... | collective-permute-start | bytes 393224 | tf_op jit(solution)/shard_map/ppermute | solution.py:377
  43.8 9.0 %collective-permute-start.17 = (f32[128,256]{1,0:T(8,128)S(1)}, f32[128,256]{1,0:T(8,128)S(1)}, u32[]{:S(2)}, u32[]{:S(2)}) collective-permute-start(f32[128,256]{1,0:T(8,128)S(1)} %get-tuple-element.72), channel_id=1, source_target_pairs={{0,16},{8,24},{16,0},{24,8},{1,17},{9,25},{17,1},{25,9},{2,18},{10... | collective-permute-start | bytes 393224 | tf_op jit(solution)/shard_map/ppermute | solution.py:377
  46.9 5.9 %collective-permute-start.18 = (f32[128,256]{1,0:T(8,128)S(1)}, f32[128,256]{1,0:T(8,128)S(1)}, u32[]{:S(2)}, u32[]{:S(2)}) collective-permute-start(f32[128,256]{1,0:T(8,128)S(1)} %get-tuple-element.73), channel_id=1, source_target_pairs={{0,24},{8,0},{16,8},{24,16},{1,25},{9,1},{17,9},{25,17},{2,26},{10... | collective-permute-start | bytes 393224 | tf_op jit(solution)/shard_map/ppermute | solution.py:377
  50.9 3.4 %collective-permute-start.9 = (f32[4,128,256]{2,1,0:T(8,128)S(1)}, f32[4,128,256]{2,1,0:T(8,128)S(1)}, u32[]{:S(2)}, u32[]{:S(2)}) collective-permute-start(f32[4,128,256]{2,1,0:T(8,128)S(1)} %get-tuple-element.63), channel_id=1, source_target_pairs={{0,4},{4,0},{1,5},{5,1},{2,6},{6,2},{3,7},{7,3},{8,12},{12,8},{9,1... | collective-permute-start | bytes 1572872 | tf_op jit(solution)/shard_map/ppermute | solution.py:373
  52.9 3.0 %collective-permute-start.19 = (f32[4,128,256]{2,1,0:T(8,128)S(1)}, f32[4,128,256]{2,1,0:T(8,128)S(1)}, u32[]{:S(2)}, u32[]{:S(2)}) collective-permute-start(f32[4,128,256]{2,1,0:T(8,128)S(1)} %get-tuple-element.76), channel_id=1, source_target_pairs={{0,4},{4,0},{1,5},{5,1},{2,6},{6,2},{3,7},{7,3},{8,12},{12,8},{9,1... | collective-permute-start | bytes 1572872 | tf_op jit(solution)/shard_map/ppermute | solution.py:373
  57.8 16.0 %collective-permute-start.21 = (f32[4,256,128]{2,1,0:T(8,128)S(1)}, f32[4,256,128]{2,1,0:T(8,128)S(1)}, u32[]{:S(2)}, u32[]{:S(2)}) collective-permute-start(f32[4,256,128]{2,1,0:T(8,128)S(1)} %get-tuple-element.82), channel_id=1, source_target_pairs={{0,2},{1,3},{2,0},{3,1},{4,6},{5,7},{6,4},{7,5},{8,10},{9,11},{10,... | collective-permute-start | bytes 1572872 | tf_op jit(solution)/shard_map/ppermute | solution.py:385
  59.9 23.3 %collective-permute-start.22 = (f32[4,256,128]{2,1,0:T(8,128)S(1)}, f32[4,256,128]{2,1,0:T(8,128)S(1)}, u32[]{:S(2)}, u32[]{:S(2)}) collective-permute-start(f32[4,256,128]{2,1,0:T(8,128)S(1)} %get-tuple-element.83), channel_id=1, source_target_pairs={{0,3},{1,0},{2,1},{3,2},{4,7},{5,4},{6,5},{7,6},{8,11},{9,8},{10,9... | collective-permute-start | bytes 1572872 | tf_op jit(solution)/shard_map/ppermute | solution.py:385
  60.7 23.8 %collective-permute-start.20 = (f32[4,256,128]{2,1,0:T(8,128)S(1)}, f32[4,256,128]{2,1,0:T(8,128)S(1)}, u32[]{:S(2)}, u32[]{:S(2)}) collective-permute-start(f32[4,256,128]{2,1,0:T(8,128)S(1)} %get-tuple-element.78.refs_0_), channel_id=1, source_target_pairs={{0,1},{1,2},{2,3},{3,0},{4,5},{5,6},{6,7},{7,4},{8,9},{9,10},{10,1... | collective-permute-start | bytes 1572872 | tf_op jit(solution)/shard_map/ppermute | solution.py:385
  (13 other events, 115.5 us)

commit v5 on v3

--- a/solution.py
+++ b/solution.py
@@ -402,18 +402,18 @@
     first, last = firsts(seg_t).astype(F32), lasts(seg_t).astype(F32)
     for i in range(G):
         g = lax.rem(2 * x + i, G)
-        out, at = outs[i // 2], i % 2
+        out_c, out_b, at = outs[i // 2], outs[4 + i // 2], i % 2
         sh, sl = split2(of_half(core, g, smine, sgot))
         hi, lo = dh_ref[g], dl_ref[g]
-        out[at] = gc_ref[g] + first * (dot_t(hi, sh) + dot_t(hi, sl) + dot_t(lo, sh))
+        out_c[at] = gc_ref[g] + first * (dot_t(hi, sh) + dot_t(hi, sl) + dot_t(lo, sh))
         scale = reverse_block(core, y, g, kept, sent, slice(N, ROWS))[ELAST - N : ELAST - N + 1]
         ah, al = split2(of_half(core, g, amine, agot) * scale)
         hi, lo = xh_ref[g], xl_ref[g]
-        out[2 + at] = gb_ref[g] + last * (dot_t(hi, ah) + dot_t(hi, al) + dot_t(lo, ah))
+        out_b[at] = gb_ref[g] + last * (dot_t(hi, ah) + dot_t(hi, al) + dot_t(lo, ah))
 
 
 def summed(*args):
-    return call(sum_kernel, args, [VMEM] * len(args), [sds(4, T, N)] * 4, [], "summed", 3000, 16, VMEM)
+    return call(sum_kernel, args, [VMEM] * len(args), [sds(2, T, N)] * 8, [], "summed", 3000, 16, VMEM)
 
 
 def token_kernel(
@@ -479,8 +479,24 @@
     )
 
 
-def over_heads(parts):
-    return [along_x(parts[s], s) for s in (1, 2, 3)]
+def finish(own_c, own_b, *more):
+    def body(*refs):
+        for k in range(2):
+            whole = refs[k][...] + refs[2 + k][...] + refs[4 + k][...]
+            refs[6 + k][...] = jnp.swapaxes(whole, 0, 1)
+
+    args = (own_c, own_b, *more)
+    return call(body, args, [VMEM] * 6, [sds(T, 2, N)] * 2, [], "finish", 1, 12, VMEM)
+
+
+def add_passed(one, one_got, two, two_got, after):
+    def body(one, one_got, two, two_got, *refs):
+        refs[-2][...] = one[...] + one_got[...]
+        refs[-1][...] = two[...] + two_got[...]
+
+    specs = [VMEM] * 4 + [HBM] * len(after)
+    args = (one, one_got, two, two_got, *after)
+    return call(body, args, specs, [sds(2, T, N)] * 2, [], "add_passed", 1, 12, VMEM)
 
 
 def per_device(inputs, step_size, decay_rate, b_proj, c_proj, grad_out, segment_ids):
@@ -499,20 +515,23 @@
     fblocks, rblocks = spread_y(fjoined), spread_y(rjoined)
     fplane = plane_join(fblocks, 0)
     rplane = plane_join(rblocks, 1, (fplane,))
-    gc, gb = local_grads(seg, data, (rplane,))
-    fenter = plane_enter(fblocks, along_z(fplane, 1), along_z(fplane, 2), 0, (gc,))
+    fenter = plane_enter(fblocks, along_z(fplane, 1), along_z(fplane, 2), 0)
     renter = plane_enter(rblocks, along_z(rplane, -1), along_z(rplane, -2), 1, (fenter[0],))
+    gc, gb = local_grads(seg, data, (renter[0],))
     smine, fother = device_enter(spread_y(fenter), fk, fgot, 0)
     sgot = swap(fother)
-    amine, rother = device_enter(spread_y(renter), rk, rgot, 1, (smine,))
+    amine, rother = device_enter(spread_y(renter), rk, rgot, 1, (smine, gc))
     agot = swap(rother)
     parts = summed(seg, dh, dl, xh, xl, smine, sgot, amine, agot, rk, rs, gc, gb)
-    got = over_heads(parts)
+    cs, bs = parts[:4], parts[4:]
+    c_passed, b_passed = along_x(cs[2], 1), along_x(bs[2], 3)
+    b_before, c_behind = along_x(bs[1], 1), along_x(cs[3], 3)
     grad_in, grad_step = token_grads(
         (rate, seg, dt, qt, xh, xl, dh, dl, b, c, smine, sgot, amine, agot, rk, rs), (parts[1],)
     )
-    whole = parts[0] + got[0] + got[1] + got[2]
-    total_c, total_b = jnp.transpose(whole[:2], (1, 0, 2)), jnp.transpose(whole[2:], (1, 0, 2))
+    c_sent, b_sent = add_passed(cs[1], c_passed, bs[3], b_passed, (grad_step,))
+    c_before, b_behind = along_x(c_sent, 1), along_x(b_sent, 3)
+    total_c, total_b = finish(cs[0], bs[0], c_before, b_before, c_behind, b_behind)
     return grad_in, jnp.transpose(grad_step, (2, 0, 1)), total_b, total_c
 
 

time: 89.5 us -> 86.5 us (0.966); the launches traced: 89.2 us -> 85.1 us
  waiting for transfers between devices: 24.4 us -> 17.7 us
  starting transfers between devices: 33.6 us -> 38.8 us
  local copies, waits for them, and re-layouts: 6.93 us -> 3.52 us
    ppermute x3 -> x6, waiting for transfers between devices: 9.78 us -> 4.84 us  [along_x(): return lax.ppermute(v, X, ring(4, shift))]
    ppermute x12, waiting for transfers between devices: 10.7 us -> 5.97 us  [along_y(): return lax.ppermute(v, Y, ring(4, shift))]
    ppermute x3 -> x6, starting transfers between devices: 4.3 us -> 8.18 us  [along_x(): return lax.ppermute(v, X, ring(4, shift))]
    ppermute x4, waiting for transfers between devices: 0.01 us -> 3.63 us  [along_z(): return lax.ppermute(v, Z, ring(8, shift))]
    unnamed x36 -> x30, local copies, waits for them, and re-layouts: 6.89 us -> 3.52 us
    ppermute x4, starting transfers between devices: 5.31 us -> 6.68 us  [swap(): return lax.ppermute(v, C, ring(2, 1))]
    pallas_call x12 -> x14, Pallas kernels: 23.5 us -> 24.3 us  [call(): pl.pallas_call(kernel, in_specs=specs, out_specs=[out_spec] * len(outs),...]
  transfers between devices with their start and end apart: 23 -> 26, of which waited for: 12 -> 9; matrix products, arithmetic and copies ran while one was open for 0% -> 0% of each run, Pallas kernels for 17% -> 18%
where the time goes in v5:
time: 86.5 us; the launch traced here: 85.1 us
  starting transfers between devices  38.8 us (45%)
  Pallas kernels  24.3 us (28%)
  waiting for transfers between devices  17.7 us (20%)
  local copies, waits for them, and re-layouts  3.52 us (4%)
    pallas_call x14, Pallas kernels, call(): pl.pallas_call(kernel, in_specs=specs, out_specs=[out_spec] * len(outs),...  24.3 us
    ppermute x12, starting transfers between devices, along_y(): return lax.ppermute(v, Y, ring(4, shift))  14.7 us
    ppermute x4, starting transfers between devices, along_z(): return lax.ppermute(v, Z, ring(8, shift))  9.24 us
    ppermute x6, starting transfers between devices, along_x(): return lax.ppermute(v, X, ring(4, shift))  8.18 us
    ppermute x4, starting transfers between devices, swap(): return lax.ppermute(v, C, ring(2, 1))  6.68 us
    ppermute x12, waiting for transfers between devices, along_y(): return lax.ppermute(v, Y, ring(4, shift))  5.97 us
    ppermute x6, waiting for transfers between devices, along_x(): return lax.ppermute(v, X, ring(4, shift))  4.84 us
    ppermute x4, waiting for transfers between devices, along_z(): return lax.ppermute(v, Z, ring(8, shift))  3.63 us
  transfers between devices with their start and end apart: 26, of which 9 were waited for; matrix products, arithmetic and copies ran while one was open for 0% of the time, Pallas kernels for 18%

profile of v5, /device:TPU:1, one launch (start us, length us, event | category | flops | bytes accessed | tf_op | source)
XLA Modules:
  0.0 85.1 jit_solution(985659834564781533)
XLA Ops:
  0.6 6.0 %summaries.1 = (bf16[8,256,256]{2,1,0:T(8,128)(2,1)}, bf16[8,256,256]{2,1,0:T(8,128)(2,1)}, bf16[8,256,256]{2,1,0:T(8,128)(2,1)}, bf16[8,256,256]{2,1,0:T(8,128)...) custom-call(f32[4,8]{1,0:T(4,128)} %bitcast.11, ...), custom_call_target="tpu_custom_call" | custom-call | flops 8000000 | bytes 1024 | tf_op jit(solution)/shard_map/summaries/pallas_call | solution.py:108
  6.6 3.3 %collective-permute-start = (f32[4,136,256]{2,1,0:T(8,128)}, f32[4,136,256]{2,1,0:T(8,128)S(1)}, u32[]{:S(2)}, u32[]{:S(2)}) collective-permute-start(f32[4,136,256]{2,1,0:T(8,128)} %get-tuple-element.59), channel_id=1, source_target_pairs={{0,4},{4,0},{1,5},{5,1},{2,6},{6,2},{3,7},{7,3},{8,12},{12,8},{9,1... | collective-permute-start | bytes 1671176 | tf_op jit(solution)/shard_map/ppermute | solution.py:373
  10.1 1.7 %collective-permute-done.refs_1_.refs_5_ = f32[4,136,256]{2,1,0:T(8,128)S(1)} collective-permute-done((f32[4,136,256]{2,1,0:T(8,128)}, f32[4,136,256]{2,1,0:T(8,128)S(1)}, u32[]{:S(2)}, u32[]{:S(2)}) %collective-permute-start) | collective-permute-done | bytes 557088 | tf_op jit(solution)/shard_map/ppermute | solution.py:373
  13.0 2.2 %collective-permute-start.2 = (f32[136,256]{1,0:T(8,128)S(1)}, f32[136,256]{1,0:T(8,128)S(1)}, u32[]{:S(2)}, u32[]{:S(2)}) collective-permute-start(f32[136,256]{1,0:T(8,128)S(1)} %get-tuple-element.62), channel_id=1, source_target_pairs={{0,16},{8,24},{16,0},{24,8},{1,17},{9,25},{17,1},{25,9},{2,18},{10... | collective-permute-start | bytes 417800 | tf_op jit(solution)/shard_map/ppermute | solution.py:377
  16.8 1.5 %collective-permute-start.12 = (f32[136,256]{1,0:T(8,128)S(1)}, f32[136,256]{1,0:T(8,128)S(1)}, u32[]{:S(2)}, u32[]{:S(2)}) collective-permute-start(f32[136,256]{1,0:T(8,128)S(1)} %get-tuple-element.74), channel_id=1, source_target_pairs={{0,16},{8,24},{16,0},{24,8},{1,17},{9,25},{17,1},{25,9},{2,18},{10... | collective-permute-start | bytes 417800 | tf_op jit(solution)/shard_map/ppermute | solution.py:377
  22.9 1.8 %collective-permute-start.5 = (f32[136,256]{1,0:T(8,128)S(1)}, f32[136,256]{1,0:T(8,128)S(1)}, u32[]{:S(2)}, u32[]{:S(2)}) collective-permute-start(f32[136,256]{1,0:T(8,128)S(1)} %plane_join.2.refs_4_), channel_id=1, source_target_pairs={{0,64},{32,96},{64,128},{96,160},{128,192},{160,224},{192,0},{224,... | collective-permute-start | bytes 417800 | tf_op jit(solution)/shard_map/ppermute | solution.py:381
  24.7 1.6 %collective-permute-start.4 = (f32[136,256]{1,0:T(8,128)S(1)}, f32[136,256]{1,0:T(8,128)S(1)}, u32[]{:S(2)}, u32[]{:S(2)}) collective-permute-start(f32[136,256]{1,0:T(8,128)S(1)} %plane_join.2.refs_4_), channel_id=1, source_target_pairs={{0,32},{32,64},{64,96},{96,128},{128,160},{160,192},{192,224},{224... | collective-permute-start | bytes 417800 | tf_op jit(solution)/shard_map/ppermute | solution.py:381
  26.3 2.2 %collective-permute-done.11.refs_1_ = f32[136,256]{1,0:T(8,128)S(1)} collective-permute-done((f32[136,256]{1,0:T(8,128)S(1)}, f32[136,256]{1,0:T(8,128)S(1)}, u32[]{:S(2)}, u32[]{:S(2)}) %collective-permute-start.11) | collective-permute-done | bytes 139296 | tf_op jit(solution)/shard_map/ppermute | solution.py:377
  28.6 5.1 %collective-permute-start.15 = (f32[136,256]{1,0:T(8,128)S(1)}, f32[136,256]{1,0:T(8,128)S(1)}, u32[]{:S(2)}, u32[]{:S(2)}) collective-permute-start(f32[136,256]{1,0:T(8,128)S(1)} %plane_join.3), channel_id=1, source_target_pairs={{0,192},{32,224},{64,0},{96,32},{128,64},{160,96},{192,128},{224,1... | collective-permute-start | bytes 417800 | tf_op jit(solution)/shard_map/ppermute | solution.py:381
  34.4 1.9 %collective-permute-done.4.refs_4_ = f32[136,256]{1,0:T(8,128)S(1)} collective-permute-done((f32[136,256]{1,0:T(8,128)S(1)}, f32[136,256]{1,0:T(8,128)S(1)}, u32[]{:S(2)}, u32[]{:S(2)}) %collective-permute-start.4) | collective-permute-done | bytes 139296 | tf_op jit(solution)/shard_map/ppermute | solution.py:381
  36.6 1.9 %collective-permute-start.7 = (f32[128,256]{1,0:T(8,128)S(1)}, f32[128,256]{1,0:T(8,128)S(1)}, u32[]{:S(2)}, u32[]{:S(2)}) collective-permute-start(f32[128,256]{1,0:T(8,128)S(1)} %get-tuple-element.66), channel_id=1, source_target_pairs={{0,16},{8,24},{16,0},{24,8},{1,17},{9,25},{17,1},{25,9},{2,18},{10... | collective-permute-start | bytes 393224 | tf_op jit(solution)/shard_map/ppermute | solution.py:377
  38.4 2.0 %collective-permute-start.8 = (f32[128,256]{1,0:T(8,128)S(1)}, f32[128,256]{1,0:T(8,128)S(1)}, u32[]{:S(2)}, u32[]{:S(2)}) collective-permute-start(f32[128,256]{1,0:T(8,128)S(1)} %get-tuple-element.67), channel_id=1, source_target_pairs={{0,24},{8,0},{16,8},{24,16},{1,25},{9,1},{17,9},{25,17},{2,26},{10... | collective-permute-start | bytes 393224 | tf_op jit(solution)/shard_map/ppermute | solution.py:377
  40.4 1.7 %collective-permute-done.14.refs_4_ = f32[136,256]{1,0:T(8,128)S(1)} collective-permute-done((f32[136,256]{1,0:T(8,128)S(1)}, f32[136,256]{1,0:T(8,128)S(1)}, u32[]{:S(2)}, u32[]{:S(2)}) %collective-permute-start.14) | collective-permute-done | bytes 139296 | tf_op jit(solution)/shard_map/ppermute | solution.py:381
  42.2 1.6 %collective-permute-start.16 = (f32[128,256]{1,0:T(8,128)S(1)}, f32[128,256]{1,0:T(8,128)S(1)}, u32[]{:S(2)}, u32[]{:S(2)}) collective-permute-start(f32[128,256]{1,0:T(8,128)S(1)} %get-tuple-element.77), channel_id=1, source_target_pairs={{0,8},{8,16},{16,24},{24,0},{1,9},{9,17},{17,25},{25,1},{2,10},{10... | collective-permute-start | bytes 393224 | tf_op jit(solution)/shard_map/ppermute | solution.py:377
  43.8 3.1 %collective-permute-start.17 = (f32[128,256]{1,0:T(8,128)S(1)}, f32[128,256]{1,0:T(8,128)S(1)}, u32[]{:S(2)}, u32[]{:S(2)}) collective-permute-start(f32[128,256]{1,0:T(8,128)S(1)} %get-tuple-element.78), channel_id=1, source_target_pairs={{0,16},{8,24},{16,0},{24,8},{1,17},{9,25},{17,1},{25,9},{2,18},{10... | collective-permute-start | bytes 393224 | tf_op jit(solution)/shard_map/ppermute | solution.py:377
  48.6 2.2 %local_grads.1 = (f32[8,256,128]{2,1,0:T(8,128)S(1)}, f32[8,256,128]{2,1,0:T(8,128)S(1)}) custom-call(s32[1,256]{1,0:T(1,128)S(1)} %bitcast.8, bf16[8,256,256]{2,1,0:T(8,128)(2,1)S(1)} %copy-done, bf16[8,256,256]{2,1,0:T(8,128)(2,1)S(1)} %copy-done.1, bf16[8,256,256]{2,1,0:T(8,128)(2,1)S(1)} %copy-done.2, bf16[8,256,256]{2,1,0:T(8,128)(2,1)S(1)} %copy-done.3, ...), custom_call_target="tpu_custom_call" | custom-call | flops 3000000 | bytes 1024 | tf_op jit(solution)/shard_map/local_grads/pallas_call | solution.py:108
  50.9 1.8 %collective-permute-start.9 = (f32[4,128,256]{2,1,0:T(8,128)S(1)}, f32[4,128,256]{2,1,0:T(8,128)S(1)}, u32[]{:S(2)}, u32[]{:S(2)}) collective-permute-start(f32[4,128,256]{2,1,0:T(8,128)S(1)} %get-tuple-element.69), channel_id=1, source_target_pairs={{0,4},{4,0},{1,5},{5,1},{2,6},{6,2},{3,7},{7,3},{8,12},{12,8},{9,1... | collective-permute-start | bytes 1572872 | tf_op jit(solution)/shard_map/ppermute | solution.py:373
  54.3 1.5 %collective-permute-done.19.agot = f32[4,128,256]{2,1,0:T(8,128)S(1)} collective-permute-done((f32[4,128,256]{2,1,0:T(8,128)S(1)}, f32[4,128,256]{2,1,0:T(8,128)S(1)}, u32[]{:S(2)}, u32[]{:S(2)}) %collective-permute-start.19) | collective-permute-done | bytes 524320 | tf_op jit(solution)/shard_map/ppermute | solution.py:373
  55.9 2.0 %summed.1 = (f32[2,256,128]{2,1,0:T(8,128)S(1)}, f32[2,256,128]{2,1,0:T(8,128)S(1)}, f32[2,256,128]{2,1,0:T(8,128)S(1)}, f32[2,256,128]{2,1,0:T(8,128)S(1)}, f32...) custom-call(s32[1,256]{1,0:T(1,128)S(1)} %bitcast.9, ...), custom_call_target="tpu_custom_call" | custom-call | flops 3000000 | bytes 1024 | tf_op jit(solution)/shard_map/summed/pallas_call | solution.py:108
  58.3 2.3 %collective-permute-start.21 = (f32[2,256,128]{2,1,0:T(8,128)S(1)}, f32[2,256,128]{2,1,0:T(8,128)S(1)}, u32[]{:S(2)}, u32[]{:S(2)}) collective-permute-start(f32[2,256,128]{2,1,0:T(8,128)S(1)} %get-tuple-element.91), channel_id=1, source_target_pairs={{0,3},{1,0},{2,1},{3,2},{4,7},{5,4},{6,5},{7,6},{8,11},{9,8},{10,9... | collective-permute-start | bytes 786440 | tf_op jit(solution)/shard_map/ppermute | solution.py:385
  60.6 2.7 %collective-permute-start.24 = (f32[2,256,128]{2,1,0:T(8,128)S(1)}, f32[2,256,128]{2,1,0:T(8,128)S(1)}, u32[]{:S(2)}, u32[]{:S(2)}) collective-permute-start(f32[2,256,128]{2,1,0:T(8,128)S(1)} %get-tuple-element.94), channel_id=1, source_target_pairs={{0,3},{1,0},{2,1},{3,2},{4,7},{5,4},{6,5},{7,6},{8,11},{9,8},{10,9... | collective-permute-start | bytes 786440 | tf_op jit(solution)/shard_map/ppermute | solution.py:385
  63.3 12.5 %token_grads.1 = (bf16[256,8,256]{2,1,0:T(8,128)(2,1)}, f32[8,4,256]{2,1,0:T(4,128)}) custom-call(f32[4,8]{1,0:T(4,128)S(1)} %bitcast.12, s32[1,256]{1,0:T(1,128)S(1)} %bitcast.10, f32[8,4,256]{2,1,0:T(4,128)S(1)} %bitcast.5, bf16[256,128]{1,0:T(8,128)(2,1)S(1)} %copy-done.11, bf16[8,256,256]{2,1,0:T(8,128)(2,1)S(1)} %copy-done, ...), custom_call_target="tpu_custom_call" | custom-call | flops 6000000 | bytes 1024 | tf_op jit(solution)/shard_map/token_grads/pallas_call | solution.py:108
  76.7 2.7 %collective-permute-start.25 = (f32[2,256,128]{2,1,0:T(8,128)S(1)}, f32[2,256,128]{2,1,0:T(8,128)S(1)}, u32[]{:S(2)}, u32[]{:S(2)}) collective-permute-start(f32[2,256,128]{2,1,0:T(8,128)S(1)} %get-tuple-element.95), channel_id=1, source_target_pairs={{0,3},{1,0},{2,1},{3,2},{4,7},{5,4},{6,5},{7,6},{8,11},{9,8},{10,9... | collective-permute-start | bytes 786440 | tf_op jit(solution)/shard_map/ppermute | solution.py:385
  79.4 4.8 %collective-permute-done.22.refs_2_ = f32[2,256,128]{2,1,0:T(8,128)S(1)} collective-permute-done((f32[2,256,128]{2,1,0:T(8,128)S(1)}, f32[2,256,128]{2,1,0:T(8,128)S(1)}, u32[]{:S(2)}, u32[]{:S(2)}) %collective-permute-start.22) | collective-permute-done | bytes 262176 | tf_op jit(solution)/shard_map/ppermute | solution.py:385
  (72 shorter events, 14.3 us)
Async XLA Ops:
  6.6 5.1 %collective-permute-start = (f32[4,136,256]{2,1,0:T(8,128)}, f32[4,136,256]{2,1,0:T(8,128)S(1)}, u32[]{:S(2)}, u32[]{:S(2)}) collective-permute-start(f32[4,136,256]{2,1,0:T(8,128)} %get-tuple-element.59), channel_id=1, source_target_pairs={{0,4},{4,0},{1,5},{5,1},{2,6},{6,2},{3,7},{7,3},{8,12},{12,8},{9,1... | collective-permute-start | bytes 1671176 | tf_op jit(solution)/shard_map/ppermute | solution.py:373
  10.0 6.3 %collective-permute-start.10 = (f32[4,136,256]{2,1,0:T(8,128)}, f32[4,136,256]{2,1,0:T(8,128)S(1)}, u32[]{:S(2)}, u32[]{:S(2)}) collective-permute-start(f32[4,136,256]{2,1,0:T(8,128)} %get-tuple-element.71.sent), channel_id=1, source_target_pairs={{0,4},{4,0},{1,5},{5,1},{2,6},{6,2},{3,7},{7,3},{8,12},{12,8},{9,1... | collective-permute-start | bytes 1671176 | tf_op jit(solution)/shard_map/ppermute | solution.py:373
  12.9 6.7 %collective-permute-start.1 = (f32[136,256]{1,0:T(8,128)S(1)}, f32[136,256]{1,0:T(8,128)S(1)}, u32[]{:S(2)}, u32[]{:S(2)}) collective-permute-start(f32[136,256]{1,0:T(8,128)S(1)} %get-tuple-element.61), channel_id=1, source_target_pairs={{0,8},{8,16},{16,24},{24,0},{1,9},{9,17},{17,25},{25,1},{2,10},{10... | collective-permute-start | bytes 417800 | tf_op jit(solution)/shard_map/ppermute | solution.py:377
  13.0 8.6 %collective-permute-start.2 = (f32[136,256]{1,0:T(8,128)S(1)}, f32[136,256]{1,0:T(8,128)S(1)}, u32[]{:S(2)}, u32[]{:S(2)}) collective-permute-start(f32[136,256]{1,0:T(8,128)S(1)} %get-tuple-element.62), channel_id=1, source_target_pairs={{0,16},{8,24},{16,0},{24,8},{1,17},{9,25},{17,1},{25,9},{2,18},{10... | collective-permute-start | bytes 417800 | tf_op jit(solution)/shard_map/ppermute | solution.py:377
  15.1 7.7 %collective-permute-start.3 = (f32[136,256]{1,0:T(8,128)S(1)}, f32[136,256]{1,0:T(8,128)S(1)}, u32[]{:S(2)}, u32[]{:S(2)}) collective-permute-start(f32[136,256]{1,0:T(8,128)S(1)} %get-tuple-element.63), channel_id=1, source_target_pairs={{0,24},{8,0},{16,8},{24,16},{1,25},{9,1},{17,9},{25,17},{2,26},{10... | collective-permute-start | bytes 417800 | tf_op jit(solution)/shard_map/ppermute | solution.py:377
  16.3 12.2 %collective-permute-start.11 = (f32[136,256]{1,0:T(8,128)S(1)}, f32[136,256]{1,0:T(8,128)S(1)}, u32[]{:S(2)}, u32[]{:S(2)}) collective-permute-start(f32[136,256]{1,0:T(8,128)S(1)} %get-tuple-element.73), channel_id=1, source_target_pairs={{0,8},{8,16},{16,24},{24,0},{1,9},{9,17},{17,25},{25,1},{2,10},{10... | collective-permute-start | bytes 417800 | tf_op jit(solution)/shard_map/ppermute | solution.py:377
  16.8 11.7 %collective-permute-start.12 = (f32[136,256]{1,0:T(8,128)S(1)}, f32[136,256]{1,0:T(8,128)S(1)}, u32[]{:S(2)}, u32[]{:S(2)}) collective-permute-start(f32[136,256]{1,0:T(8,128)S(1)} %get-tuple-element.74), channel_id=1, source_target_pairs={{0,16},{8,24},{16,0},{24,8},{1,17},{9,25},{17,1},{25,9},{2,18},{10... | collective-permute-start | bytes 417800 | tf_op jit(solution)/shard_map/ppermute | solution.py:377
  19.5 8.9 %collective-permute-start.13 = (f32[136,256]{1,0:T(8,128)S(1)}, f32[136,256]{1,0:T(8,128)S(1)}, u32[]{:S(2)}, u32[]{:S(2)}) collective-permute-start(f32[136,256]{1,0:T(8,128)S(1)} %get-tuple-element.75), channel_id=1, source_target_pairs={{0,24},{8,0},{16,8},{24,16},{1,25},{9,1},{17,9},{25,17},{2,26},{10... | collective-permute-start | bytes 417800 | tf_op jit(solution)/shard_map/ppermute | solution.py:377
  22.9 11.5 %collective-permute-start.5 = (f32[136,256]{1,0:T(8,128)S(1)}, f32[136,256]{1,0:T(8,128)S(1)}, u32[]{:S(2)}, u32[]{:S(2)}) collective-permute-start(f32[136,256]{1,0:T(8,128)S(1)} %plane_join.2.refs_4_), channel_id=1, source_target_pairs={{0,64},{32,96},{64,128},{96,160},{128,192},{160,224},{192,0},{224,... | collective-permute-start | bytes 417800 | tf_op jit(solution)/shard_map/ppermute | solution.py:381
  24.7 11.6 %collective-permute-start.4 = (f32[136,256]{1,0:T(8,128)S(1)}, f32[136,256]{1,0:T(8,128)S(1)}, u32[]{:S(2)}, u32[]{:S(2)}) collective-permute-start(f32[136,256]{1,0:T(8,128)S(1)} %plane_join.2.refs_4_), channel_id=1, source_target_pairs={{0,32},{32,64},{64,96},{96,128},{128,160},{160,192},{192,224},{224... | collective-permute-start | bytes 417800 | tf_op jit(solution)/shard_map/ppermute | solution.py:381
  28.6 11.8 %collective-permute-start.15 = (f32[136,256]{1,0:T(8,128)S(1)}, f32[136,256]{1,0:T(8,128)S(1)}, u32[]{:S(2)}, u32[]{:S(2)}) collective-permute-start(f32[136,256]{1,0:T(8,128)S(1)} %plane_join.3), channel_id=1, source_target_pairs={{0,192},{32,224},{64,0},{96,32},{128,64},{160,96},{192,128},{224,1... | collective-permute-start | bytes 417800 | tf_op jit(solution)/shard_map/ppermute | solution.py:381
  33.7 8.4 %collective-permute-start.14 = (f32[136,256]{1,0:T(8,128)S(1)}, f32[136,256]{1,0:T(8,128)S(1)}, u32[]{:S(2)}, u32[]{:S(2)}) collective-permute-start(f32[136,256]{1,0:T(8,128)S(1)} %plane_join.3), channel_id=1, source_target_pairs={{0,224},{32,0},{64,32},{96,64},{128,96},{160,128},{192,160},{224,1... | collective-permute-start | bytes 417800 | tf_op jit(solution)/shard_map/ppermute | solution.py:381
  36.4 10.5 %collective-permute-start.6 = (f32[128,256]{1,0:T(8,128)S(1)}, f32[128,256]{1,0:T(8,128)S(1)}, u32[]{:S(2)}, u32[]{:S(2)}) collective-permute-start(f32[128,256]{1,0:T(8,128)S(1)} %get-tuple-element.65), channel_id=1, source_target_pairs={{0,8},{8,16},{16,24},{24,0},{1,9},{9,17},{17,25},{25,1},{2,10},{10... | collective-permute-start | bytes 393224 | tf_op jit(solution)/shard_map/ppermute | solution.py:377
  36.6 14.2 %collective-permute-start.7 = (f32[128,256]{1,0:T(8,128)S(1)}, f32[128,256]{1,0:T(8,128)S(1)}, u32[]{:S(2)}, u32[]{:S(2)}) collective-permute-start(f32[128,256]{1,0:T(8,128)S(1)} %get-tuple-element.66), channel_id=1, source_target_pairs={{0,16},{8,24},{16,0},{24,8},{1,17},{9,25},{17,1},{25,9},{2,18},{10... | collective-permute-start | bytes 393224 | tf_op jit(solution)/shard_map/ppermute | solution.py:377
  38.4 12.4 %collective-permute-start.8 = (f32[128,256]{1,0:T(8,128)S(1)}, f32[128,256]{1,0:T(8,128)S(1)}, u32[]{:S(2)}, u32[]{:S(2)}) collective-permute-start(f32[128,256]{1,0:T(8,128)S(1)} %get-tuple-element.67), channel_id=1, source_target_pairs={{0,24},{8,0},{16,8},{24,16},{1,25},{9,1},{17,9},{25,17},{2,26},{10... | collective-permute-start | bytes 393224 | tf_op jit(solution)/shard_map/ppermute | solution.py:377
  42.2 10.6 %collective-permute-start.16 = (f32[128,256]{1,0:T(8,128)S(1)}, f32[128,256]{1,0:T(8,128)S(1)}, u32[]{:S(2)}, u32[]{:S(2)}) collective-permute-start(f32[128,256]{1,0:T(8,128)S(1)} %get-tuple-element.77), channel_id=1, source_target_pairs={{0,8},{8,16},{16,24},{24,0},{1,9},{9,17},{17,25},{25,1},{2,10},{10... | collective-permute-start | bytes 393224 | tf_op jit(solution)/shard_map/ppermute | solution.py:377
  43.8 9.0 %collective-permute-start.17 = (f32[128,256]{1,0:T(8,128)S(1)}, f32[128,256]{1,0:T(8,128)S(1)}, u32[]{:S(2)}, u32[]{:S(2)}) collective-permute-start(f32[128,256]{1,0:T(8,128)S(1)} %get-tuple-element.78), channel_id=1, source_target_pairs={{0,16},{8,24},{16,0},{24,8},{1,17},{9,25},{17,1},{25,9},{2,18},{10... | collective-permute-start | bytes 393224 | tf_op jit(solution)/shard_map/ppermute | solution.py:377
  46.9 5.9 %collective-permute-start.18 = (f32[128,256]{1,0:T(8,128)S(1)}, f32[128,256]{1,0:T(8,128)S(1)}, u32[]{:S(2)}, u32[]{:S(2)}) collective-permute-start(f32[128,256]{1,0:T(8,128)S(1)} %get-tuple-element.79), channel_id=1, source_target_pairs={{0,24},{8,0},{16,8},{24,16},{1,25},{9,1},{17,9},{25,17},{2,26},{10... | collective-permute-start | bytes 393224 | tf_op jit(solution)/shard_map/ppermute | solution.py:377
  57.9 18.0 %collective-permute-start.20 = (f32[2,256,128]{2,1,0:T(8,128)S(1)}, f32[2,256,128]{2,1,0:T(8,128)S(1)}, u32[]{:S(2)}, u32[]{:S(2)}) collective-permute-start(f32[2,256,128]{2,1,0:T(8,128)S(1)} %get-tuple-element.89), channel_id=1, source_target_pairs={{0,1},{1,2},{2,3},{3,0},{4,5},{5,6},{6,7},{7,4},{8,9},{9,10},{10,1... | collective-permute-start | bytes 786440 | tf_op jit(solution)/shard_map/ppermute | solution.py:385
  58.3 17.5 %collective-permute-start.21 = (f32[2,256,128]{2,1,0:T(8,128)S(1)}, f32[2,256,128]{2,1,0:T(8,128)S(1)}, u32[]{:S(2)}, u32[]{:S(2)}) collective-permute-start(f32[2,256,128]{2,1,0:T(8,128)S(1)} %get-tuple-element.91), channel_id=1, source_target_pairs={{0,3},{1,0},{2,1},{3,2},{4,7},{5,4},{6,5},{7,6},{8,11},{9,8},{10,9... | collective-permute-start | bytes 786440 | tf_op jit(solution)/shard_map/ppermute | solution.py:385
  60.6 18.8 %collective-permute-start.23 = (f32[2,256,128]{2,1,0:T(8,128)S(1)}, f32[2,256,128]{2,1,0:T(8,128)S(1)}, u32[]{:S(2)}, u32[]{:S(2)}) collective-permute-start(f32[2,256,128]{2,1,0:T(8,128)S(1)} %get-tuple-element.93), channel_id=1, source_target_pairs={{0,1},{1,2},{2,3},{3,0},{4,5},{5,6},{6,7},{7,4},{8,9},{9,10},{10,1... | collective-permute-start | bytes 786440 | tf_op jit(solution)/shard_map/ppermute | solution.py:385
  60.6 18.8 %collective-permute-start.24 = (f32[2,256,128]{2,1,0:T(8,128)S(1)}, f32[2,256,128]{2,1,0:T(8,128)S(1)}, u32[]{:S(2)}, u32[]{:S(2)}) collective-permute-start(f32[2,256,128]{2,1,0:T(8,128)S(1)} %get-tuple-element.94), channel_id=1, source_target_pairs={{0,3},{1,0},{2,1},{3,2},{4,7},{5,4},{6,5},{7,6},{8,11},{9,8},{10,9... | collective-permute-start | bytes 786440 | tf_op jit(solution)/shard_map/ppermute | solution.py:385
  76.6 7.6 %collective-permute-start.22 = (f32[2,256,128]{2,1,0:T(8,128)S(1)}, f32[2,256,128]{2,1,0:T(8,128)S(1)}, u32[]{:S(2)}, u32[]{:S(2)}) collective-permute-start(f32[2,256,128]{2,1,0:T(8,128)S(1)} %get-tuple-element.92), channel_id=1, source_target_pairs={{0,1},{1,2},{2,3},{3,0},{4,5},{5,6},{6,7},{7,4},{8,9},{9,10},{10,1... | collective-permute-start | bytes 786440 | tf_op jit(solution)/shard_map/ppermute | solution.py:385
  76.7 7.5 %collective-permute-start.25 = (f32[2,256,128]{2,1,0:T(8,128)S(1)}, f32[2,256,128]{2,1,0:T(8,128)S(1)}, u32[]{:S(2)}, u32[]{:S(2)}) collective-permute-start(f32[2,256,128]{2,1,0:T(8,128)S(1)} %get-tuple-element.95), channel_id=1, source_target_pairs={{0,3},{1,0},{2,1},{3,2},{4,7},{5,4},{6,5},{7,6},{8,11},{9,8},{10,9... | collective-permute-start | bytes 786440 | tf_op jit(solution)/shard_map/ppermute | solution.py:385
  (17 other events, 161.8 us)

commit v6 on v4

--- a/solution.py
+++ b/solution.py
@@ -112,7 +112,7 @@
         out_shape=outs,
         scratch_shapes=scratch,
         compiler_params=pltpu.CompilerParams(vmem_limit_bytes=mib * 2**20),
-        cost_estimate=pl.CostEstimate(flops=mega * 10**3, bytes_accessed=2**10, transcendentals=0),
+        cost_estimate=pl.CostEstimate(flops=mega * 10**5, bytes_accessed=2**10, transcendentals=0),
         name=name,
         **more,
     )(*args)

time: 85.6 us -> 85.6 us (level)
  no operation moved by 1% of the time
where the time goes in v6:
time: 85.6 us; the launch traced here: 85.4 us
  starting transfers between devices  34.1 us (40%)
  Pallas kernels  24.3 us (28%)
  waiting for transfers between devices  23.5 us (27%)
  local copies, waits for them, and re-layouts  2.76 us (3%)
    pallas_call x13, Pallas kernels, call(): pl.pallas_call(kernel, in_specs=specs, out_specs=[out_spec] * len(outs),...  24.3 us
    ppermute x12, starting transfers between devices, along_y(): return lax.ppermute(v, Y, ring(4, shift))  14.7 us
    ppermute x3, waiting for transfers between devices, along_x(): return lax.ppermute(v, X, ring(4, shift))  10.6 us
    ppermute x4, starting transfers between devices, along_z(): return lax.ppermute(v, Z, ring(8, shift))  9.24 us
    ppermute x4, starting transfers between devices, swap(): return lax.ppermute(v, C, ring(2, 1))  6.68 us
    ppermute x12, waiting for transfers between devices, along_y(): return lax.ppermute(v, Y, ring(4, shift))  5.97 us
    ppermute x4, waiting for transfers between devices, along_z(): return lax.ppermute(v, Z, ring(8, shift))  3.63 us
    ppermute x3, starting transfers between devices, along_x(): return lax.ppermute(v, X, ring(4, shift))  3.49 us
  transfers between devices with their start and end apart: 23, of which 10 were waited for; matrix products, arithmetic and copies ran while one was open for 0% of the time, Pallas kernels for 18%

profile of v6, /device:TPU:1, one launch (start us, length us, event | category | flops | bytes accessed | tf_op | source)
XLA Modules:
  0.0 85.4 jit_solution(15210635495974201060)
XLA Ops:
  0.6 6.0 %summaries.1 = (bf16[8,256,256]{2,1,0:T(8,128)(2,1)}, bf16[8,256,256]{2,1,0:T(8,128)(2,1)}, bf16[8,256,256]{2,1,0:T(8,128)(2,1)}, bf16[8,256,256]{2,1,0:T(8,128)...) custom-call(f32[4,8]{1,0:T(4,128)} %bitcast.10, ...), custom_call_target="tpu_custom_call" | custom-call | flops 800000000 | bytes 1024 | tf_op jit(solution)/shard_map/summaries/pallas_call | solution.py:108
  6.6 3.3 %collective-permute-start = (f32[4,136,256]{2,1,0:T(8,128)}, f32[4,136,256]{2,1,0:T(8,128)S(1)}, u32[]{:S(2)}, u32[]{:S(2)}) collective-permute-start(f32[4,136,256]{2,1,0:T(8,128)} %get-tuple-element.53), channel_id=1, source_target_pairs={{0,4},{4,0},{1,5},{5,1},{2,6},{6,2},{3,7},{7,3},{8,12},{12,8},{9,1... | collective-permute-start | bytes 1671176 | tf_op jit(solution)/shard_map/ppermute | solution.py:373
  10.1 1.7 %collective-permute-done.refs_1_.refs_5_ = f32[4,136,256]{2,1,0:T(8,128)S(1)} collective-permute-done((f32[4,136,256]{2,1,0:T(8,128)}, f32[4,136,256]{2,1,0:T(8,128)S(1)}, u32[]{:S(2)}, u32[]{:S(2)}) %collective-permute-start) | collective-permute-done | bytes 557088 | tf_op jit(solution)/shard_map/ppermute | solution.py:373
  13.0 2.2 %collective-permute-start.2 = (f32[136,256]{1,0:T(8,128)S(1)}, f32[136,256]{1,0:T(8,128)S(1)}, u32[]{:S(2)}, u32[]{:S(2)}) collective-permute-start(f32[136,256]{1,0:T(8,128)S(1)} %get-tuple-element.56), channel_id=1, source_target_pairs={{0,16},{8,24},{16,0},{24,8},{1,17},{9,25},{17,1},{25,9},{2,18},{10... | collective-permute-start | bytes 417800 | tf_op jit(solution)/shard_map/ppermute | solution.py:377
  16.8 1.5 %collective-permute-start.12 = (f32[136,256]{1,0:T(8,128)S(1)}, f32[136,256]{1,0:T(8,128)S(1)}, u32[]{:S(2)}, u32[]{:S(2)}) collective-permute-start(f32[136,256]{1,0:T(8,128)S(1)} %get-tuple-element.68), channel_id=1, source_target_pairs={{0,16},{8,24},{16,0},{24,8},{1,17},{9,25},{17,1},{25,9},{2,18},{10... | collective-permute-start | bytes 417800 | tf_op jit(solution)/shard_map/ppermute | solution.py:377
  22.9 1.8 %collective-permute-start.5 = (f32[136,256]{1,0:T(8,128)S(1)}, f32[136,256]{1,0:T(8,128)S(1)}, u32[]{:S(2)}, u32[]{:S(2)}) collective-permute-start(f32[136,256]{1,0:T(8,128)S(1)} %plane_join.2.refs_4_), channel_id=1, source_target_pairs={{0,64},{32,96},{64,128},{96,160},{128,192},{160,224},{192,0},{224,... | collective-permute-start | bytes 417800 | tf_op jit(solution)/shard_map/ppermute | solution.py:381
  24.7 1.6 %collective-permute-start.4 = (f32[136,256]{1,0:T(8,128)S(1)}, f32[136,256]{1,0:T(8,128)S(1)}, u32[]{:S(2)}, u32[]{:S(2)}) collective-permute-start(f32[136,256]{1,0:T(8,128)S(1)} %plane_join.2.refs_4_), channel_id=1, source_target_pairs={{0,32},{32,64},{64,96},{96,128},{128,160},{160,192},{192,224},{224... | collective-permute-start | bytes 417800 | tf_op jit(solution)/shard_map/ppermute | solution.py:381
  26.3 2.2 %collective-permute-done.11.refs_1_ = f32[136,256]{1,0:T(8,128)S(1)} collective-permute-done((f32[136,256]{1,0:T(8,128)S(1)}, f32[136,256]{1,0:T(8,128)S(1)}, u32[]{:S(2)}, u32[]{:S(2)}) %collective-permute-start.11) | collective-permute-done | bytes 139296 | tf_op jit(solution)/shard_map/ppermute | solution.py:377
  28.6 5.1 %collective-permute-start.15 = (f32[136,256]{1,0:T(8,128)S(1)}, f32[136,256]{1,0:T(8,128)S(1)}, u32[]{:S(2)}, u32[]{:S(2)}) collective-permute-start(f32[136,256]{1,0:T(8,128)S(1)} %plane_join.3), channel_id=1, source_target_pairs={{0,192},{32,224},{64,0},{96,32},{128,64},{160,96},{192,128},{224,1... | collective-permute-start | bytes 417800 | tf_op jit(solution)/shard_map/ppermute | solution.py:381
  34.4 1.9 %collective-permute-done.4.refs_4_ = f32[136,256]{1,0:T(8,128)S(1)} collective-permute-done((f32[136,256]{1,0:T(8,128)S(1)}, f32[136,256]{1,0:T(8,128)S(1)}, u32[]{:S(2)}, u32[]{:S(2)}) %collective-permute-start.4) | collective-permute-done | bytes 139296 | tf_op jit(solution)/shard_map/ppermute | solution.py:381
  36.5 1.9 %collective-permute-start.7 = (f32[128,256]{1,0:T(8,128)S(1)}, f32[128,256]{1,0:T(8,128)S(1)}, u32[]{:S(2)}, u32[]{:S(2)}) collective-permute-start(f32[128,256]{1,0:T(8,128)S(1)} %get-tuple-element.60), channel_id=1, source_target_pairs={{0,16},{8,24},{16,0},{24,8},{1,17},{9,25},{17,1},{25,9},{2,18},{10... | collective-permute-start | bytes 393224 | tf_op jit(solution)/shard_map/ppermute | solution.py:377
  38.4 2.0 %collective-permute-start.8 = (f32[128,256]{1,0:T(8,128)S(1)}, f32[128,256]{1,0:T(8,128)S(1)}, u32[]{:S(2)}, u32[]{:S(2)}) collective-permute-start(f32[128,256]{1,0:T(8,128)S(1)} %get-tuple-element.61), channel_id=1, source_target_pairs={{0,24},{8,0},{16,8},{24,16},{1,25},{9,1},{17,9},{25,17},{2,26},{10... | collective-permute-start | bytes 393224 | tf_op jit(solution)/shard_map/ppermute | solution.py:377
  40.4 1.7 %collective-permute-done.14.refs_4_ = f32[136,256]{1,0:T(8,128)S(1)} collective-permute-done((f32[136,256]{1,0:T(8,128)S(1)}, f32[136,256]{1,0:T(8,128)S(1)}, u32[]{:S(2)}, u32[]{:S(2)}) %collective-permute-start.14) | collective-permute-done | bytes 139296 | tf_op jit(solution)/shard_map/ppermute | solution.py:381
  42.2 1.6 %collective-permute-start.16 = (f32[128,256]{1,0:T(8,128)S(1)}, f32[128,256]{1,0:T(8,128)S(1)}, u32[]{:S(2)}, u32[]{:S(2)}) collective-permute-start(f32[128,256]{1,0:T(8,128)S(1)} %get-tuple-element.71), channel_id=1, source_target_pairs={{0,8},{8,16},{16,24},{24,0},{1,9},{9,17},{17,25},{25,1},{2,10},{10... | collective-permute-start | bytes 393224 | tf_op jit(solution)/shard_map/ppermute | solution.py:377
  43.8 3.1 %collective-permute-start.17 = (f32[128,256]{1,0:T(8,128)S(1)}, f32[128,256]{1,0:T(8,128)S(1)}, u32[]{:S(2)}, u32[]{:S(2)}) collective-permute-start(f32[128,256]{1,0:T(8,128)S(1)} %get-tuple-element.72), channel_id=1, source_target_pairs={{0,16},{8,24},{16,0},{24,8},{1,17},{9,25},{17,1},{25,9},{2,18},{10... | collective-permute-start | bytes 393224 | tf_op jit(solution)/shard_map/ppermute | solution.py:377
  48.6 2.2 %local_grads.1 = (f32[8,256,128]{2,1,0:T(8,128)S(1)}, f32[8,256,128]{2,1,0:T(8,128)S(1)}) custom-call(s32[1,256]{1,0:T(1,128)S(1)} %bitcast.7, bf16[8,256,256]{2,1,0:T(8,128)(2,1)S(1)} %copy-done, bf16[8,256,256]{2,1,0:T(8,128)(2,1)S(1)} %copy-done.1, bf16[8,256,256]{2,1,0:T(8,128)(2,1)S(1)} %copy-done.2, bf16[8,256,256]{2,1,0:T(8,128)(2,1)S(1)} %copy-done.3, ...), custom_call_target="tpu_custom_call" | custom-call | flops 300000000 | bytes 1024 | tf_op jit(solution)/shard_map/local_grads/pallas_call | solution.py:108
  50.9 1.8 %collective-permute-start.9 = (f32[4,128,256]{2,1,0:T(8,128)S(1)}, f32[4,128,256]{2,1,0:T(8,128)S(1)}, u32[]{:S(2)}, u32[]{:S(2)}) collective-permute-start(f32[4,128,256]{2,1,0:T(8,128)S(1)} %get-tuple-element.63), channel_id=1, source_target_pairs={{0,4},{4,0},{1,5},{5,1},{2,6},{6,2},{3,7},{7,3},{8,12},{12,8},{9,1... | collective-permute-start | bytes 1572872 | tf_op jit(solution)/shard_map/ppermute | solution.py:373
  52.9 1.4 %collective-permute-start.19 = (f32[4,128,256]{2,1,0:T(8,128)S(1)}, f32[4,128,256]{2,1,0:T(8,128)S(1)}, u32[]{:S(2)}, u32[]{:S(2)}) collective-permute-start(f32[4,128,256]{2,1,0:T(8,128)S(1)} %get-tuple-element.76), channel_id=1, source_target_pairs={{0,4},{4,0},{1,5},{5,1},{2,6},{6,2},{3,7},{7,3},{8,12},{12,8},{9,1... | collective-permute-start | bytes 1572872 | tf_op jit(solution)/shard_map/ppermute | solution.py:373
  54.3 1.5 %collective-permute-done.19.agot = f32[4,128,256]{2,1,0:T(8,128)S(1)} collective-permute-done((f32[4,128,256]{2,1,0:T(8,128)S(1)}, f32[4,128,256]{2,1,0:T(8,128)S(1)}, u32[]{:S(2)}, u32[]{:S(2)}) %collective-permute-start.19) | collective-permute-done | bytes 524320 | tf_op jit(solution)/shard_map/ppermute | solution.py:373
  55.9 2.0 %summed.1 = (f32[4,256,128]{2,1,0:T(8,128)S(1)}, f32[4,256,128]{2,1,0:T(8,128)S(1)}, f32[4,256,128]{2,1,0:T(8,128)S(1)}, f32[4,256,128]{2,1,0:T(8,128)S(1)}) custom-call(s32[1,256]{1,0:T(1,128)S(1)} %bitcast.8, bf16[8,256,256]{2,1,0:T(8,128)(2,1)S(1)} %copy-done.2, bf16[8,256,256]{2,1,0:T(8,128)(2,1)S(1)} %copy-done.3, bf16[8,256,256]{2,1,0:T(8,128)(2,1)S(1)} %copy-done, ...), custom_call_target="tpu_custom_call" | custom-call | flops 300000000 | bytes 1024 | tf_op jit(solution)/shard_map/summed/pallas_call | solution.py:108
  57.8 2.0 %collective-permute-start.21 = (f32[4,256,128]{2,1,0:T(8,128)S(1)}, f32[4,256,128]{2,1,0:T(8,128)S(1)}, u32[]{:S(2)}, u32[]{:S(2)}) collective-permute-start(f32[4,256,128]{2,1,0:T(8,128)S(1)} %get-tuple-element.82), channel_id=1, source_target_pairs={{0,2},{1,3},{2,0},{3,1},{4,6},{5,7},{6,4},{7,5},{8,10},{9,11},{10,... | collective-permute-start | bytes 1572872 | tf_op jit(solution)/shard_map/ppermute | solution.py:385
  61.3 12.5 %token_grads.1 = (bf16[256,8,256]{2,1,0:T(8,128)(2,1)}, f32[8,4,256]{2,1,0:T(4,128)}) custom-call(f32[4,8]{1,0:T(4,128)S(1)} %bitcast.11, s32[1,256]{1,0:T(1,128)S(1)} %bitcast.9, f32[8,4,256]{2,1,0:T(4,128)S(1)} %bitcast.5, bf16[256,128]{1,0:T(8,128)(2,1)S(1)} %copy-done.11, bf16[8,256,256]{2,1,0:T(8,128)(2,1)S(1)} %copy-done, ...), custom_call_target="tpu_custom_call" | custom-call | flops 600000000 | bytes 1024 | tf_op jit(solution)/shard_map/token_grads/pallas_call | solution.py:108
  73.9 9.3 %collective-permute-done.22.refs_3_ = f32[4,256,128]{2,1,0:T(8,128)S(1)} collective-permute-done((f32[4,256,128]{2,1,0:T(8,128)S(1)}, f32[4,256,128]{2,1,0:T(8,128)S(1)}, u32[]{:S(2)}, u32[]{:S(2)}) %collective-permute-start.22) | collective-permute-done | bytes 524320 | tf_op jit(solution)/shard_map/ppermute | solution.py:385
  83.1 1.4 %collective-permute-done.20.refs_1_ = f32[4,256,128]{2,1,0:T(8,128)S(1)} collective-permute-done((f32[4,256,128]{2,1,0:T(8,128)S(1)}, f32[4,256,128]{2,1,0:T(8,128)S(1)}, u32[]{:S(2)}, u32[]{:S(2)}) %collective-permute-start.20) | collective-permute-done | bytes 524320 | tf_op jit(solution)/shard_map/ppermute | solution.py:385
  (63 shorter events, 13.0 us)
Async XLA Ops:
  6.6 5.1 %collective-permute-start = (f32[4,136,256]{2,1,0:T(8,128)}, f32[4,136,256]{2,1,0:T(8,128)S(1)}, u32[]{:S(2)}, u32[]{:S(2)}) collective-permute-start(f32[4,136,256]{2,1,0:T(8,128)} %get-tuple-element.53), channel_id=1, source_target_pairs={{0,4},{4,0},{1,5},{5,1},{2,6},{6,2},{3,7},{7,3},{8,12},{12,8},{9,1... | collective-permute-start | bytes 1671176 | tf_op jit(solution)/shard_map/ppermute | solution.py:373
  9.9 6.3 %collective-permute-start.10 = (f32[4,136,256]{2,1,0:T(8,128)}, f32[4,136,256]{2,1,0:T(8,128)S(1)}, u32[]{:S(2)}, u32[]{:S(2)}) collective-permute-start(f32[4,136,256]{2,1,0:T(8,128)} %get-tuple-element.65.sent), channel_id=1, source_target_pairs={{0,4},{4,0},{1,5},{5,1},{2,6},{6,2},{3,7},{7,3},{8,12},{12,8},{9,1... | collective-permute-start | bytes 1671176 | tf_op jit(solution)/shard_map/ppermute | solution.py:373
  12.8 34.1 %copy-start.8 = (bf16[8,256,128]{2,1,0:T(8,128)(2,1)S(1)}, bf16[8,256,128]{2,1,0:T(8,128)(2,1)}, u32[]{:S(2)}) copy-start(bf16[8,256,128]{2,1,0:T(8,128)(2,1)} %get-tuple-element.50.b_ref) | copy-start | bytes 1572868
  12.9 6.7 %collective-permute-start.1 = (f32[136,256]{1,0:T(8,128)S(1)}, f32[136,256]{1,0:T(8,128)S(1)}, u32[]{:S(2)}, u32[]{:S(2)}) collective-permute-start(f32[136,256]{1,0:T(8,128)S(1)} %get-tuple-element.55), channel_id=1, source_target_pairs={{0,8},{8,16},{16,24},{24,0},{1,9},{9,17},{17,25},{25,1},{2,10},{10... | collective-permute-start | bytes 417800 | tf_op jit(solution)/shard_map/ppermute | solution.py:377
  13.0 8.6 %collective-permute-start.2 = (f32[136,256]{1,0:T(8,128)S(1)}, f32[136,256]{1,0:T(8,128)S(1)}, u32[]{:S(2)}, u32[]{:S(2)}) collective-permute-start(f32[136,256]{1,0:T(8,128)S(1)} %get-tuple-element.56), channel_id=1, source_target_pairs={{0,16},{8,24},{16,0},{24,8},{1,17},{9,25},{17,1},{25,9},{2,18},{10... | collective-permute-start | bytes 417800 | tf_op jit(solution)/shard_map/ppermute | solution.py:377
  15.1 7.7 %collective-permute-start.3 = (f32[136,256]{1,0:T(8,128)S(1)}, f32[136,256]{1,0:T(8,128)S(1)}, u32[]{:S(2)}, u32[]{:S(2)}) collective-permute-start(f32[136,256]{1,0:T(8,128)S(1)} %get-tuple-element.57), channel_id=1, source_target_pairs={{0,24},{8,0},{16,8},{24,16},{1,25},{9,1},{17,9},{25,17},{2,26},{10... | collective-permute-start | bytes 417800 | tf_op jit(solution)/shard_map/ppermute | solution.py:377
  16.3 12.2 %collective-permute-start.11 = (f32[136,256]{1,0:T(8,128)S(1)}, f32[136,256]{1,0:T(8,128)S(1)}, u32[]{:S(2)}, u32[]{:S(2)}) collective-permute-start(f32[136,256]{1,0:T(8,128)S(1)} %get-tuple-element.67), channel_id=1, source_target_pairs={{0,8},{8,16},{16,24},{24,0},{1,9},{9,17},{17,25},{25,1},{2,10},{10... | collective-permute-start | bytes 417800 | tf_op jit(solution)/shard_map/ppermute | solution.py:377
  16.8 11.7 %collective-permute-start.12 = (f32[136,256]{1,0:T(8,128)S(1)}, f32[136,256]{1,0:T(8,128)S(1)}, u32[]{:S(2)}, u32[]{:S(2)}) collective-permute-start(f32[136,256]{1,0:T(8,128)S(1)} %get-tuple-element.68), channel_id=1, source_target_pairs={{0,16},{8,24},{16,0},{24,8},{1,17},{9,25},{17,1},{25,9},{2,18},{10... | collective-permute-start | bytes 417800 | tf_op jit(solution)/shard_map/ppermute | solution.py:377
  19.5 8.9 %collective-permute-start.13 = (f32[136,256]{1,0:T(8,128)S(1)}, f32[136,256]{1,0:T(8,128)S(1)}, u32[]{:S(2)}, u32[]{:S(2)}) collective-permute-start(f32[136,256]{1,0:T(8,128)S(1)} %get-tuple-element.69), channel_id=1, source_target_pairs={{0,24},{8,0},{16,8},{24,16},{1,25},{9,1},{17,9},{25,17},{2,26},{10... | collective-permute-start | bytes 417800 | tf_op jit(solution)/shard_map/ppermute | solution.py:377
  22.9 11.5 %collective-permute-start.5 = (f32[136,256]{1,0:T(8,128)S(1)}, f32[136,256]{1,0:T(8,128)S(1)}, u32[]{:S(2)}, u32[]{:S(2)}) collective-permute-start(f32[136,256]{1,0:T(8,128)S(1)} %plane_join.2.refs_4_), channel_id=1, source_target_pairs={{0,64},{32,96},{64,128},{96,160},{128,192},{160,224},{192,0},{224,... | collective-permute-start | bytes 417800 | tf_op jit(solution)/shard_map/ppermute | solution.py:381
  24.7 11.6 %collective-permute-start.4 = (f32[136,256]{1,0:T(8,128)S(1)}, f32[136,256]{1,0:T(8,128)S(1)}, u32[]{:S(2)}, u32[]{:S(2)}) collective-permute-start(f32[136,256]{1,0:T(8,128)S(1)} %plane_join.2.refs_4_), channel_id=1, source_target_pairs={{0,32},{32,64},{64,96},{96,128},{128,160},{160,192},{192,224},{224... | collective-permute-start | bytes 417800 | tf_op jit(solution)/shard_map/ppermute | solution.py:381
  28.6 11.8 %collective-permute-start.15 = (f32[136,256]{1,0:T(8,128)S(1)}, f32[136,256]{1,0:T(8,128)S(1)}, u32[]{:S(2)}, u32[]{:S(2)}) collective-permute-start(f32[136,256]{1,0:T(8,128)S(1)} %plane_join.3), channel_id=1, source_target_pairs={{0,192},{32,224},{64,0},{96,32},{128,64},{160,96},{192,128},{224,1... | collective-permute-start | bytes 417800 | tf_op jit(solution)/shard_map/ppermute | solution.py:381
  33.7 8.4 %collective-permute-start.14 = (f32[136,256]{1,0:T(8,128)S(1)}, f32[136,256]{1,0:T(8,128)S(1)}, u32[]{:S(2)}, u32[]{:S(2)}) collective-permute-start(f32[136,256]{1,0:T(8,128)S(1)} %plane_join.3), channel_id=1, source_target_pairs={{0,224},{32,0},{64,32},{96,64},{128,96},{160,128},{192,160},{224,1... | collective-permute-start | bytes 417800 | tf_op jit(solution)/shard_map/ppermute | solution.py:381
  36.4 10.5 %collective-permute-start.6 = (f32[128,256]{1,0:T(8,128)S(1)}, f32[128,256]{1,0:T(8,128)S(1)}, u32[]{:S(2)}, u32[]{:S(2)}) collective-permute-start(f32[128,256]{1,0:T(8,128)S(1)} %get-tuple-element.59), channel_id=1, source_target_pairs={{0,8},{8,16},{16,24},{24,0},{1,9},{9,17},{17,25},{25,1},{2,10},{10... | collective-permute-start | bytes 393224 | tf_op jit(solution)/shard_map/ppermute | solution.py:377
  36.5 14.2 %collective-permute-start.7 = (f32[128,256]{1,0:T(8,128)S(1)}, f32[128,256]{1,0:T(8,128)S(1)}, u32[]{:S(2)}, u32[]{:S(2)}) collective-permute-start(f32[128,256]{1,0:T(8,128)S(1)} %get-tuple-element.60), channel_id=1, source_target_pairs={{0,16},{8,24},{16,0},{24,8},{1,17},{9,25},{17,1},{25,9},{2,18},{10... | collective-permute-start | bytes 393224 | tf_op jit(solution)/shard_map/ppermute | solution.py:377
  38.4 12.4 %collective-permute-start.8 = (f32[128,256]{1,0:T(8,128)S(1)}, f32[128,256]{1,0:T(8,128)S(1)}, u32[]{:S(2)}, u32[]{:S(2)}) collective-permute-start(f32[128,256]{1,0:T(8,128)S(1)} %get-tuple-element.61), channel_id=1, source_target_pairs={{0,24},{8,0},{16,8},{24,16},{1,25},{9,1},{17,9},{25,17},{2,26},{10... | collective-permute-start | bytes 393224 | tf_op jit(solution)/shard_map/ppermute | solution.py:377
  42.2 10.6 %collective-permute-start.16 = (f32[128,256]{1,0:T(8,128)S(1)}, f32[128,256]{1,0:T(8,128)S(1)}, u32[]{:S(2)}, u32[]{:S(2)}) collective-permute-start(f32[128,256]{1,0:T(8,128)S(1)} %get-tuple-element.71), channel_id=1, source_target_pairs={{0,8},{8,16},{16,24},{24,0},{1,9},{9,17},{17,25},{25,1},{2,10},{10... | collective-permute-start | bytes 393224 | tf_op jit(solution)/shard_map/ppermute | solution.py:377
  43.8 9.0 %collective-permute-start.17 = (f32[128,256]{1,0:T(8,128)S(1)}, f32[128,256]{1,0:T(8,128)S(1)}, u32[]{:S(2)}, u32[]{:S(2)}) collective-permute-start(f32[128,256]{1,0:T(8,128)S(1)} %get-tuple-element.72), channel_id=1, source_target_pairs={{0,16},{8,24},{16,0},{24,8},{1,17},{9,25},{17,1},{25,9},{2,18},{10... | collective-permute-start | bytes 393224 | tf_op jit(solution)/shard_map/ppermute | solution.py:377
  46.9 5.9 %collective-permute-start.18 = (f32[128,256]{1,0:T(8,128)S(1)}, f32[128,256]{1,0:T(8,128)S(1)}, u32[]{:S(2)}, u32[]{:S(2)}) collective-permute-start(f32[128,256]{1,0:T(8,128)S(1)} %get-tuple-element.73), channel_id=1, source_target_pairs={{0,24},{8,0},{16,8},{24,16},{1,25},{9,1},{17,9},{25,17},{2,26},{10... | collective-permute-start | bytes 393224 | tf_op jit(solution)/shard_map/ppermute | solution.py:377
  50.9 3.4 %collective-permute-start.9 = (f32[4,128,256]{2,1,0:T(8,128)S(1)}, f32[4,128,256]{2,1,0:T(8,128)S(1)}, u32[]{:S(2)}, u32[]{:S(2)}) collective-permute-start(f32[4,128,256]{2,1,0:T(8,128)S(1)} %get-tuple-element.63), channel_id=1, source_target_pairs={{0,4},{4,0},{1,5},{5,1},{2,6},{6,2},{3,7},{7,3},{8,12},{12,8},{9,1... | collective-permute-start | bytes 1572872 | tf_op jit(solution)/shard_map/ppermute | solution.py:373
  52.9 3.0 %collective-permute-start.19 = (f32[4,128,256]{2,1,0:T(8,128)S(1)}, f32[4,128,256]{2,1,0:T(8,128)S(1)}, u32[]{:S(2)}, u32[]{:S(2)}) collective-permute-start(f32[4,128,256]{2,1,0:T(8,128)S(1)} %get-tuple-element.76), channel_id=1, source_target_pairs={{0,4},{4,0},{1,5},{5,1},{2,6},{6,2},{3,7},{7,3},{8,12},{12,8},{9,1... | collective-permute-start | bytes 1572872 | tf_op jit(solution)/shard_map/ppermute | solution.py:373
  57.8 16.0 %collective-permute-start.21 = (f32[4,256,128]{2,1,0:T(8,128)S(1)}, f32[4,256,128]{2,1,0:T(8,128)S(1)}, u32[]{:S(2)}, u32[]{:S(2)}) collective-permute-start(f32[4,256,128]{2,1,0:T(8,128)S(1)} %get-tuple-element.82), channel_id=1, source_target_pairs={{0,2},{1,3},{2,0},{3,1},{4,6},{5,7},{6,4},{7,5},{8,10},{9,11},{10,... | collective-permute-start | bytes 1572872 | tf_op jit(solution)/shard_map/ppermute | solution.py:385
  59.9 23.3 %collective-permute-start.22 = (f32[4,256,128]{2,1,0:T(8,128)S(1)}, f32[4,256,128]{2,1,0:T(8,128)S(1)}, u32[]{:S(2)}, u32[]{:S(2)}) collective-permute-start(f32[4,256,128]{2,1,0:T(8,128)S(1)} %get-tuple-element.83), channel_id=1, source_target_pairs={{0,3},{1,0},{2,1},{3,2},{4,7},{5,4},{6,5},{7,6},{8,11},{9,8},{10,9... | collective-permute-start | bytes 1572872 | tf_op jit(solution)/shard_map/ppermute | solution.py:385
  60.7 23.8 %collective-permute-start.20 = (f32[4,256,128]{2,1,0:T(8,128)S(1)}, f32[4,256,128]{2,1,0:T(8,128)S(1)}, u32[]{:S(2)}, u32[]{:S(2)}) collective-permute-start(f32[4,256,128]{2,1,0:T(8,128)S(1)} %get-tuple-element.78.refs_0_), channel_id=1, source_target_pairs={{0,1},{1,2},{2,3},{3,0},{4,5},{5,6},{6,7},{7,4},{8,9},{9,10},{10,1... | collective-permute-start | bytes 1572872 | tf_op jit(solution)/shard_map/ppermute | solution.py:385
  (13 other events, 115.5 us)
